TPU v7x, 512 devices: a whole 4x4x16 slice. The times are simulated.
512 devices in a mesh: row: 32 (over x, z_hi, core), col: 16 (over z_lo, y).
Axes of the slice: x: 4, y: 4, z: 16 (z_hi: 4, z_lo: 4; z = z_hi * 4 + z_lo), core: 2. Of those that a mesh axis runs over, the one named last changes fastest.
Arguments:
- matrix: float32 [8192, 8192], P('row', 'col'), as said below
Outputs:
- reduced: float32 [8192, 8192], P('row', 'col')
Inputs may be any that keep to these rules, and one draw needn't show every extreme that they name: matrix is symmetric.
All inputs are finite; a program needn't handle non-finite values.
Results may differ from a plain program's by a relative error of at most 0.0003.
Values sent between devices are 32-bit elements; how exact they have to be, the bound alone decides.
No kernel may reach another device: no remote copies, remote signals or barrier semaphores. Data moves between devices by JAX's collectives and lax.ppermute only.
A program may use at most 64 MiB of HBM per device.

v0:
```python
import jax
import jax.numpy as jnp
from jax import lax
from jax.sharding import PartitionSpec as P

B = 32


HIGHEST = lax.Precision.HIGHEST


def from_root(shard, axis, root):
    mine = lax.axis_index(axis) == root
    return lax.psum(jnp.where(mine, shard, jnp.zeros_like(shard)), axis)


def householder(panel_cols):
    count = panel_cols.shape[0]
    width = panel_cols.shape[1]
    rows_at = jnp.arange(count, dtype=jnp.int32)

    def sweep(column_at, carried):
        working, reflectors = carried
        column = lax.dynamic_slice_in_dim(working, column_at, 1, 1)[:, 0]
        pivot = width + column_at
        below = jnp.where(rows_at >= pivot, column, 0.0)
        col_norm = jnp.sqrt(jnp.sum(below * below))
        pivot_value = lax.dynamic_slice_in_dim(column, pivot, 1, 0)[0]
        pivot_sign = jnp.where(pivot_value >= 0.0, 1.0, -1.0)
        vector = below + jnp.where(rows_at == pivot, pivot_sign * col_norm, 0.0)
        vector = vector / jnp.sqrt(jnp.sum(vector * vector) + 1e-06)
        weights = jnp.dot(vector, working, precision=HIGHEST)
        working = working - 2.0 * vector[:, None] * weights[None, :]
        reflectors = lax.dynamic_update_slice_in_dim(reflectors, vector[:, None], column_at, 1)
        return (working, reflectors)

    finished, reflectors = lax.fori_loop(0, width, sweep, (panel_cols, jnp.zeros_like(panel_cols)))
    gram = jnp.dot(reflectors.T, reflectors, precision=HIGHEST)
    order = jnp.arange(width, dtype=jnp.int32)

    def extend(column_at, triangle):
        earlier = jnp.where(
            order < column_at, lax.dynamic_slice_in_dim(gram, column_at, 1, 1)[:, 0], 0.0
        )
        column = -2.0 * jnp.dot(triangle, earlier, precision=HIGHEST) + jnp.where(
            order == column_at, 2.0, 0.0
        )
        return lax.dynamic_update_slice_in_dim(triangle, column[:, None], column_at, 1)

    triangle = lax.fori_loop(0, width, extend, jnp.zeros((width, width), panel_cols.dtype))
    return (reflectors, triangle)


def on_device(matrix):
    rows_dev = matrix.shape[0]
    cols_dev = matrix.shape[1]
    row_at = lax.axis_index("row")
    col_at = lax.axis_index("col")
    gathered = lax.all_gather(matrix[:, :B], "row", axis=0, tiled=True)
    gathered = from_root(gathered, "col", 0)
    rows_at = jnp.arange(gathered.shape[0], dtype=jnp.int32)
    panel_cols = jnp.where(rows_at[:, None] >= B, gathered, 0.0)
    reflectors, triangle = householder(panel_cols)
    own_rows = lax.dynamic_slice_in_dim(reflectors, row_at * rows_dev, rows_dev, 0)
    own_cols = lax.dynamic_slice_in_dim(reflectors, col_at * cols_dev, cols_dev, 0)
    row_product = lax.psum(jnp.dot(matrix, own_cols, precision=HIGHEST), "col")
    row_scaled = jnp.dot(row_product, triangle, precision=HIGHEST)
    whole = lax.all_gather(row_scaled, "row", axis=0, tiled=True)
    inner = jnp.dot(reflectors.T, whole, precision=HIGHEST)
    col_scaled = lax.dynamic_slice_in_dim(whole, col_at * cols_dev, cols_dev, 0)
    correction = jnp.dot(triangle.T, inner, precision=HIGHEST)
    row_coupled = row_scaled - 0.5 * jnp.dot(own_rows, correction, precision=HIGHEST)
    col_coupled = col_scaled - 0.5 * jnp.dot(own_cols, correction, precision=HIGHEST)
    left = jnp.concatenate([row_coupled, own_rows], axis=1)
    right = jnp.concatenate([own_cols, col_coupled], axis=1)
    return matrix - lax.dot_general(left, right, (((1,), (1,)), ((), ())), precision=HIGHEST)


def solution(mesh):
    return jax.shard_map(
        on_device,
        mesh=mesh,
        in_specs=(P("row", "col"),),
        out_specs=P("row", "col"),
        check_vma=False,
    )
```

profile of v0, /device:TPU:1, one launch (start us, length us, event | category | flops | bytes accessed | tf_op | source)
XLA Modules:
  0.0 600.5 jit_solution(14947038674513282538)
XLA Ops:
  8.2 80.3 %all-gather.3.cloned.1.call-done = f32[8192,32]{0,1:T(8,128)} async-done(((f32[256,32]{0,1:T(8,128)}), f32[8192,32]{0,1:T(8,128)}) %all-gather.3.cloned.1.call-update) | async-done | bytes 1048592 | tf_op jit(solution)/shard_map/all_gather | solution.py:59
  88.5 2.3 broadcast_select_fusion.2
  90.9 159.7 %all-reduce.2.cloned.1.call-done = f32[8192,32]{0,1:T(8,128)} async-done(((f32[8192,32]{0,1:T(8,128)}), f32[8192,32]{0,1:T(8,128)}) %all-reduce.2.cloned.1.call-update) | async-done | bytes 1048592 | tf_op jit(solution)/shard_map/psum | solution.py:14
  250.6 1.3 broadcast_select_fusion.1
  251.9 169.6 %while.37 = (s32[]{:T(128)}, f32[8192,32]{0,1:T(8,128)S(1)}, f32[8192,32]{0,1:T(8,128)S(1)}, f32[1,1]{0,1:T(1,128)}, f32[1,1]{0,1:T(1,128)}, /*index=5*/f32[1,1]{0,1:T(1,128)}) while((s32[]{:T(128)}, f32[8192,32]{0,1:T(8,128)S(1)}, f32[8192,32]{0,1:T(8,128)S(1)}, f32[1,1]{0,1:T(1,128)}, f32[1,1]{0,1:T(1,128)}, ...), condition=%wide.region_4.5_spmd.clone.clone.clone, body=%wide.region_1.4_spmd.clone.clone.sunk.clone | while | flops 3850250 | bytes 3654161 | solution.py:37
  256.1 0.9 convolution_bitcast_fusion.5
  261.4 0.9 convolution_bitcast_fusion.5
  266.7 0.9 convolution_bitcast_fusion.5
  272.0 0.9 convolution_bitcast_fusion.5
  277.3 0.9 convolution_bitcast_fusion.5
  282.6 0.9 convolution_bitcast_fusion.5
  287.9 0.9 convolution_bitcast_fusion.5
  293.2 0.9 convolution_bitcast_fusion.5
  298.5 0.9 convolution_bitcast_fusion.5
  303.8 0.9 convolution_bitcast_fusion.5
  309.1 0.9 convolution_bitcast_fusion.5
  314.4 0.9 convolution_bitcast_fusion.5
  421.6 1.0 fusion.29
  423.2 64.7 %psum.15 = f32[256,32]{0,1:T(8,128)S(1)} all-reduce(f32[256,32]{0,1:T(8,128)S(1)} %convolution_bitcast_fusion.2), channel_id=1, replica_groups=mesh['row'=32,'col'=16] {'col'}, use_global_device_ids=true, to_apply=%region_5.6 | all-reduce | flops 8192 | bytes 65536 | tf_op jit(solution)/shard_map/psum | solution.py:66
  487.8 5.6 while.38
  494.3 94.0 %all-gather.5.cloned.1.call-done = f32[8192,32]{0,1:T(8,128)} async-done(((f32[256,32]{0,1:T(8,128)}), f32[8192,32]{0,1:T(8,128)}) %all-gather.5.cloned.1.call-update) | async-done | bytes 1048592 | tf_op jit(solution)/shard_map/all_gather | solution.py:68
  588.3 2.2 fusion.31
  591.5 1.1 fusion.19
  592.6 1.4 convolution_subtract_fusion
  (394 shorter events, 104.2 us)
Async XLA Ops:
  6.5 0.9 slice-start
  6.5 82.0 %all-gather.3.cloned.1.call-start = ((), (), s32[]{:S(2)}) async-start(), calls=%async_computation | async-start | bytes 1081344 | tf_op jit(solution)/shard_map/all_gather | solution.py:59
  8.2 242.5 %all-reduce.2.cloned.1.call-start = ((), (), s32[]{:S(2)}) async-start(), calls=%async_computation.1 | async-start | bytes 2097152 | tf_op jit(solution)/shard_map/psum | solution.py:14
  90.8 497.5 %all-gather.5.cloned.1.call-start = ((), (), s32[]{:S(2)}) async-start(), calls=%async_computation.2 | async-start | bytes 1081344 | tf_op jit(solution)/shard_map/all_gather | solution.py:68
  421.5 1.0 copy-start
  590.5 0.8 copy-start.1
Sparse Core Ops, SparseCore 0:
  10.4 78.0 all-gather.2
  91.4 159.1 all-reduce.1
  494.4 93.8 all-gather.4
where the time goes:
time: 602 us; the launch traced here: 601 us
  waiting for transfers between devices  334 us (55%)
  blocking collectives  64.7 us (11%)
  loops' own time  64.1 us (11%)
  other arithmetic  55.5 us (9%)
  matrix products  41.1 us (7%)
  local copies, waits for them, and re-layouts  27.7 us (5%)
  between operations  13.2 us (2%)
    psum x1, waiting for transfers between devices, from_root(): return lax.psum(jnp.where(mine, shard, jnp.zeros_like(shard)), axis)  160 us
    all_gather x1, waiting for transfers between devices, on_device(): whole = lax.all_gather(row_scaled, 'row', axis=0, tiled=True)  94 us
    all_gather x1, waiting for transfers between devices, on_device(): gathered = lax.all_gather(matrix[:, :B], 'row', axis=0, tiled=True)  80.3 us
    psum x1, blocking collectives, on_device(): row_product = lax.psum(jnp.dot(matrix, own_cols, precision=HIGHEST), 'col')  64.7 us
    another operation x1, loops' own time, householder(): lax.fori_loop(0, width, sweep, (panel_cols, jnp.zeros_like(panel_cols)))  63.7 us
    dot_general x32, matrix products, sweep(): weights = jnp.dot(vector, working, precision=HIGHEST)  29.4 us
    reduce_sum x32, other arithmetic, sweep(): col_norm = jnp.sqrt(jnp.sum(below * below))  22.1 us
    reduce_sum x32, other arithmetic, sweep(): vector = vector / jnp.sqrt(jnp.sum(vector * vector) + 1e-06)  19.3 us
  transfers between devices with their start and end apart: 3, of which 3 were waited for; matrix products, arithmetic and copies ran while one was open for 0% of the time, Pallas kernels for 0%

commit v1 on v0

--- a/solution.py
+++ b/solution.py
@@ -1,10 +1,20 @@
 import jax
 import jax.numpy as jnp
 from jax import lax
+from jax.experimental import pallas as pl
+from jax.experimental.pallas import tpu as pltpu
 from jax.sharding import PartitionSpec as P
 
 B = 32
-
+ROWS = 32
+COLS = 16
+PIECE = 16
+LANES = 128
+EPS = 1e-06
+AMPLIFY_MAX = 16.0
+GRAM_MIN = 1e-06
+GRAM_MAX = 1e08
+VALUE_MAX = 1e25
 
 HIGHEST = lax.Precision.HIGHEST
 
@@ -28,7 +38,7 @@
         pivot_value = lax.dynamic_slice_in_dim(column, pivot, 1, 0)[0]
         pivot_sign = jnp.where(pivot_value >= 0.0, 1.0, -1.0)
         vector = below + jnp.where(rows_at == pivot, pivot_sign * col_norm, 0.0)
-        vector = vector / jnp.sqrt(jnp.sum(vector * vector) + 1e-06)
+        vector = vector / jnp.sqrt(jnp.sum(vector * vector) + EPS)
         weights = jnp.dot(vector, working, precision=HIGHEST)
         working = working - 2.0 * vector[:, None] * weights[None, :]
         reflectors = lax.dynamic_update_slice_in_dim(reflectors, vector[:, None], column_at, 1)
@@ -51,7 +61,7 @@
     return (reflectors, triangle)
 
 
-def on_device(matrix):
+def general_path(matrix):
     rows_dev = matrix.shape[0]
     cols_dev = matrix.shape[1]
     row_at = lax.axis_index("row")
@@ -76,6 +86,243 @@
     return matrix - lax.dot_general(left, right, (((1,), (1,)), ((), ())), precision=HIGHEST)
 
 
+def dot(a, b, over=((1,), (0,))):
+    return lax.dot_general(
+        a, b, (over, ((), ())), precision=HIGHEST, preferred_element_type=jnp.float32
+    )
+
+
+def dot_nt(a, b):
+    return dot(a, b, ((1,), (1,)))
+
+
+def dot_tn(a, b):
+    return dot(a, b, ((0,), (0,)))
+
+
+def iota(shape, axis):
+    return lax.broadcasted_iota(jnp.int32, shape, axis)
+
+
+def partial_kernel(a_ref, strip_ref, out_ref):
+    first_col = lax.axis_index("col") == 0
+    strip = strip_ref[0:B, :]
+    start = jnp.where(first_col, 2 * B, 0)
+    below_t = jnp.where(iota(strip.shape, 1) >= start, strip, 0.0)
+    padded = jnp.concatenate([below_t, jnp.zeros((LANES - B, strip.shape[1]), jnp.float32)], axis=0)
+    a = a_ref[...]
+    rows = a.shape[0]
+    product = dot_nt(a, padded)
+    near = pltpu.roll(a[:, :LANES], B, 1)
+    piece = jnp.where(iota((rows, LANES), 1) < B, product, near)
+    out_ref[:, 0:PIECE, :] = piece.reshape(COLS, PIECE, LANES)
+    gram = dot_nt(below_t, padded)
+    corner = pltpu.roll(strip_ref[B : 2 * B, :LANES], B, 1)
+    both = jnp.where(iota((B, LANES), 1) < B, gram, corner)
+    out_ref[:, PIECE : PIECE + B, :] = jnp.broadcast_to(both[None], (COLS, B, LANES))
+
+
+def sum_kernel(in_ref, out_ref, piece_ref, gram_ref):
+    lane = iota((PIECE, LANES), 1)
+    total = jnp.sum(in_ref[:, 0:PIECE, :], axis=0)
+    piece = jnp.where(lane < B, total, in_ref[0, 0:PIECE, :])
+    largest = jnp.max(jnp.where(lane < 3 * B, jnp.abs(piece), 0.0), keepdims=True)
+    bad = jnp.where(largest <= VALUE_MAX, 0.0, jnp.inf)
+    piece = jnp.where(lane < B, piece + bad, piece)
+    piece_ref[...] = piece
+    half = PIECE // 2
+    folded = jnp.where(
+        iota((half, LANES), 1) < 2 * B, piece[:half], pltpu.roll(piece[half:], LANES // 2, 1)
+    )
+    out_ref[...] = jnp.broadcast_to(folded[None], (ROWS, half, LANES))
+    gram = jnp.sum(in_ref[:, PIECE : PIECE + B, :], axis=0)
+    gram_ref[...] = jnp.where(iota((B, LANES), 1) < B, gram, in_ref[0, PIECE : PIECE + B, :])
+
+
+def factor_kernel(gram_ref, out_ref, flag_ref):
+    both = gram_ref[...]
+    gram = both[:, :B]
+    top0 = pltpu.roll(both, LANES - B, 1)[:, :B]
+    sub = iota((B, B), 0)
+    lane = iota((B, B), 1)
+    eye = jnp.where(sub == lane, 1.0, 0.0)
+    work = top0
+    coef = eye
+    image = gram
+    top = jnp.zeros((B, B), jnp.float32)
+    coefs = jnp.zeros((B, B), jnp.float32)
+    for j in range(B):
+        x_top = jnp.broadcast_to(work[:, j : j + 1], (B, B))
+        x_top = jnp.where(sub >= j, x_top, 0.0)
+        x_coef = jnp.broadcast_to(coef[:, j : j + 1], (B, B))
+        x_image = jnp.broadcast_to(image[:, j : j + 1], (B, B))
+        inner = jnp.sum(x_top * work + x_coef * image, axis=0, keepdims=True)
+        norm2 = jnp.broadcast_to(inner[:, j : j + 1], (1, B))
+        pivot = jnp.broadcast_to(work[j : j + 1, j : j + 1], (1, B))
+        norm = jnp.sqrt(norm2)
+        signed = jnp.where(pivot >= 0.0, norm, -norm)
+        scale = lax.rsqrt(2.0 * (norm2 + signed * pivot) + EPS)
+        weights = scale * (inner + signed * work[j : j + 1, :])
+        x_top = scale * jnp.where(sub == j, x_top + signed, x_top)
+        x_coef = scale * x_coef
+        x_image = scale * x_image
+        twice = 2.0 * weights
+        work = work - x_top * twice
+        coef = coef - x_coef * twice
+        image = image - x_image * twice
+        top = jnp.where(lane == j, x_top, top)
+        coefs = jnp.where(lane == j, x_coef, coefs)
+    overlap = dot_tn(top, top) + dot_tn(coefs, dot(gram, coefs))
+    upper = jnp.where(sub < lane, overlap, 0.0)
+    triangle = 2.0 * eye
+    width = 1
+    while width < B:
+        joined = (sub // (2 * width) == lane // (2 * width)) & (sub // width != lane // width)
+        triangle = triangle - dot(triangle, dot(jnp.where(joined, upper, 0.0), triangle))
+        width *= 2
+    out_ref[0] = coefs
+    out_ref[1] = top
+    out_ref[2] = dot(coefs, triangle)
+    out_ref[3] = dot(top, triangle)
+    diag = jnp.sum(jnp.where(sub == lane, gram, 0.0), axis=1, keepdims=True)
+    growth = jnp.sum(jnp.abs(coefs) * jnp.sqrt(diag), axis=0, keepdims=True)
+    worst = jnp.max(growth, keepdims=True)
+    low = jnp.min(diag, keepdims=True)
+    high = jnp.max(diag, keepdims=True)
+    fine = (worst <= AMPLIFY_MAX) & (low >= GRAM_MIN) & (high <= GRAM_MAX)
+    flag_ref[...] = jnp.broadcast_to(jnp.where(fine, 0.0, jnp.inf), flag_ref.shape)
+
+
+def inner_kernel(in_ref, piece_ref, flag_ref, out_ref):
+    col_at = lax.axis_index("col")
+    half = PIECE // 2
+    folded = in_ref[...]
+    second = pltpu.roll(folded.reshape(ROWS * half, LANES), LANES // 2, 1).reshape(folded.shape)
+    rows = jnp.concatenate([folded, second], axis=1)
+    order = iota(rows.shape, 0) * (COLS * PIECE) + col_at * PIECE + iota(rows.shape, 1)
+    lane = iota(rows.shape, 2)
+    product = jnp.where(lane < B, rows, 0.0)
+    below = jnp.where((order >= 2 * B) & (lane >= B) & (lane < 2 * B), rows, 0.0)
+    count = ROWS * PIECE
+    square = dot_tn(below.reshape(count, LANES), product.reshape(count, LANES))[B : 2 * B, :]
+    largest = jnp.max(jnp.abs(product).reshape(count, LANES), keepdims=True)
+    bad = jnp.where(largest <= VALUE_MAX, flag_ref[0:1, 0:1], jnp.inf)
+    square = square + bad
+    lane8 = iota((8, LANES), 1)
+    packed = jnp.zeros((8, LANES), jnp.float32)
+    for k in range(B // 8):
+        part = square[8 * k : 8 * k + 8]
+        part = part if k == 0 else pltpu.roll(part, B * k, 1)
+        packed = jnp.where(lane8 // B == k, part, packed)
+    out_ref[:, 0:PIECE, :] = jnp.broadcast_to(piece_ref[...][None], (COLS, PIECE, LANES))
+    out_ref[:, PIECE : 2 * PIECE, :] = folded.reshape(COLS, PIECE, LANES)
+    out_ref[:, 2 * PIECE : 2 * PIECE + 8, :] = jnp.broadcast_to(in_ref[0][None], (COLS, 8, LANES))
+    out_ref[:, 2 * PIECE + 8 : 2 * PIECE + 16, :] = jnp.broadcast_to(packed[None], (COLS, 8, LANES))
+
+
+def update_kernel(a_ref, strip_ref, in_ref, gram_ref, factor_ref, out_ref, ok_ref):
+    first_row = lax.axis_index("row") == 0
+    first_col = lax.axis_index("col") == 0
+    half_lanes = LANES // 2
+    packed = jnp.sum(in_ref[:, 2 * PIECE + 8 : 2 * PIECE + 16, :], axis=0)
+    square = jnp.concatenate(
+        [packed] + [pltpu.roll(packed, LANES - B * k, 1) for k in range(1, B // 8)], axis=0
+    )[:, :B]
+    near = []
+    for source in (2, 3):
+        block = in_ref[source, 2 * PIECE : 2 * PIECE + 8, :]
+        near += [block, pltpu.roll(block, half_lanes, 1)]
+    near = jnp.concatenate(near, axis=0)[:, :B]
+    corner = pltpu.roll(gram_ref[...], LANES - 2 * B, 1)[:, :B]
+    largest = jnp.max(jnp.abs(square), keepdims=True)
+    ok_ref[0, 0] = (jnp.max(jnp.where(largest <= VALUE_MAX, 1.0, 0.0)) > 0.5).astype(jnp.int32)
+    coefs, top, coefs_t, top_t = (factor_ref[k] for k in range(4))
+    inner = dot_tn(coefs_t, dot(square, coefs_t) + dot_tn(near, top_t)) + dot_tn(
+        top_t, dot(near, coefs_t) + dot(corner, top_t)
+    )
+    shift = 0.5 * inner
+    zero = jnp.zeros((B, B), jnp.float32)
+    vector = jnp.concatenate([zero, coefs, zero, top], axis=0)
+    coupled = jnp.concatenate([coefs_t, zero, top_t, zero], axis=0) - dot(vector, shift)
+    middle = dot_nt(coupled, vector) + dot_nt(vector, coupled)
+    rows = a_ref.shape[0]
+    cols = a_ref.shape[1]
+    left = in_ref[:, 0:PIECE, :].reshape(rows, LANES)
+    at = iota(left.shape, 0)
+    lane = iota(left.shape, 1)
+    start = jnp.where(first_row, 2 * B, 0)
+    left = jnp.where((lane >= B) & (lane < 2 * B) & (at < start), 0.0, left)
+    unit = jnp.where(first_row & (at - B == lane - 3 * B), 1.0, 0.0)
+    left = jnp.where(lane >= 3 * B, unit, left)
+    scaled = dot(left, middle)
+    strip = strip_ref[0:B, :]
+    lane_c = iota(strip.shape, 1)
+    start_c = jnp.where(first_col, 2 * B, 0)
+    below_t = jnp.where(lane_c >= start_c, strip, 0.0)
+    unit_t = jnp.where(first_col & (iota(strip.shape, 0) == lane_c - B), 1.0, 0.0)
+    parts = []
+    for k in range(2):
+        block = in_ref[:, PIECE + 8 * k : PIECE + 8 * k + 8, :]
+        other = pltpu.roll(block.reshape(COLS * 8, LANES), half_lanes, 1).reshape(block.shape)
+        unfolded = jnp.concatenate([block, other], axis=1).reshape(COLS * PIECE, LANES)
+        parts.append(jnp.transpose(unfolded)[:B])
+    product_t = jnp.concatenate(parts, axis=1)
+    right = jnp.concatenate([product_t, below_t, strip_ref[B : 2 * B, :], unit_t], axis=0)
+    out_ref[...] = a_ref[...] - dot(scaled, right)
+
+
+def call(kernel, *shapes, smem=()):
+    vmem = pl.BlockSpec(memory_space=pltpu.VMEM)
+    specs = [
+        pl.BlockSpec(memory_space=pltpu.SMEM) if k in smem else vmem for k in range(len(shapes))
+    ]
+    return pl.pallas_call(
+        kernel,
+        out_shape=list(shapes),
+        out_specs=specs,
+        compiler_params=pltpu.CompilerParams(vmem_limit_bytes=32 * 1024 * 1024),
+    )
+
+
+def array(*shape, dtype=jnp.float32):
+    return jax.ShapeDtypeStruct(shape, dtype)
+
+
+def spread(strip):
+    at = lax.axis_index("row")
+    for pairs_of in (
+        [[(0, 2 * z)] for z in (2, 1, 3)],
+        [[(2 * z, 8 * x + 2 * z) for z in range(4)] for x in (2, 1, 3)],
+        [[(k, k + 1) for k in range(0, ROWS, 2)]],
+    ):
+        held = strip
+        for pairs in pairs_of:
+            arrived = lax.ppermute(strip, "row", pairs)
+            here = jnp.zeros((), jnp.bool_)
+            for _, target in pairs:
+                here = here | (at == target)
+            held = jnp.where(here, arrived, held)
+        strip = held
+    return strip
+
+
+def on_device(matrix):
+    strip = spread(matrix[: 2 * B, :])
+    (sent,) = call(partial_kernel, array(COLS, PIECE + B, LANES))(matrix, strip)
+    got = lax.all_to_all(sent, "col", 0, 0)
+    sent, piece, gram = call(
+        sum_kernel, array(ROWS, PIECE // 2, LANES), array(PIECE, LANES), array(B, LANES)
+    )(got)
+    factor, flag = call(factor_kernel, array(4, B, B), array(8, LANES))(gram)
+    got = lax.all_to_all(sent, "row", 0, 0)
+    (sent,) = call(inner_kernel, array(COLS, 3 * PIECE, LANES))(got, piece, flag)
+    got = lax.all_to_all(sent, "col", 0, 0)
+    fast, fine = call(
+        update_kernel, array(*matrix.shape), array(1, 1, dtype=jnp.int32), smem=(1,)
+    )(matrix, strip, got, gram, factor)
+    return lax.cond(fine[0, 0] > 0, lambda: fast, lambda: general_path(matrix))
+
+
 def solution(mesh):
     return jax.shard_map(
         on_device,

time: 602 us -> 122 us (0.20)
  waiting for transfers between devices: 334 us -> 35.6 us
  loops' own time: 64.1 us -> 0.01 us
  other arithmetic: 55.5 us -> 1 us
  matrix products: 41.1 us -> 0 us
  blocking collectives: 64.7 us -> 35.6 us
  local copies, waits for them, and re-layouts: 27.7 us -> 1.71 us
  starting transfers between devices: 0.09 us -> 21.5 us
  Pallas kernels: 0 us -> 12.1 us
    all_gather x2 -> x0, waiting for transfers between devices: 174 us -> none  [the longest x1 94 us: on_device(): whole = lax.all_gather(row_scaled, 'row', axis=0, tiled=True)]
    psum x1 -> x0, waiting for transfers between devices: 160 us -> none  [from_root(): return lax.psum(jnp.where(mine, shard, jnp.zeros_like(shard)), axis)]
    psum x1 -> x0, blocking collectives: 64.7 us -> none  [on_device(): row_product = lax.psum(jnp.dot(matrix, own_cols, precision=HIGHEST), 'col')]
    another operation x2 -> x1, loops' own time: 64.1 us -> 0.01 us  [on_device(): return lax.cond(fine[0, 0] > 0, lambda: fast, lambda: general_path(matrix))]
    reduce_sum x64 -> x0, other arithmetic: 41.4 us -> none  [the longest x32 22.1 us: sweep(): col_norm = jnp.sqrt(jnp.sum(below * below))]
    dot_general x72 -> x0, matrix products: 41.1 us -> none  [the longest x32 29.4 us: sweep(): weights = jnp.dot(vector, working, precision=HIGHEST)]
    all_to_all x0 -> x2, blocking collectives: none -> 35.6 us  [on_device(): got = lax.all_to_all(sent, 'col', 0, 0)]
    ppermute x0 -> x7, waiting for transfers between devices: none -> 26.7 us  [spread(): arrived = lax.ppermute(strip, 'row', pairs)]
  transfers between devices with their start and end apart: 3 -> 8, of which waited for: 3 -> 2; matrix products, arithmetic and copies ran while one was open for 0% -> 0% of each run, Pallas kernels for 0% -> 6%
where the time goes in v1:
time: 122 us
  waiting for transfers between devices  35.6 us (29%)
  blocking collectives  35.6 us (29%)
  starting transfers between devices  21.5 us (18%)
  between operations  14.3 us (12%)
  Pallas kernels  12.1 us (10%)
  local copies, waits for them, and re-layouts  1.71 us (1%)
    all_to_all x2, blocking collectives, on_device(): got = lax.all_to_all(sent, 'col', 0, 0)  35.6 us
    ppermute x7, waiting for transfers between devices, spread(): arrived = lax.ppermute(strip, 'row', pairs)  26.7 us
    all_to_all x1, starting transfers between devices, on_device(): got = lax.all_to_all(sent, 'row', 0, 0)  16.1 us
    all_to_all x1, waiting for transfers between devices, on_device(): got = lax.all_to_all(sent, 'row', 0, 0)  8.88 us
    pallas_call x1, Pallas kernels, on_device(): factor, flag = call(factor_kernel, array(4, B, B), array(8, LANES))(gram)  7.79 us
    ppermute x7, starting transfers between devices, spread(): arrived = lax.ppermute(strip, 'row', pairs)  5.44 us
  transfers between devices with their start and end apart: 8, of which 2 were waited for; matrix products, arithmetic and copies ran while one was open for 0% of the time, Pallas kernels for 6%

profile of v1, /device:TPU:1, one launch (start us, length us, event | category | flops | bytes accessed | tf_op | source)
XLA Modules:
  0.0 121.9 jit_solution(7545188969745055234)
XLA Ops:
  6.5 0.9 slice.6
  7.5 0.7 collective-permute-start
  8.1 0.7 collective-permute-start.1
  8.8 0.7 collective-permute-start.2
  9.5 0.0 collective-permute-done
  9.5 0.0 collective-permute-done.2
  9.5 0.9 select_select_fusion.1
  10.5 0.7 collective-permute-start.3
  11.1 0.7 collective-permute-start.4
  11.8 0.7 collective-permute-start.5
  12.5 0.0 copy-start
  12.6 1.4 %collective-permute-start.6 = (f32[64,512]{1,0:T(8,128)S(1)}, f32[64,512]{1,0:T(8,128)S(1)}, u32[]{:S(2)}, u32[]{:S(2)}) collective-permute-start(f32[64,512]{1,0:T(8,128)S(1)} %select_select_fusion), channel_id=1, source_target_pairs={{0,16},{32,48},{64,80},{96,112},{128,144},{160,176},{192,208},{224... | collective-permute-start | bytes 393224 | tf_op jit(solution)/shard_map/ppermute | solution.py:300
  14.1 26.7 %collective-permute-done.6 = f32[64,512]{1,0:T(8,128)S(1)} collective-permute-done((f32[64,512]{1,0:T(8,128)S(1)}, f32[64,512]{1,0:T(8,128)S(1)}, u32[]{:S(2)}, u32[]{:S(2)}) %collective-permute-start.6) | collective-permute-done | bytes 131104 | tf_op jit(solution)/shard_map/ppermute | solution.py:300
  40.8 0.6 shard_map.22
  41.5 18.9 %all_to_all.15.in_ref = f32[16,48,128]{2,1,0:T(8,128)S(1)} all-to-all(f32[16,48,128]{2,1,0:T(8,128)S(1)} %shard_map.22), channel_id=1, replica_groups=mesh['row'=32,'col'=16] {'col'}, dimensions={0} | all-to-all | bytes 786432 | tf_op jit(solution)/shard_map/all_to_all | solution.py:312
  60.4 0.9 shard_map.23
  61.3 16.1 %all-to-all-start.1 = ((f32[32,8,128]{2,1,0:T(8,128)}), f32[32,8,128]{2,1,0:T(8,128)S(1)}, u32[]{:S(2)}, u32[]{:S(2)}) async-start(f32[32,8,128]{2,1,0:T(8,128)} %get-tuple-element.229), calls=%async_computation.1 | async-start | bytes 262144 | tf_op jit(solution)/shard_map/all_to_all | solution.py:317
  77.4 7.8 %shard_map.24 = (f32[4,32,32]{2,1,0:T(8,128)S(1)}, f32[8,128]{1,0:T(8,128)S(1)}) custom-call(f32[32,128]{1,0:T(8,128)S(1)} %get-tuple-element.231.gram_ref), custom_call_target="tpu_custom_call" | custom-call | tf_op jit(solution)/shard_map/pallas_call | solution.py:316
  85.2 8.9 %all-to-all-done.1.in_ref = f32[32,8,128]{2,1,0:T(8,128)S(1)} async-done(((f32[32,8,128]{2,1,0:T(8,128)}), f32[32,8,128]{2,1,0:T(8,128)S(1)}, u32[]{:S(2)}, u32[]{:S(2)}) %all-to-all-start.1) | async-done | bytes 131104 | tf_op jit(solution)/shard_map/all_to_all | solution.py:317
  94.0 0.6 shard_map.25
  94.6 16.7 %all_to_all.16.in_ref = f32[16,48,128]{2,1,0:T(8,128)S(1)} all-to-all(f32[16,48,128]{2,1,0:T(8,128)S(1)} %shard_map.25), channel_id=1, replica_groups=mesh['row'=32,'col'=16] {'col'}, dimensions={0} | all-to-all | bytes 786432 | tf_op jit(solution)/shard_map/all_to_all | solution.py:319
  111.4 2.2 %shard_map.26 = (f32[256,512]{1,0:T(8,128)S(1)}, s32[1,1]{1,0:T(1,128)}) custom-call(f32[256,512]{1,0:T(8,128)S(1)} %copy-done, f32[64,512]{1,0:T(8,128)S(1)} %broadcast_select_fusion.3.strip_ref, f32[16,48,128]{2,1,0:T(8,128)S(1)} %all_to_all.16.in_ref, f32[32,128]{1,0:T(8,128)S(1)} %get-tuple-element.231.gram_ref, ...), custom_call_target="tpu_custom_call" | custom-call | tf_op jit(solution)/shard_map/pallas_call | solution.py:320
  114.2 0.0 copy-start.2
  114.3 0.8 copy-done.2
  (8 shorter events, 0.1 us)
Async XLA Ops:
  7.5 2.0 %collective-permute-start = (f32[64,512]{1,0:T(8,128)S(1)}, f32[64,512]{1,0:T(8,128)S(1)}, u32[]{:S(2)}, u32[]{:S(2)}) collective-permute-start(f32[64,512]{1,0:T(8,128)S(1)} %slice.6), channel_id=1, source_target_pairs={{0,96},{1,97},{2,98},{3,99},{4,100},{5,101},{6,102},{7,103},{8,104... | collective-permute-start | bytes 393224 | tf_op jit(solution)/shard_map/ppermute | solution.py:300
  8.1 1.4 %collective-permute-start.1 = (f32[64,512]{1,0:T(8,128)S(1)}, f32[64,512]{1,0:T(8,128)S(1)}, u32[]{:S(2)}, u32[]{:S(2)}) collective-permute-start(f32[64,512]{1,0:T(8,128)S(1)} %slice.6), channel_id=1, source_target_pairs={{0,32},{1,33},{2,34},{3,35},{4,36},{5,37},{6,38},{7,39},{8,40},{9,... | collective-permute-start | bytes 393224 | tf_op jit(solution)/shard_map/ppermute | solution.py:300
  8.8 0.7 collective-permute-start.2
  10.5 2.1 %collective-permute-start.3 = (f32[64,512]{1,0:T(8,128)S(1)}, f32[64,512]{1,0:T(8,128)S(1)}, u32[]{:S(2)}, u32[]{:S(2)}) collective-permute-start(f32[64,512]{1,0:T(8,128)S(1)} %select_select_fusion.1), channel_id=1, source_target_pairs={{0,384},{32,416},{64,448},{96,480},{1,385},{33,417},{65,449},{97,4... | collective-permute-start | bytes 393224 | tf_op jit(solution)/shard_map/ppermute | solution.py:300
  11.1 1.4 %collective-permute-start.4 = (f32[64,512]{1,0:T(8,128)S(1)}, f32[64,512]{1,0:T(8,128)S(1)}, u32[]{:S(2)}, u32[]{:S(2)}) collective-permute-start(f32[64,512]{1,0:T(8,128)S(1)} %select_select_fusion.1), channel_id=1, source_target_pairs={{0,128},{32,160},{64,192},{96,224},{1,129},{33,161},{65,193},{97,2... | collective-permute-start | bytes 393224 | tf_op jit(solution)/shard_map/ppermute | solution.py:300
  11.8 0.7 collective-permute-start.5
  12.5 28.3 %copy-start = (f32[256,512]{1,0:T(8,128)S(1)}, f32[256,512]{1,0:T(8,128)}, u32[]{:S(2)}) copy-start(f32[256,512]{1,0:T(8,128)} %a_ref.3) | copy-start | bytes 1572868
  12.6 28.2 %collective-permute-start.6 = (f32[64,512]{1,0:T(8,128)S(1)}, f32[64,512]{1,0:T(8,128)S(1)}, u32[]{:S(2)}, u32[]{:S(2)}) collective-permute-start(f32[64,512]{1,0:T(8,128)S(1)} %select_select_fusion), channel_id=1, source_target_pairs={{0,16},{32,48},{64,80},{96,112},{128,144},{160,176},{192,208},{224... | collective-permute-start | bytes 393224 | tf_op jit(solution)/shard_map/ppermute | solution.py:300
  61.3 32.8 %all-to-all-start.1 = ((f32[32,8,128]{2,1,0:T(8,128)}), f32[32,8,128]{2,1,0:T(8,128)S(1)}, u32[]{:S(2)}, u32[]{:S(2)}) async-start(f32[32,8,128]{2,1,0:T(8,128)} %get-tuple-element.229), calls=%async_computation.1 | async-start | bytes 262144 | tf_op jit(solution)/shard_map/all_to_all | solution.py:317
  114.2 0.8 copy-start.2

commit v2 on v1

v2 whole, which is shorter than its diff:
```python
import jax
import jax.numpy as jnp
from jax import lax
from jax.experimental import pallas as pl
from jax.experimental.pallas import tpu as pltpu
from jax.sharding import PartitionSpec as P

B = 32
ROWS = 32
COLS = 16
PIECE = 16
LANES = 128
EPS = 1e-06
AMPLIFY_MAX = 16.0
GRAM_MIN = 1e-06
GRAM_MAX = 1e08
VALUE_MAX = 1e25

HIGHEST = lax.Precision.HIGHEST


def gather(shard, axis, count):
    return lax.all_to_all(jnp.broadcast_to(shard[None], (count, *shard.shape)), axis, 0, 0)


def householder(panel_cols):
    count = panel_cols.shape[0]
    width = panel_cols.shape[1]
    rows_at = jnp.arange(count, dtype=jnp.int32)

    def sweep(column_at, carried):
        working, reflectors = carried
        column = lax.dynamic_slice_in_dim(working, column_at, 1, 1)[:, 0]
        pivot = width + column_at
        below = jnp.where(rows_at >= pivot, column, 0.0)
        col_norm = jnp.sqrt(jnp.sum(below * below))
        pivot_value = lax.dynamic_slice_in_dim(column, pivot, 1, 0)[0]
        pivot_sign = jnp.where(pivot_value >= 0.0, 1.0, -1.0)
        vector = below + jnp.where(rows_at == pivot, pivot_sign * col_norm, 0.0)
        vector = vector / jnp.sqrt(jnp.sum(vector * vector) + EPS)
        weights = jnp.dot(vector, working, precision=HIGHEST)
        working = working - 2.0 * vector[:, None] * weights[None, :]
        reflectors = lax.dynamic_update_slice_in_dim(reflectors, vector[:, None], column_at, 1)
        return (working, reflectors)

    finished, reflectors = lax.fori_loop(0, width, sweep, (panel_cols, jnp.zeros_like(panel_cols)))
    gram = jnp.dot(reflectors.T, reflectors, precision=HIGHEST)
    order = jnp.arange(width, dtype=jnp.int32)

    def extend(column_at, triangle):
        earlier = jnp.where(
            order < column_at, lax.dynamic_slice_in_dim(gram, column_at, 1, 1)[:, 0], 0.0
        )
        column = -2.0 * jnp.dot(triangle, earlier, precision=HIGHEST) + jnp.where(
            order == column_at, 2.0, 0.0
        )
        return lax.dynamic_update_slice_in_dim(triangle, column[:, None], column_at, 1)

    triangle = lax.fori_loop(0, width, extend, jnp.zeros((width, width), panel_cols.dtype))
    return (reflectors, triangle)


def general_path(matrix, strip):
    rows_dev = matrix.shape[0]
    cols_dev = matrix.shape[1]
    row_at = lax.axis_index("row")
    col_at = lax.axis_index("col")
    gathered = gather(strip[:B], "col", COLS).transpose(0, 2, 1).reshape(COLS * cols_dev, B)
    rows_at = jnp.arange(gathered.shape[0], dtype=jnp.int32)
    panel_cols = jnp.where(rows_at[:, None] >= B, gathered, 0.0)
    reflectors, triangle = householder(panel_cols)
    own_rows = lax.dynamic_slice_in_dim(reflectors, row_at * rows_dev, rows_dev, 0)
    own_cols = lax.dynamic_slice_in_dim(reflectors, col_at * cols_dev, cols_dev, 0)
    row_product = jnp.sum(gather(jnp.dot(matrix, own_cols, precision=HIGHEST), "col", COLS), axis=0)
    row_scaled = jnp.dot(row_product, triangle, precision=HIGHEST)
    whole = gather(row_scaled, "row", ROWS).reshape(ROWS * rows_dev, B)
    inner = jnp.dot(reflectors.T, whole, precision=HIGHEST)
    col_scaled = lax.dynamic_slice_in_dim(whole, col_at * cols_dev, cols_dev, 0)
    correction = jnp.dot(triangle.T, inner, precision=HIGHEST)
    row_coupled = row_scaled - 0.5 * jnp.dot(own_rows, correction, precision=HIGHEST)
    col_coupled = col_scaled - 0.5 * jnp.dot(own_cols, correction, precision=HIGHEST)
    left = jnp.concatenate([row_coupled, own_rows], axis=1)
    right = jnp.concatenate([own_cols, col_coupled], axis=1)
    return matrix - lax.dot_general(left, right, (((1,), (1,)), ((), ())), precision=HIGHEST)


def dot(a, b, over=((1,), (0,))):
    return lax.dot_general(
        a, b, (over, ((), ())), precision=HIGHEST, preferred_element_type=jnp.float32
    )


def dot_nt(a, b):
    return dot(a, b, ((1,), (1,)))


def dot_tn(a, b):
    return dot(a, b, ((0,), (0,)))


def iota(shape, axis):
    return lax.broadcasted_iota(jnp.int32, shape, axis)


def beyond(x):
    return jnp.max(jnp.where(jnp.abs(x) <= VALUE_MAX, 0.0, 1.0), keepdims=True)


def fold(square):
    group = iota((8, LANES), 1) // B
    packed = square[0:8]
    for k in range(1, B // 8):
        packed = jnp.where(group == k, pltpu.roll(square[8 * k : 8 * k + 8], B * k, 1), packed)
    return packed


def unfold(packed):
    parts = [packed] + [pltpu.roll(packed, LANES - B * k, 1) for k in range(1, B // 8)]
    return jnp.concatenate(parts, axis=0)[:, :B]


def partial_kernel(a_ref, strip_ref, out_ref):
    first_col = lax.axis_index("col") == 0
    strip = strip_ref[0:B, :]
    start = jnp.where(first_col, 2 * B, 0)
    below_t = jnp.where(iota(strip.shape, 1) >= start, strip, 0.0)
    padded = jnp.concatenate([below_t, jnp.zeros((LANES - B, strip.shape[1]), jnp.float32)], axis=0)
    a = a_ref[...]
    rows = a.shape[0]
    product = dot_nt(a, padded)
    near = pltpu.roll(a[:, :LANES], B, 1)
    piece = jnp.where(iota((rows, LANES), 1) < B, product, near)
    out_ref[:, 0:PIECE, :] = piece.reshape(COLS, PIECE, LANES)
    gram = fold(dot_nt(below_t, padded))
    corner = fold(strip_ref[B : 2 * B, :LANES])
    out_ref[:, PIECE : PIECE + 8, :] = jnp.broadcast_to(gram[None], (COLS, 8, LANES))
    out_ref[:, PIECE + 8 : PIECE + 16, :] = jnp.broadcast_to(corner[None], (COLS, 8, LANES))


def sum_kernel(in_ref, out_ref, piece_ref, gram_ref):
    lane = iota((PIECE, LANES), 1)
    total = jnp.sum(in_ref[:, 0:PIECE, :], axis=0)
    piece = jnp.where(lane < B, total, in_ref[0, 0:PIECE, :])
    bad = jnp.where(beyond(jnp.where(lane < 3 * B, piece, 0.0)) > 0.0, jnp.inf, 0.0)
    piece = jnp.where(lane < B, piece + bad, piece)
    piece_ref[...] = piece
    half = PIECE // 2
    folded = jnp.where(
        iota((half, LANES), 1) < 2 * B, piece[:half], pltpu.roll(piece[half:], LANES // 2, 1)
    )
    out_ref[...] = jnp.broadcast_to(folded[None], (ROWS, half, LANES))
    gram_ref[0:8, :] = jnp.sum(in_ref[:, PIECE : PIECE + 8, :], axis=0)
    gram_ref[8:16, :] = in_ref[0, PIECE + 8 : PIECE + 16, :]


def factor_kernel(gram_ref, out_ref, flag_ref):
    gram = unfold(gram_ref[0:8, :])
    sub = iota((B, B), 0)
    lane = iota((B, B), 1)
    eye = jnp.where(sub == lane, 1.0, 0.0)

    def column(of, j):
        return jnp.broadcast_to(of[:, j : j + 1], (B, B))

    def total(x):
        return jnp.sum(x, axis=0, keepdims=True)

    work = unfold(gram_ref[8:16, :])
    coef = eye
    image = gram
    top = jnp.zeros((B, B), jnp.float32)
    coefs = jnp.zeros((B, B), jnp.float32)
    images = jnp.zeros((B, B), jnp.float32)
    wrong = jnp.zeros((1, B), jnp.float32)
    x_top, x_coef, x_image = column(work, 0), column(coef, 0), column(image, 0)
    for j in range(B):
        pivot = x_top[j : j + 1, :]
        norm2 = total(x_top * x_top + x_coef * x_image)
        inner = total(x_top * work + x_coef * image)
        wrong = jnp.where(norm2 > 0.0, wrong, 1.0)
        norm = norm2 * lax.rsqrt(norm2)
        scale = lax.rsqrt(2.0 * (norm2 + jnp.abs(pivot) * norm) + EPS)
        signed = jnp.where(pivot >= 0.0, norm, -norm)
        v_top = scale * jnp.where(sub == j, x_top + signed, x_top)
        v_coef = scale * x_coef
        v_image = scale * x_image
        top = jnp.where(lane == j, v_top, top)
        coefs = jnp.where(lane == j, v_coef, coefs)
        images = jnp.where(lane == j, v_image, images)
        if j + 1 < B:
            y_top, y_coef, y_image = column(work, j + 1), column(coef, j + 1), column(image, j + 1)
            near = total(x_top * y_top + x_coef * y_image)
            near = (2.0 * scale) * (near + signed * y_top[j : j + 1, :])
            twice = (2.0 * scale) * (inner + signed * work[j : j + 1, :])
            work = work - v_top * twice
            coef = coef - v_coef * twice
            image = image - v_image * twice
            x_top = jnp.where(sub > j, y_top - v_top * near, 0.0)
            x_coef = y_coef - v_coef * near
            x_image = y_image - v_image * near
    vectors = jnp.concatenate([coefs, top], axis=0)
    overlap = dot_tn(vectors, jnp.concatenate([images, top], axis=0))
    upper = jnp.where(sub < lane, overlap, 0.0)
    triangle = 2.0 * eye
    for k in range(B - 1, 0, -1):
        triangle = triangle - (2.0 * column(upper, k)) * triangle[k : k + 1, :]
    out_ref[0] = vectors
    out_ref[1] = dot(vectors, triangle)
    diag = jnp.sum(jnp.where(sub == lane, gram, 0.0), axis=1, keepdims=True)
    growth = total(jnp.abs(coefs) * jnp.sqrt(diag))
    wrong = jnp.where(growth <= AMPLIFY_MAX, wrong, 1.0)
    outside = jnp.where((diag >= GRAM_MIN) & (diag <= GRAM_MAX), 0.0, 1.0)
    wrong = jnp.maximum(jnp.max(wrong, keepdims=True), jnp.max(outside, keepdims=True))
    flag_ref[...] = jnp.broadcast_to(jnp.where(wrong > 0.0, jnp.inf, 0.0), flag_ref.shape)


def inner_kernel(in_ref, piece_ref, factor_ref, flag_ref, strip_ref, out_ref):
    col_at = lax.axis_index("col")
    half = PIECE // 2
    count = ROWS * PIECE
    folded = in_ref[...]
    second = pltpu.roll(folded.reshape(ROWS * half, LANES), LANES // 2, 1).reshape(folded.shape)
    rows = jnp.concatenate([folded, second], axis=1)
    order = iota(rows.shape, 0) * (COLS * PIECE) + col_at * PIECE + iota(rows.shape, 1)
    lane = iota(rows.shape, 2)
    product = jnp.where(lane < B, rows, 0.0)
    below = jnp.where((order >= 2 * B) & (lane >= B) & (lane < 2 * B), rows, 0.0)
    square = dot_tn(below.reshape(count, LANES), product.reshape(count, LANES))[B : 2 * B, :B]
    bad = beyond(product.reshape(count, LANES)) > 0.0
    near = jnp.concatenate(
        [jnp.where(col_at == k, product[0], 0.0) for k in (2, 3)], axis=0
    )[:, :B]
    corner = pltpu.roll(strip_ref[B : 2 * B, :LANES], LANES - B, 1)[:, :B]
    corner = jnp.where(col_at == 0, corner, 0.0)
    vectors_t = factor_ref[1]
    coefs_t = vectors_t[:B]
    top_t = vectors_t[B:]
    images = jnp.concatenate(
        [dot(square, coefs_t) + dot_tn(near, top_t), dot(near, coefs_t) + dot(corner, top_t)], axis=0
    )
    padded = jnp.concatenate([images, jnp.zeros((2 * B, LANES - B), jnp.float32)], axis=1)
    inner = fold(dot_tn(vectors_t, padded))
    inner = inner + jnp.where(bad, jnp.inf, flag_ref[0:1, 0:1])
    out_ref[:, 0:PIECE, :] = jnp.broadcast_to(piece_ref[...][None], (COLS, PIECE, LANES))
    pairs = in_ref[...].reshape(COLS, 2, half, LANES)
    flat = (COLS * half, LANES)
    even, odd = pairs[:, 0].reshape(flat), pairs[:, 1].reshape(flat)
    group = iota(flat, 1) // B
    packed = jnp.where(group == 0, even, pltpu.roll(even, LANES - B, 1))
    packed = jnp.where(group == 2, pltpu.roll(odd, 2 * B, 1), packed)
    packed = jnp.where(group == 3, pltpu.roll(odd, B, 1), packed)
    out_ref[:, PIECE : PIECE + 8, :] = packed.reshape(COLS, half, LANES)
    out_ref[:, PIECE + 8 : PIECE + 16, :] = jnp.broadcast_to(inner[None], (COLS, 8, LANES))


def update_kernel(a_ref, strip_ref, in_ref, factor_ref, out_ref, ok_ref):
    first_row = lax.axis_index("row") == 0
    first_col = lax.axis_index("col") == 0
    packed = jnp.sum(in_ref[:, PIECE + 8 : PIECE + 16, :], axis=0)
    ok_ref[0, 0] = 1 - jnp.max(beyond(packed)).astype(jnp.int32)
    shift = 0.5 * unfold(packed)
    vectors = factor_ref[0]
    vectors_t = factor_ref[1]
    zero = jnp.zeros((B, B), jnp.float32)
    vector = jnp.concatenate([zero, vectors[:B], zero, vectors[B:]], axis=0)
    coupled = jnp.concatenate([vectors_t[:B], zero, vectors_t[B:], zero], axis=0)
    coupled = coupled - dot(vector, shift)
    middle = dot_nt(coupled, vector) + dot_nt(vector, coupled)
    rows = a_ref.shape[0]
    left = in_ref[:, 0:PIECE, :].reshape(rows, LANES)
    at = iota(left.shape, 0)
    lane = iota(left.shape, 1)
    start = jnp.where(first_row, 2 * B, 0)
    left = jnp.where((lane >= B) & (lane < 2 * B) & (at < start), 0.0, left)
    unit = jnp.where(first_row & (at - B == lane - 3 * B), 1.0, 0.0)
    left = jnp.where(lane >= 3 * B, unit, left)
    scaled = dot(left, middle)
    strip = strip_ref[0:B, :]
    lane_c = iota(strip.shape, 1)
    start_c = jnp.where(first_col, 2 * B, 0)
    below_t = jnp.where(lane_c >= start_c, strip, 0.0)
    unit_t = jnp.where(first_col & (iota(strip.shape, 0) == lane_c - B), 1.0, 0.0)
    block = in_ref[:, PIECE : PIECE + 8, :]
    flat = block.reshape(COLS * 8, LANES)
    quarter = [block] + [pltpu.roll(flat, LANES - B * k, 1).reshape(block.shape) for k in (1, 2, 3)]
    parts = []
    for k in (0, 2):
        unfolded = jnp.concatenate([quarter[k], quarter[k + 1]], axis=1)
        parts.append(jnp.transpose(unfolded.reshape(COLS * PIECE, LANES))[:B])
    product_t = jnp.concatenate(parts, axis=1)
    right = jnp.concatenate([product_t, below_t, strip_ref[B : 2 * B, :], unit_t], axis=0)
    out_ref[...] = a_ref[...] - dot(scaled, right)


def call(kernel, *shapes, smem=()):
    vmem = pl.BlockSpec(memory_space=pltpu.VMEM)
    specs = [
        pl.BlockSpec(memory_space=pltpu.SMEM) if k in smem else vmem for k in range(len(shapes))
    ]
    return pl.pallas_call(
        kernel,
        out_shape=list(shapes),
        out_specs=specs,
        compiler_params=pltpu.CompilerParams(vmem_limit_bytes=32 * 1024 * 1024),
    )


def array(*shape, dtype=jnp.float32):
    return jax.ShapeDtypeStruct(shape, dtype)


def spread(strip):
    strip = jnp.where(lax.axis_index("row") == 0, strip, 0.0)
    held = [0]
    for step in (4, 2, 16, 8, 1):
        strip = strip + lax.ppermute(strip, "row", [(k, k + step) for k in held])
        held = held + [k + step for k in held]
    return strip


def on_device(matrix):
    strip = spread(matrix[: 2 * B, :])
    (sent,) = call(partial_kernel, array(COLS, 2 * PIECE, LANES))(matrix, strip)
    got = lax.all_to_all(sent, "col", 0, 0)
    sent, piece, gram = call(
        sum_kernel, array(ROWS, PIECE // 2, LANES), array(PIECE, LANES), array(16, LANES)
    )(got)
    factor, flag = call(factor_kernel, array(2, 2 * B, B), array(8, LANES))(gram)
    got = lax.all_to_all(sent, "row", 0, 0)
    (sent,) = call(inner_kernel, array(COLS, 2 * PIECE, LANES))(got, piece, factor, flag, strip)
    got = lax.all_to_all(sent, "col", 0, 0)
    fast, fine = call(
        update_kernel, array(*matrix.shape), array(1, 1, dtype=jnp.int32), smem=(1,)
    )(matrix, strip, got, factor)
    return lax.cond(fine[0, 0] > 0, lambda: fast, lambda: general_path(matrix, strip))


def solution(mesh):
    return jax.shard_map(
        on_device,
        mesh=mesh,
        in_specs=(P("row", "col"),),
        out_specs=P("row", "col"),
        check_vma=False,
    )
```

time: 122 us -> 112 us (0.918)
  waiting for transfers between devices: 35.6 us -> 52.9 us
  blocking collectives: 35.6 us -> 18.8 us
  between operations: 14.3 us -> 0.81 us
  starting transfers between devices: 21.5 us -> 28.5 us
  Pallas kernels: 12.1 us -> 8.24 us
    all_to_all x2 -> x1, blocking collectives: 35.6 us -> 18.8 us  [on_device(): got = lax.all_to_all(sent, 'col', 0, 0)]
    all_to_all x0 -> x1, waiting for transfers between devices: none -> 10.1 us  [on_device(): got = lax.all_to_all(sent, 'col', 0, 0)]
    all_to_all x0 -> x1, starting transfers between devices: none -> 4.77 us  [on_device(): got = lax.all_to_all(sent, 'col', 0, 0)]
    all_to_all x1, waiting for transfers between devices: 8.88 us -> 13.6 us  [on_device(): got = lax.all_to_all(sent, 'row', 0, 0)]
    pallas_call x3, Pallas kernels: 9.01 us -> 5.19 us  [the longest x1 2.81 us: on_device(): call(factor_kernel, array(2, 2 * B, B), array(8, LANES))(gram)]
    all_to_all x1, starting transfers between devices: 16.1 us -> 19.7 us  [on_device(): got = lax.all_to_all(sent, 'row', 0, 0)]
    ppermute x7 -> x5, waiting for transfers between devices: 26.7 us -> 29.2 us  [spread(): strip = strip + lax.ppermute(strip, 'row', [(k, k + step) for k in held])]
    ppermute x7 -> x5, starting transfers between devices: 5.44 us -> 4.1 us  [spread(): strip = strip + lax.ppermute(strip, 'row', [(k, k + step) for k in held])]
  transfers between devices with their start and end apart: 8 -> 7, of which waited for: 2 -> 3; matrix products, arithmetic and copies ran while one was open for 0% -> 0% of each run, Pallas kernels for 6% -> 3%
where the time goes in v2:
time: 112 us
  waiting for transfers between devices  52.9 us (47%)
  starting transfers between devices  28.5 us (25%)
  blocking collectives  18.8 us (17%)
  Pallas kernels  8.24 us (7%)
  other arithmetic  1.92 us (2%)
    ppermute x5, waiting for transfers between devices, spread(): strip = strip + lax.ppermute(strip, 'row', [(k, k + step) for k in held])  29.2 us
    all_to_all x1, starting transfers between devices, on_device(): got = lax.all_to_all(sent, 'row', 0, 0)  19.7 us
    all_to_all x1, blocking collectives, on_device(): got = lax.all_to_all(sent, 'col', 0, 0)  18.8 us
    all_to_all x1, waiting for transfers between devices, on_device(): got = lax.all_to_all(sent, 'row', 0, 0)  13.6 us
    all_to_all x1, waiting for transfers between devices, on_device(): got = lax.all_to_all(sent, 'col', 0, 0)  10.1 us
    all_to_all x1, starting transfers between devices, on_device(): got = lax.all_to_all(sent, 'col', 0, 0)  4.77 us
    ppermute x5, starting transfers between devices, spread(): strip = strip + lax.ppermute(strip, 'row', [(k, k + step) for k in held])  4.1 us
    pallas_call x1, Pallas kernels, on_device(): call(factor_kernel, array(2, 2 * B, B), array(8, LANES))(gram)  2.81 us
  transfers between devices with their start and end apart: 7, of which 3 were waited for; matrix products, arithmetic and copies ran while one was open for 0% of the time, Pallas kernels for 3%

profile of v2, /device:TPU:1, one launch (start us, length us, event | category | flops | bytes accessed | tf_op | source)
XLA Modules:
  0.0 111.9 jit_solution(11657670899689905560)
XLA Ops:
  0.0 0.9 slice_select_fusion
  0.9 0.7 collective-permute-start
  1.6 0.0 collective-permute-done
  1.6 0.9 fusion.50
  2.5 0.7 collective-permute-start.1
  3.2 0.0 copy-start
  3.3 0.8 collective-permute-start.2
  4.1 0.0 collective-permute-done.2
  4.1 0.7 collective-permute-start.3
  4.8 0.0 collective-permute-done.3
  4.8 1.3 %collective-permute-start.4 = (f32[64,512]{1,0:T(8,128)S(1)}, f32[64,512]{1,0:T(8,128)S(1)}, u32[]{:S(2)}, u32[]{:S(2)}) collective-permute-start(f32[64,512]{1,0:T(8,128)S(1)} %add.152), channel_id=1, source_target_pairs={{0,16},{64,80},{32,48},{96,112},{256,272},{320,336},{288,304},{352... | collective-permute-start | bytes 393224 | tf_op jit(solution)/shard_map/ppermute | solution.py:316
  6.1 29.2 %collective-permute-done.4 = f32[64,512]{1,0:T(8,128)S(1)} collective-permute-done((f32[64,512]{1,0:T(8,128)S(1)}, f32[64,512]{1,0:T(8,128)S(1)}, u32[]{:S(2)}, u32[]{:S(2)}) %collective-permute-start.4) | collective-permute-done | bytes 131104 | tf_op jit(solution)/shard_map/ppermute | solution.py:316
  35.3 0.7 shard_map.19
  36.0 18.8 %all_to_all.27.in_ref = f32[16,32,128]{2,1,0:T(8,128)S(1)} all-to-all(f32[16,32,128]{2,1,0:T(8,128)S(1)} %shard_map.19), channel_id=1, replica_groups=mesh['row'=32,'col'=16] {'col'}, dimensions={0} | all-to-all | bytes 524288 | tf_op jit(solution)/shard_map/all_to_all | solution.py:324
  54.8 0.9 shard_map.20
  55.7 19.7 %all-to-all-start.4 = ((f32[32,8,128]{2,1,0:T(8,128)}), f32[32,8,128]{2,1,0:T(8,128)S(1)}, u32[]{:S(2)}, u32[]{:S(2)}) async-start(f32[32,8,128]{2,1,0:T(8,128)} %get-tuple-element.234), calls=%async_computation.4 | async-start | bytes 262144 | tf_op jit(solution)/shard_map/all_to_all | solution.py:329
  75.4 2.8 %shard_map.21 = (f32[2,64,32]{2,1,0:T(8,128)S(1)}, f32[8,128]{1,0:T(8,128)S(1)}) custom-call(f32[16,128]{1,0:T(8,128)S(1)} %get-tuple-element.236.gram_ref), custom_call_target="tpu_custom_call" | custom-call | tf_op jit(solution)/shard_map/pallas_call | solution.py:328
  78.2 13.6 %all-to-all-done.4.in_ref = f32[32,8,128]{2,1,0:T(8,128)S(1)} async-done(((f32[32,8,128]{2,1,0:T(8,128)}), f32[32,8,128]{2,1,0:T(8,128)S(1)}, u32[]{:S(2)}, u32[]{:S(2)}) %all-to-all-start.4) | async-done | bytes 131104 | tf_op jit(solution)/shard_map/all_to_all | solution.py:329
  91.7 1.7 %shard_map.22 = f32[16,32,128]{2,1,0:T(8,128)} custom-call(f32[32,8,128]{2,1,0:T(8,128)S(1)} %all-to-all-done.4.in_ref, f32[16,128]{1,0:T(8,128)S(1)} %get-tuple-element.235.piece_ref, f32[2,64,32]{2,1,0:T(8,128)S(1)} %get-tuple-element.237.factor_ref, f32[8,128]{1,0:T(8,128)S(1)} %get-tuple-element.238.flag_ref, f32[64,512]{1,0:T(8,128)S(1)} %add.153.strip_ref), custom_call_target="tpu_custom_call" | custom-call | tf_op jit(solution)/shard_map/pallas_call | solution.py:330
  93.4 4.8 %all-to-all-start.5 = ((f32[16,32,128]{2,1,0:T(8,128)}), f32[16,32,128]{2,1,0:T(8,128)S(1)}, u32[]{:S(2)}, u32[]{:S(2)}) async-start(f32[16,32,128]{2,1,0:T(8,128)} %shard_map.22), calls=%async_computation.5 | async-start | bytes 524288 | tf_op jit(solution)/shard_map/all_to_all | solution.py:331
  98.2 10.1 %all-to-all-done.5.in_ref = f32[16,32,128]{2,1,0:T(8,128)S(1)} async-done(((f32[16,32,128]{2,1,0:T(8,128)}), f32[16,32,128]{2,1,0:T(8,128)S(1)}, u32[]{:S(2)}, u32[]{:S(2)}) %all-to-all-start.5) | async-done | bytes 262176 | tf_op jit(solution)/shard_map/all_to_all | solution.py:331
  108.3 2.2 %shard_map.23 = (f32[256,512]{1,0:T(8,128)S(1)}, s32[1,1]{1,0:T(1,128)}) custom-call(f32[256,512]{1,0:T(8,128)S(1)} %copy-done, f32[64,512]{1,0:T(8,128)S(1)} %add.153.strip_ref, f32[16,32,128]{2,1,0:T(8,128)S(1)} %all-to-all-done.5.in_ref, f32[2,64,32]{2,1,0:T(8,128)S(1)} %get-tuple-element.237.factor_ref), custom_call_target="tpu_custom_call" | custom-call | tf_op jit(solution)/shard_map/pallas_call | solution.py:332
  111.1 0.0 copy-start.1
  111.2 0.8 copy-done.1
  (7 shorter events, 0.1 us)
Async XLA Ops:
  0.9 0.7 collective-permute-start
  2.5 0.7 collective-permute-start.1
  3.2 32.1 %copy-start = (f32[256,512]{1,0:T(8,128)S(1)}, f32[256,512]{1,0:T(8,128)}, u32[]{:S(2)}) copy-start(f32[256,512]{1,0:T(8,128)} %a_ref.3) | copy-start | bytes 1572868
  3.3 0.8 collective-permute-start.2
  4.1 0.7 collective-permute-start.3
  4.8 30.5 %collective-permute-start.4 = (f32[64,512]{1,0:T(8,128)S(1)}, f32[64,512]{1,0:T(8,128)S(1)}, u32[]{:S(2)}, u32[]{:S(2)}) collective-permute-start(f32[64,512]{1,0:T(8,128)S(1)} %add.152), channel_id=1, source_target_pairs={{0,16},{64,80},{32,48},{96,112},{256,272},{320,336},{288,304},{352... | collective-permute-start | bytes 393224 | tf_op jit(solution)/shard_map/ppermute | solution.py:316
  55.7 36.1 %all-to-all-start.4 = ((f32[32,8,128]{2,1,0:T(8,128)}), f32[32,8,128]{2,1,0:T(8,128)S(1)}, u32[]{:S(2)}, u32[]{:S(2)}) async-start(f32[32,8,128]{2,1,0:T(8,128)} %get-tuple-element.234), calls=%async_computation.4 | async-start | bytes 262144 | tf_op jit(solution)/shard_map/all_to_all | solution.py:329
  93.4 14.9 %all-to-all-start.5 = ((f32[16,32,128]{2,1,0:T(8,128)}), f32[16,32,128]{2,1,0:T(8,128)S(1)}, u32[]{:S(2)}, u32[]{:S(2)}) async-start(f32[16,32,128]{2,1,0:T(8,128)} %shard_map.22), calls=%async_computation.5 | async-start | bytes 524288 | tf_op jit(solution)/shard_map/all_to_all | solution.py:331
  111.1 0.8 copy-start.1

commit v3 on v2

--- a/solution.py
+++ b/solution.py
@@ -121,32 +121,42 @@
 
 def partial_kernel(a_ref, strip_ref, out_ref):
     first_col = lax.axis_index("col") == 0
-    strip = strip_ref[0:B, :]
+    strip = strip_ref[...]
     start = jnp.where(first_col, 2 * B, 0)
     below_t = jnp.where(iota(strip.shape, 1) >= start, strip, 0.0)
     padded = jnp.concatenate([below_t, jnp.zeros((LANES - B, strip.shape[1]), jnp.float32)], axis=0)
     a = a_ref[...]
     rows = a.shape[0]
     product = dot_nt(a, padded)
-    near = pltpu.roll(a[:, :LANES], B, 1)
-    piece = jnp.where(iota((rows, LANES), 1) < B, product, near)
+    zero = jnp.zeros((B, rows), jnp.float32)
+    panel = jnp.transpose(
+        jnp.concatenate([zero, strip[:, :rows], strip[:, rows:], zero], axis=0)
+    )
+    lane = iota((rows, LANES), 1)
+    piece = jnp.where(lane < B, product, panel)
+    piece = jnp.where(lane >= 3 * B, pltpu.roll(a[:, :LANES], 2 * B, 1), piece)
     out_ref[:, 0:PIECE, :] = piece.reshape(COLS, PIECE, LANES)
     gram = fold(dot_nt(below_t, padded))
-    corner = fold(strip_ref[B : 2 * B, :LANES])
+    corner = fold(pltpu.roll(panel[B : 2 * B], LANES - B, 1))
     out_ref[:, PIECE : PIECE + 8, :] = jnp.broadcast_to(gram[None], (COLS, 8, LANES))
     out_ref[:, PIECE + 8 : PIECE + 16, :] = jnp.broadcast_to(corner[None], (COLS, 8, LANES))
 
 
 def sum_kernel(in_ref, out_ref, piece_ref, gram_ref):
+    row_at = lax.axis_index("row")
     lane = iota((PIECE, LANES), 1)
     total = jnp.sum(in_ref[:, 0:PIECE, :], axis=0)
-    piece = jnp.where(lane < B, total, in_ref[0, 0:PIECE, :])
+    panel = in_ref[row_at // 2, 0:PIECE, :]
+    panel = jnp.where(row_at % 2 == 0, panel, pltpu.roll(panel, LANES - B, 1))
+    other = pltpu.roll(in_ref[0, 0:PIECE, :], LANES - B, 1)
+    piece = jnp.where(lane < B, total, jnp.where(lane < 2 * B, panel, other))
     bad = jnp.where(beyond(jnp.where(lane < 3 * B, piece, 0.0)) > 0.0, jnp.inf, 0.0)
     piece = jnp.where(lane < B, piece + bad, piece)
     piece_ref[...] = piece
     half = PIECE // 2
+    near = jnp.where(lane < B, piece, pltpu.roll(piece, LANES - B, 1))
     folded = jnp.where(
-        iota((half, LANES), 1) < 2 * B, piece[:half], pltpu.roll(piece[half:], LANES // 2, 1)
+        iota((half, LANES), 1) < 2 * B, near[:half], pltpu.roll(near[half:], LANES // 2, 1)
     )
     out_ref[...] = jnp.broadcast_to(folded[None], (ROWS, half, LANES))
     gram_ref[0:8, :] = jnp.sum(in_ref[:, PIECE : PIECE + 8, :], axis=0)
@@ -214,24 +224,28 @@
     flag_ref[...] = jnp.broadcast_to(jnp.where(wrong > 0.0, jnp.inf, 0.0), flag_ref.shape)
 
 
-def inner_kernel(in_ref, piece_ref, factor_ref, flag_ref, strip_ref, out_ref):
+def unfold_rows(block):
+    flat = block.reshape(COLS * 8, LANES)
+    upper = pltpu.roll(flat, LANES // 2, 1).reshape(block.shape)
+    return jnp.concatenate([block, upper], axis=1).reshape(COLS * PIECE, LANES)
+
+
+def inner_kernel(in_ref, panel_ref, piece_ref, factor_ref, flag_ref, out_ref):
     col_at = lax.axis_index("col")
-    half = PIECE // 2
-    count = ROWS * PIECE
-    folded = in_ref[...]
-    second = pltpu.roll(folded.reshape(ROWS * half, LANES), LANES // 2, 1).reshape(folded.shape)
-    rows = jnp.concatenate([folded, second], axis=1)
-    order = iota(rows.shape, 0) * (COLS * PIECE) + col_at * PIECE + iota(rows.shape, 1)
-    lane = iota(rows.shape, 2)
-    product = jnp.where(lane < B, rows, 0.0)
-    below = jnp.where((order >= 2 * B) & (lane >= B) & (lane < 2 * B), rows, 0.0)
-    square = dot_tn(below.reshape(count, LANES), product.reshape(count, LANES))[B : 2 * B, :B]
-    bad = beyond(product.reshape(count, LANES)) > 0.0
+    pairs = in_ref[...].reshape(COLS, 2, PIECE // 2, LANES)
+    first, second = unfold_rows(pairs[:, 0]), unfold_rows(pairs[:, 1])
+    panel = panel_ref[:, 0:PIECE, :]
+    source = iota(panel.shape, 0)
+    order = iota(panel.shape, 1) + col_at * PIECE
+    above = (source == 0) & (order < 2 * B) & (iota(panel.shape, 2) < 2 * B)
+    below = jnp.where(above, 0.0, panel).reshape(COLS * PIECE, LANES)
+    square = dot_tn(below, first)[B : 2 * B, :B] + dot_tn(below, second)[2 * B : 3 * B, :B]
+    bad = beyond(in_ref[...].reshape(ROWS * PIECE // 2, LANES)) > 0.0
     near = jnp.concatenate(
-        [jnp.where(col_at == k, product[0], 0.0) for k in (2, 3)], axis=0
-    )[:, :B]
-    corner = pltpu.roll(strip_ref[B : 2 * B, :LANES], LANES - B, 1)[:, :B]
-    corner = jnp.where(col_at == 0, corner, 0.0)
+        [jnp.where(col_at == k, first[:PIECE], 0.0) for k in (2, 3)], axis=0
+    )
+    corner = pltpu.roll(near, LANES - B, 1)[:, :B]
+    near = near[:, :B]
     vectors_t = factor_ref[1]
     coefs_t = vectors_t[:B]
     top_t = vectors_t[B:]
@@ -242,21 +256,14 @@
     inner = fold(dot_tn(vectors_t, padded))
     inner = inner + jnp.where(bad, jnp.inf, flag_ref[0:1, 0:1])
     out_ref[:, 0:PIECE, :] = jnp.broadcast_to(piece_ref[...][None], (COLS, PIECE, LANES))
-    pairs = in_ref[...].reshape(COLS, 2, half, LANES)
-    flat = (COLS * half, LANES)
-    even, odd = pairs[:, 0].reshape(flat), pairs[:, 1].reshape(flat)
-    group = iota(flat, 1) // B
-    packed = jnp.where(group == 0, even, pltpu.roll(even, LANES - B, 1))
-    packed = jnp.where(group == 2, pltpu.roll(odd, 2 * B, 1), packed)
-    packed = jnp.where(group == 3, pltpu.roll(odd, B, 1), packed)
-    out_ref[:, PIECE : PIECE + 8, :] = packed.reshape(COLS, half, LANES)
-    out_ref[:, PIECE + 8 : PIECE + 16, :] = jnp.broadcast_to(inner[None], (COLS, 8, LANES))
+    out_ref[:, PIECE : 2 * PIECE, :] = in_ref[...].reshape(COLS, PIECE, LANES)
+    out_ref[:, 2 * PIECE : 2 * PIECE + 8, :] = jnp.broadcast_to(inner[None], (COLS, 8, LANES))
 
 
 def update_kernel(a_ref, strip_ref, in_ref, factor_ref, out_ref, ok_ref):
     first_row = lax.axis_index("row") == 0
     first_col = lax.axis_index("col") == 0
-    packed = jnp.sum(in_ref[:, PIECE + 8 : PIECE + 16, :], axis=0)
+    packed = jnp.sum(in_ref[:, 2 * PIECE : 2 * PIECE + 8, :], axis=0)
     ok_ref[0, 0] = 1 - jnp.max(beyond(packed)).astype(jnp.int32)
     shift = 0.5 * unfold(packed)
     vectors = factor_ref[0]
@@ -275,20 +282,17 @@
     unit = jnp.where(first_row & (at - B == lane - 3 * B), 1.0, 0.0)
     left = jnp.where(lane >= 3 * B, unit, left)
     scaled = dot(left, middle)
-    strip = strip_ref[0:B, :]
+    strip = strip_ref[...]
     lane_c = iota(strip.shape, 1)
     start_c = jnp.where(first_col, 2 * B, 0)
     below_t = jnp.where(lane_c >= start_c, strip, 0.0)
     unit_t = jnp.where(first_col & (iota(strip.shape, 0) == lane_c - B), 1.0, 0.0)
-    block = in_ref[:, PIECE : PIECE + 8, :]
-    flat = block.reshape(COLS * 8, LANES)
-    quarter = [block] + [pltpu.roll(flat, LANES - B * k, 1).reshape(block.shape) for k in (1, 2, 3)]
-    parts = []
-    for k in (0, 2):
-        unfolded = jnp.concatenate([quarter[k], quarter[k + 1]], axis=1)
-        parts.append(jnp.transpose(unfolded.reshape(COLS * PIECE, LANES))[:B])
-    product_t = jnp.concatenate(parts, axis=1)
-    right = jnp.concatenate([product_t, below_t, strip_ref[B : 2 * B, :], unit_t], axis=0)
+    halves = [
+        jnp.transpose(unfold_rows(in_ref[:, PIECE + 8 * k : PIECE + 8 * k + 8, :]))[: 2 * B]
+        for k in range(2)
+    ]
+    both = jnp.concatenate(halves, axis=1)
+    right = jnp.concatenate([both[:B], below_t, both[B:], unit_t], axis=0)
     out_ref[...] = a_ref[...] - dot(scaled, right)
 
 
@@ -311,23 +315,29 @@
 
 def spread(strip):
     strip = jnp.where(lax.axis_index("row") == 0, strip, 0.0)
-    held = [0]
-    for step in (4, 2, 16, 8, 1):
-        strip = strip + lax.ppermute(strip, "row", [(k, k + step) for k in held])
-        held = held + [k + step for k in held]
+    for stage in (
+        [[(0, 8 * x)] for x in (2, 1, 3)],
+        [[(8 * x, 8 * x + 2 * z) for x in range(4)] for z in (1, 3)],
+        [[(8 * x + 2, 8 * x + 4) for x in range(4)]],
+        [[(k, k + 1) for k in range(0, ROWS, 2)]],
+    ):
+        held = strip
+        for pairs in stage:
+            held = held + lax.ppermute(strip, "row", pairs)
+        strip = held
     return strip
 
 
 def on_device(matrix):
-    strip = spread(matrix[: 2 * B, :])
+    strip = spread(matrix[:B, :])
     (sent,) = call(partial_kernel, array(COLS, 2 * PIECE, LANES))(matrix, strip)
-    got = lax.all_to_all(sent, "col", 0, 0)
+    panel = lax.all_to_all(sent, "col", 0, 0)
     sent, piece, gram = call(
         sum_kernel, array(ROWS, PIECE // 2, LANES), array(PIECE, LANES), array(16, LANES)
-    )(got)
+    )(panel)
     factor, flag = call(factor_kernel, array(2, 2 * B, B), array(8, LANES))(gram)
     got = lax.all_to_all(sent, "row", 0, 0)
-    (sent,) = call(inner_kernel, array(COLS, 2 * PIECE, LANES))(got, piece, factor, flag, strip)
+    (sent,) = call(inner_kernel, array(COLS, 2 * PIECE + 8, LANES))(got, panel, piece, factor, flag)
     got = lax.all_to_all(sent, "col", 0, 0)
     fast, fine = call(
         update_kernel, array(*matrix.shape), array(1, 1, dtype=jnp.int32), smem=(1,)

time: 112 us -> 103 us (0.920)
  waiting for transfers between devices: 52.9 us -> 41.5 us
  starting transfers between devices: 28.5 us -> 33.8 us
  blocking collectives: 18.8 us -> 15.6 us
    ppermute x5 -> x7, waiting for transfers between devices: 29.2 us -> 16.8 us  [spread(): held = held + lax.ppermute(strip, 'row', pairs)]
    all_to_all x1, starting transfers between devices: 19.7 us -> 23.6 us  [on_device(): got = lax.all_to_all(sent, 'row', 0, 0)]
    all_to_all x1, blocking collectives: 18.8 us -> 15.6 us  [on_device(): panel = lax.all_to_all(sent, 'col', 0, 0)]
    ppermute x5 -> x7, starting transfers between devices: 4.1 us -> 5.4 us  [spread(): held = held + lax.ppermute(strip, 'row', pairs)]
  transfers between devices with their start and end apart: 7 -> 9, of which waited for: 3 -> 3; matrix products, arithmetic and copies ran while one was open for 0% -> 0% of each run, Pallas kernels for 3% -> 3%
where the time goes in v3:
time: 103 us; the launch traced here: 102 us
  waiting for transfers between devices  41.5 us (40%)
  starting transfers between devices  33.8 us (33%)
  blocking collectives  15.6 us (15%)
  Pallas kernels  8.29 us (8%)
  other arithmetic  1.75 us (2%)
    all_to_all x1, starting transfers between devices, on_device(): got = lax.all_to_all(sent, 'row', 0, 0)  23.6 us
    ppermute x7, waiting for transfers between devices, spread(): held = held + lax.ppermute(strip, 'row', pairs)  16.8 us
    all_to_all x1, blocking collectives, on_device(): panel = lax.all_to_all(sent, 'col', 0, 0)  15.6 us
    all_to_all x1, waiting for transfers between devices, on_device(): got = lax.all_to_all(sent, 'row', 0, 0)  13.6 us
    all_to_all x1, waiting for transfers between devices, on_device(): got = lax.all_to_all(sent, 'col', 0, 0)  11.1 us
    ppermute x7, starting transfers between devices, spread(): held = held + lax.ppermute(strip, 'row', pairs)  5.4 us
    all_to_all x1, starting transfers between devices, on_device(): got = lax.all_to_all(sent, 'col', 0, 0)  4.76 us
    pallas_call x1, Pallas kernels, on_device(): call(factor_kernel, array(2, 2 * B, B), array(8, LANES))(gram)  2.81 us
  transfers between devices with their start and end apart: 9, of which 3 were waited for; matrix products, arithmetic and copies ran while one was open for 0% of the time, Pallas kernels for 3%

profile of v3, /device:TPU:1, one launch (start us, length us, event | category | flops | bytes accessed | tf_op | source)
XLA Modules:
  0.0 102.5 jit_solution(11879238494247925817)
XLA Ops:
  0.0 0.8 slice_select_fusion
  0.8 0.8 collective-permute-start.2
  1.6 0.7 collective-permute-start.1
  2.3 0.7 collective-permute-start
  3.0 0.0 collective-permute-done.2
  3.0 0.0 collective-permute-done.1
  3.0 0.9 add_add_fusion.1
  3.9 0.7 collective-permute-start.4
  4.6 0.7 collective-permute-start.3
  5.3 0.7 collective-permute-start.5
  6.0 1.3 %collective-permute-start.6 = (f32[32,512]{1,0:T(8,128)S(1)}, f32[32,512]{1,0:T(8,128)S(1)}, u32[]{:S(2)}, u32[]{:S(2)}) collective-permute-start(f32[32,512]{1,0:T(8,128)S(1)} %add.160), channel_id=1, source_target_pairs={{0,16},{32,48},{64,80},{96,112},{128,144},{160,176},{192,208},{224... | collective-permute-start | bytes 196616 | tf_op jit(solution)/shard_map/ppermute | solution.py:326
  7.3 16.8 %collective-permute-done.6 = f32[32,512]{1,0:T(8,128)S(1)} collective-permute-done((f32[32,512]{1,0:T(8,128)S(1)}, f32[32,512]{1,0:T(8,128)S(1)}, u32[]{:S(2)}, u32[]{:S(2)}) %collective-permute-start.6) | collective-permute-done | bytes 65568 | tf_op jit(solution)/shard_map/ppermute | solution.py:326
  24.1 0.7 shard_map.19
  24.8 15.6 %all_to_all.27.in_ref.panel_ref = f32[16,32,128]{2,1,0:T(8,128)S(1)} all-to-all(f32[16,32,128]{2,1,0:T(8,128)S(1)} %shard_map.19), channel_id=1, replica_groups=mesh['row'=32,'col'=16] {'col'}, dimensions={0} | all-to-all | bytes 524288 | tf_op jit(solution)/shard_map/all_to_all | solution.py:334
  40.3 1.0 shard_map.20
  41.3 23.6 %all-to-all-start.4 = ((f32[32,8,128]{2,1,0:T(8,128)}), f32[32,8,128]{2,1,0:T(8,128)S(1)}, u32[]{:S(2)}, u32[]{:S(2)}) async-start(f32[32,8,128]{2,1,0:T(8,128)} %get-tuple-element.234), calls=%async_computation.4 | async-start | bytes 262144 | tf_op jit(solution)/shard_map/all_to_all | solution.py:339
  65.0 2.8 %shard_map.21 = (f32[2,64,32]{2,1,0:T(8,128)S(1)}, f32[8,128]{1,0:T(8,128)S(1)}) custom-call(f32[16,128]{1,0:T(8,128)S(1)} %get-tuple-element.236.gram_ref), custom_call_target="tpu_custom_call" | custom-call | tf_op jit(solution)/shard_map/pallas_call | solution.py:338
  67.8 13.6 %all-to-all-done.4.in_ref = f32[32,8,128]{2,1,0:T(8,128)S(1)} async-done(((f32[32,8,128]{2,1,0:T(8,128)}), f32[32,8,128]{2,1,0:T(8,128)S(1)}, u32[]{:S(2)}, u32[]{:S(2)}) %all-to-all-start.4) | async-done | bytes 131104 | tf_op jit(solution)/shard_map/all_to_all | solution.py:339
  81.3 1.6 %shard_map.22 = f32[16,40,128]{2,1,0:T(8,128)} custom-call(f32[32,8,128]{2,1,0:T(8,128)S(1)} %all-to-all-done.4.in_ref, f32[16,32,128]{2,1,0:T(8,128)S(1)} %all_to_all.27.in_ref.panel_ref, f32[16,128]{1,0:T(8,128)S(1)} %get-tuple-element.235.piece_ref, f32[2,64,32]{2,1,0:T(8,128)S(1)} %get-tuple-element.237.factor_ref, f32[8,128]{1,0:T(8,128)S(1)} %get-tuple-element.238.flag_ref), custom_call_target="tpu_custom_call" | custom-call | tf_op jit(solution)/shard_map/pallas_call | solution.py:340
  83.0 4.8 %all-to-all-start.5 = ((f32[16,40,128]{2,1,0:T(8,128)}), f32[16,40,128]{2,1,0:T(8,128)S(1)}, u32[]{:S(2)}, u32[]{:S(2)}) async-start(f32[16,40,128]{2,1,0:T(8,128)} %shard_map.22), calls=%async_computation.5 | async-start | bytes 655360 | tf_op jit(solution)/shard_map/all_to_all | solution.py:341
  87.7 11.1 %all-to-all-done.5.in_ref = f32[16,40,128]{2,1,0:T(8,128)S(1)} async-done(((f32[16,40,128]{2,1,0:T(8,128)}), f32[16,40,128]{2,1,0:T(8,128)S(1)}, u32[]{:S(2)}, u32[]{:S(2)}) %all-to-all-start.5) | async-done | bytes 327712 | tf_op jit(solution)/shard_map/all_to_all | solution.py:341
  98.8 2.2 %shard_map.23 = (f32[256,512]{1,0:T(8,128)S(1)}, s32[1,1]{1,0:T(1,128)}) custom-call(f32[256,512]{1,0:T(8,128)S(1)} %copy-done, f32[32,512]{1,0:T(8,128)S(1)} %add.161.strip_ref, f32[16,40,128]{2,1,0:T(8,128)S(1)} %all-to-all-done.5.in_ref, f32[2,64,32]{2,1,0:T(8,128)S(1)} %get-tuple-element.237.factor_ref), custom_call_target="tpu_custom_call" | custom-call | tf_op jit(solution)/shard_map/pallas_call | solution.py:342
  101.7 0.0 copy-start.1
  101.7 0.8 copy-done.1
  (10 shorter events, 0.1 us)
Async XLA Ops:
  0.8 23.2 %copy-start = (f32[256,512]{1,0:T(8,128)S(1)}, f32[256,512]{1,0:T(8,128)}, u32[]{:S(2)}) copy-start(f32[256,512]{1,0:T(8,128)} %a_ref.3) | copy-start | bytes 1572868
  0.8 2.1 %collective-permute-start.2 = (f32[32,512]{1,0:T(8,128)S(1)}, f32[32,512]{1,0:T(8,128)S(1)}, u32[]{:S(2)}, u32[]{:S(2)}) collective-permute-start(f32[32,512]{1,0:T(8,128)S(1)} %slice_select_fusion), channel_id=1, source_target_pairs={{0,384},{1,385},{2,386},{3,387},{4,388},{5,389},{6,390},{7,391},{8... | collective-permute-start | bytes 196616 | tf_op jit(solution)/shard_map/ppermute | solution.py:326
  1.6 1.4 %collective-permute-start.1 = (f32[32,512]{1,0:T(8,128)S(1)}, f32[32,512]{1,0:T(8,128)S(1)}, u32[]{:S(2)}, u32[]{:S(2)}) collective-permute-start(f32[32,512]{1,0:T(8,128)S(1)} %slice_select_fusion), channel_id=1, source_target_pairs={{0,128},{1,129},{2,130},{3,131},{4,132},{5,133},{6,134},{7,135},{8... | collective-permute-start | bytes 196616 | tf_op jit(solution)/shard_map/ppermute | solution.py:326
  2.3 0.7 collective-permute-start
  3.9 1.3 %collective-permute-start.4 = (f32[32,512]{1,0:T(8,128)S(1)}, f32[32,512]{1,0:T(8,128)S(1)}, u32[]{:S(2)}, u32[]{:S(2)}) collective-permute-start(f32[32,512]{1,0:T(8,128)S(1)} %add_add_fusion.1), channel_id=1, source_target_pairs={{0,96},{128,224},{256,352},{384,480},{1,97},{129,225},{257,353},{3... | collective-permute-start | bytes 196616 | tf_op jit(solution)/shard_map/ppermute | solution.py:326
  4.6 0.7 collective-permute-start.3
  5.3 0.7 collective-permute-start.5
  6.0 18.1 %collective-permute-start.6 = (f32[32,512]{1,0:T(8,128)S(1)}, f32[32,512]{1,0:T(8,128)S(1)}, u32[]{:S(2)}, u32[]{:S(2)}) collective-permute-start(f32[32,512]{1,0:T(8,128)S(1)} %add.160), channel_id=1, source_target_pairs={{0,16},{32,48},{64,80},{96,112},{128,144},{160,176},{192,208},{224... | collective-permute-start | bytes 196616 | tf_op jit(solution)/shard_map/ppermute | solution.py:326
  41.3 40.0 %all-to-all-start.4 = ((f32[32,8,128]{2,1,0:T(8,128)}), f32[32,8,128]{2,1,0:T(8,128)S(1)}, u32[]{:S(2)}, u32[]{:S(2)}) async-start(f32[32,8,128]{2,1,0:T(8,128)} %get-tuple-element.234), calls=%async_computation.4 | async-start | bytes 262144 | tf_op jit(solution)/shard_map/all_to_all | solution.py:339
  83.0 15.9 %all-to-all-start.5 = ((f32[16,40,128]{2,1,0:T(8,128)}), f32[16,40,128]{2,1,0:T(8,128)S(1)}, u32[]{:S(2)}, u32[]{:S(2)}) async-start(f32[16,40,128]{2,1,0:T(8,128)} %shard_map.22), calls=%async_computation.5 | async-start | bytes 655360 | tf_op jit(solution)/shard_map/all_to_all | solution.py:341
  101.7 0.8 copy-start.1

commit v4 on v3

--- a/solution.py
+++ b/solution.py
@@ -314,18 +314,29 @@
 
 
 def spread(strip):
-    strip = jnp.where(lax.axis_index("row") == 0, strip, 0.0)
-    for stage in (
-        [[(0, 8 * x)] for x in (2, 1, 3)],
-        [[(8 * x, 8 * x + 2 * z) for x in range(4)] for z in (1, 3)],
-        [[(8 * x + 2, 8 * x + 4) for x in range(4)]],
-        [[(k, k + 1) for k in range(0, ROWS, 2)]],
-    ):
-        held = strip
-        for pairs in stage:
-            held = held + lax.ppermute(strip, "row", pairs)
-        strip = held
-    return strip
+    row_at = lax.axis_index("row")
+    x_at = row_at // 8
+    strip = lax.optimization_barrier(jnp.where(row_at == 0, strip, 0.0))
+    width = strip.shape[1] // 4
+    held = strip[:, :width]
+    for x in (2, 1, 3):
+        held = held + lax.ppermute(strip[:, x * width : (x + 1) * width], "row", [(0, 8 * x)])
+    near = held
+    for z in (1, 3):
+        near = near + lax.ppermute(held, "row", [(8 * x, 8 * x + 2 * z) for x in range(4)])
+    own = near + lax.ppermute(near, "row", [(8 * x + 2, 8 * x + 4) for x in range(4)])
+    of = [own]
+    for step in (1, 2, 3):
+        pairs = [(8 * x + z, 8 * ((x + step) % 4) + z) for x in range(4) for z in (0, 2, 4, 6)]
+        of.append(lax.ppermute(own, "row", pairs))
+    quarters = []
+    for quarter in range(4):
+        found = of[0]
+        for step in (1, 2, 3):
+            found = jnp.where(x_at == (quarter + step) % 4, of[step], found)
+        quarters.append(found)
+    strip = jnp.concatenate(quarters, axis=1)
+    return strip + lax.ppermute(strip, "row", [(k, k + 1) for k in range(0, ROWS, 2)])
 
 
 def on_device(matrix):

time: 103 us -> 110 us (1.068)
  waiting for transfers between devices: 41.5 us -> 53.2 us
  starting transfers between devices: 33.8 us -> 29.8 us
    ppermute x7 -> x10, waiting for transfers between devices: 16.8 us -> 28.5 us  [the longest x1 28.5 us: spread(): lax.ppermute(strip, 'row', [(k, k + 1) for k in range(0, ROWS, 2)])]
    all_to_all x1, starting transfers between devices: 23.6 us -> 17.8 us  [on_device(): got = lax.all_to_all(sent, 'row', 0, 0)]
    ppermute x7 -> x10, starting transfers between devices: 5.4 us -> 7.25 us  [the longest x3 1.99 us: spread(): of.append(lax.ppermute(own, 'row', pairs))]
  transfers between devices with their start and end apart: 9 -> 12, of which waited for: 3 -> 3; matrix products, arithmetic and copies ran while one was open for 0% -> 0% of each run, Pallas kernels for 3% -> 3%
where the time goes in v4:
time: 110 us
  waiting for transfers between devices  53.2 us (48%)
  starting transfers between devices  29.8 us (27%)
  blocking collectives  15.6 us (14%)
  Pallas kernels  8.28 us (8%)
    ppermute x1, waiting for transfers between devices, spread(): lax.ppermute(strip, 'row', [(k, k + 1) for k in range(0, ROWS, 2)])  28.5 us
    all_to_all x1, starting transfers between devices, on_device(): got = lax.all_to_all(sent, 'row', 0, 0)  17.8 us
    all_to_all x1, blocking collectives, on_device(): panel = lax.all_to_all(sent, 'col', 0, 0)  15.6 us
    all_to_all x1, waiting for transfers between devices, on_device(): got = lax.all_to_all(sent, 'row', 0, 0)  13.6 us
    all_to_all x1, waiting for transfers between devices, on_device(): got = lax.all_to_all(sent, 'col', 0, 0)  11.1 us
    all_to_all x1, starting transfers between devices, on_device(): got = lax.all_to_all(sent, 'col', 0, 0)  4.77 us
    pallas_call x1, Pallas kernels, on_device(): call(factor_kernel, array(2, 2 * B, B), array(8, LANES))(gram)  2.81 us
  transfers between devices with their start and end apart: 12, of which 3 were waited for; matrix products, arithmetic and copies ran while one was open for 0% of the time, Pallas kernels for 3%

profile of v4, /device:TPU:1, one launch (start us, length us, event | category | flops | bytes accessed | tf_op | source)
XLA Modules:
  0.0 109.5 jit_solution(18312478560705269458)
XLA Ops:
  0.0 0.9 slice_select_fusion
  0.9 0.7 collective-permute-start.2
  1.6 0.7 collective-permute-start.1
  2.3 0.7 collective-permute-start
  3.0 0.7 collective-permute-start.4
  3.7 0.7 collective-permute-start.3
  4.4 0.7 collective-permute-start.5
  5.1 0.7 collective-permute-start.6
  5.7 0.7 collective-permute-start.7
  6.4 0.7 collective-permute-start.8
  7.2 1.3 %collective-permute-start.9 = (f32[32,512]{1,0:T(8,128)S(1)}, f32[32,512]{1,0:T(8,128)S(1)}, u32[]{:S(2)}, u32[]{:S(2)}) collective-permute-start(f32[32,512]{1,0:T(8,128)S(1)} %pad_maximum_fusion), channel_id=1, source_target_pairs={{0,16},{32,48},{64,80},{96,112},{128,144},{160,176},{192,208},{224... | collective-permute-start | bytes 196616 | tf_op jit(solution)/shard_map/ppermute | solution.py:339
  8.5 28.5 %collective-permute-done.9 = f32[32,512]{1,0:T(8,128)S(1)} collective-permute-done((f32[32,512]{1,0:T(8,128)S(1)}, f32[32,512]{1,0:T(8,128)S(1)}, u32[]{:S(2)}, u32[]{:S(2)}) %collective-permute-start.9) | collective-permute-done | bytes 65568 | tf_op jit(solution)/shard_map/ppermute | solution.py:339
  37.0 0.7 shard_map.19
  37.6 15.6 %all_to_all.27.in_ref.panel_ref = f32[16,32,128]{2,1,0:T(8,128)S(1)} all-to-all(f32[16,32,128]{2,1,0:T(8,128)S(1)} %shard_map.19), channel_id=1, replica_groups=mesh['row'=32,'col'=16] {'col'}, dimensions={0} | all-to-all | bytes 524288 | tf_op jit(solution)/shard_map/all_to_all | solution.py:345
  53.2 1.0 shard_map.20
  54.2 17.8 %all-to-all-start.4 = ((f32[32,8,128]{2,1,0:T(8,128)}), f32[32,8,128]{2,1,0:T(8,128)S(1)}, u32[]{:S(2)}, u32[]{:S(2)}) async-start(f32[32,8,128]{2,1,0:T(8,128)} %get-tuple-element.234), calls=%async_computation.4 | async-start | bytes 262144 | tf_op jit(solution)/shard_map/all_to_all | solution.py:350
  72.0 2.8 %shard_map.21 = (f32[2,64,32]{2,1,0:T(8,128)S(1)}, f32[8,128]{1,0:T(8,128)S(1)}) custom-call(f32[16,128]{1,0:T(8,128)S(1)} %get-tuple-element.236.gram_ref), custom_call_target="tpu_custom_call" | custom-call | tf_op jit(solution)/shard_map/pallas_call | solution.py:349
  74.8 13.6 %all-to-all-done.4.in_ref = f32[32,8,128]{2,1,0:T(8,128)S(1)} async-done(((f32[32,8,128]{2,1,0:T(8,128)}), f32[32,8,128]{2,1,0:T(8,128)S(1)}, u32[]{:S(2)}, u32[]{:S(2)}) %all-to-all-start.4) | async-done | bytes 131104 | tf_op jit(solution)/shard_map/all_to_all | solution.py:350
  88.4 1.6 %shard_map.22 = f32[16,40,128]{2,1,0:T(8,128)} custom-call(f32[32,8,128]{2,1,0:T(8,128)S(1)} %all-to-all-done.4.in_ref, f32[16,32,128]{2,1,0:T(8,128)S(1)} %all_to_all.27.in_ref.panel_ref, f32[16,128]{1,0:T(8,128)S(1)} %get-tuple-element.235.piece_ref, f32[2,64,32]{2,1,0:T(8,128)S(1)} %get-tuple-element.237.factor_ref, f32[8,128]{1,0:T(8,128)S(1)} %get-tuple-element.238.flag_ref), custom_call_target="tpu_custom_call" | custom-call | tf_op jit(solution)/shard_map/pallas_call | solution.py:351
  90.0 4.8 %all-to-all-start.5 = ((f32[16,40,128]{2,1,0:T(8,128)}), f32[16,40,128]{2,1,0:T(8,128)S(1)}, u32[]{:S(2)}, u32[]{:S(2)}) async-start(f32[16,40,128]{2,1,0:T(8,128)} %shard_map.22), calls=%async_computation.5 | async-start | bytes 655360 | tf_op jit(solution)/shard_map/all_to_all | solution.py:352
  94.8 11.1 %all-to-all-done.5.in_ref = f32[16,40,128]{2,1,0:T(8,128)S(1)} async-done(((f32[16,40,128]{2,1,0:T(8,128)}), f32[16,40,128]{2,1,0:T(8,128)S(1)}, u32[]{:S(2)}, u32[]{:S(2)}) %all-to-all-start.5) | async-done | bytes 327712 | tf_op jit(solution)/shard_map/all_to_all | solution.py:352
  105.9 2.2 %shard_map.23 = (f32[256,512]{1,0:T(8,128)S(1)}, s32[1,1]{1,0:T(1,128)}) custom-call(f32[256,512]{1,0:T(8,128)S(1)} %copy-done, f32[32,512]{1,0:T(8,128)S(1)} %fusion.30.strip_ref, f32[16,40,128]{2,1,0:T(8,128)S(1)} %all-to-all-done.5.in_ref, f32[2,64,32]{2,1,0:T(8,128)S(1)} %get-tuple-element.237.factor_ref), custom_call_target="tpu_custom_call" | custom-call | tf_op jit(solution)/shard_map/pallas_call | solution.py:353
  108.7 0.0 copy-start.1
  108.7 0.8 copy-done.1
  (19 shorter events, 0.1 us)
Async XLA Ops:
  0.0 36.9 %copy-start = (f32[256,512]{1,0:T(8,128)S(1)}, f32[256,512]{1,0:T(8,128)}, u32[]{:S(2)}) copy-start(f32[256,512]{1,0:T(8,128)} %a_ref.3) | copy-start | bytes 1572868
  0.9 2.0 %collective-permute-start.2 = (f32[32,128]{1,0:T(8,128)S(1)}, f32[32,128]{1,0:T(8,128)S(1)}, u32[]{:S(2)}, u32[]{:S(2)}) collective-permute-start(f32[32,128]{1,0:T(8,128)S(1)} %get-tuple-element.320), channel_id=1, source_target_pairs={{0,384},{1,385},{2,386},{3,387},{4,388},{5,389},{6,390},{7,391},{8... | collective-permute-start | bytes 49160 | tf_op jit(solution)/shard_map/ppermute | solution.py:323
  1.6 1.4 %collective-permute-start.1 = (f32[32,128]{1,0:T(8,128)S(1)}, f32[32,128]{1,0:T(8,128)S(1)}, u32[]{:S(2)}, u32[]{:S(2)}) collective-permute-start(f32[32,128]{1,0:T(8,128)S(1)} %get-tuple-element.321), channel_id=1, source_target_pairs={{0,128},{1,129},{2,130},{3,131},{4,132},{5,133},{6,134},{7,135},{8... | collective-permute-start | bytes 49160 | tf_op jit(solution)/shard_map/ppermute | solution.py:323
  2.3 0.7 collective-permute-start
  3.0 1.3 %collective-permute-start.4 = (f32[32,128]{1,0:T(8,128)S(1)}, f32[32,128]{1,0:T(8,128)S(1)}, u32[]{:S(2)}, u32[]{:S(2)}) collective-permute-start(f32[32,128]{1,0:T(8,128)S(1)} %fusion.29), channel_id=1, source_target_pairs={{0,96},{128,224},{256,352},{384,480},{1,97},{129,225},{257,353},{3... | collective-permute-start | bytes 49160 | tf_op jit(solution)/shard_map/ppermute | solution.py:326
  3.7 0.7 collective-permute-start.3
  4.4 0.7 collective-permute-start.5
  5.1 2.0 %collective-permute-start.6 = (f32[32,128]{1,0:T(8,128)S(1)}, f32[32,128]{1,0:T(8,128)S(1)}, u32[]{:S(2)}, u32[]{:S(2)}) collective-permute-start(f32[32,128]{1,0:T(8,128)S(1)} %add.161), channel_id=1, source_target_pairs={{0,384},{32,416},{64,448},{96,480},{128,0},{160,32},{192,64},{224,... | collective-permute-start | bytes 49160 | tf_op jit(solution)/shard_map/ppermute | solution.py:331
  5.7 1.4 %collective-permute-start.7 = (f32[32,128]{1,0:T(8,128)S(1)}, f32[32,128]{1,0:T(8,128)S(1)}, u32[]{:S(2)}, u32[]{:S(2)}) collective-permute-start(f32[32,128]{1,0:T(8,128)S(1)} %add.161), channel_id=1, source_target_pairs={{0,256},{32,288},{64,320},{96,352},{128,384},{160,416},{192,448},{... | collective-permute-start | bytes 49160 | tf_op jit(solution)/shard_map/ppermute | solution.py:331
  6.4 0.7 collective-permute-start.8
  7.2 29.8 %collective-permute-start.9 = (f32[32,512]{1,0:T(8,128)S(1)}, f32[32,512]{1,0:T(8,128)S(1)}, u32[]{:S(2)}, u32[]{:S(2)}) collective-permute-start(f32[32,512]{1,0:T(8,128)S(1)} %pad_maximum_fusion), channel_id=1, source_target_pairs={{0,16},{32,48},{64,80},{96,112},{128,144},{160,176},{192,208},{224... | collective-permute-start | bytes 196616 | tf_op jit(solution)/shard_map/ppermute | solution.py:339
  54.2 34.2 %all-to-all-start.4 = ((f32[32,8,128]{2,1,0:T(8,128)}), f32[32,8,128]{2,1,0:T(8,128)S(1)}, u32[]{:S(2)}, u32[]{:S(2)}) async-start(f32[32,8,128]{2,1,0:T(8,128)} %get-tuple-element.234), calls=%async_computation.4 | async-start | bytes 262144 | tf_op jit(solution)/shard_map/all_to_all | solution.py:350
  90.0 15.9 %all-to-all-start.5 = ((f32[16,40,128]{2,1,0:T(8,128)}), f32[16,40,128]{2,1,0:T(8,128)S(1)}, u32[]{:S(2)}, u32[]{:S(2)}) async-start(f32[16,40,128]{2,1,0:T(8,128)} %shard_map.22), calls=%async_computation.5 | async-start | bytes 655360 | tf_op jit(solution)/shard_map/all_to_all | solution.py:352
  108.7 0.8 copy-start.1

commit v5 on v3

--- a/solution.py
+++ b/solution.py
@@ -314,17 +314,15 @@
 
 
 def spread(strip):
-    strip = jnp.where(lax.axis_index("row") == 0, strip, 0.0)
-    for stage in (
-        [[(0, 8 * x)] for x in (2, 1, 3)],
-        [[(8 * x, 8 * x + 2 * z) for x in range(4)] for z in (1, 3)],
-        [[(8 * x + 2, 8 * x + 4) for x in range(4)]],
-        [[(k, k + 1) for k in range(0, ROWS, 2)]],
+    strip = lax.optimization_barrier(jnp.where(lax.axis_index("row") == 0, strip, 0.0))
+    for pairs in (
+        [(0, 16)],
+        [(0, 8), (16, 24)],
+        [(8 * x, 8 * x + 2) for x in range(4)],
+        [(8 * x + z, 8 * x + (z + 2 if z else 6)) for x in range(4) for z in (0, 2)],
+        [(k, k + 1) for k in range(0, ROWS, 2)],
     ):
-        held = strip
-        for pairs in stage:
-            held = held + lax.ppermute(strip, "row", pairs)
-        strip = held
+        strip = strip + lax.ppermute(strip, "row", pairs)
     return strip
 
 

time: 103 us -> 98.8 us (0.959)
  starting transfers between devices: 33.8 us -> 28.1 us
  blocking collectives: 15.6 us -> 16.9 us
    all_to_all x1, starting transfers between devices: 23.6 us -> 19.3 us  [on_device(): got = lax.all_to_all(sent, 'row', 0, 0)]
    all_to_all x1, blocking collectives: 15.6 us -> 16.9 us  [on_device(): panel = lax.all_to_all(sent, 'col', 0, 0)]
    ppermute x7 -> x5, starting transfers between devices: 5.4 us -> 4.07 us  [spread(): strip = strip + lax.ppermute(strip, 'row', pairs)]
    ppermute x7 -> x5, waiting for transfers between devices: 16.8 us -> 17.8 us  [spread(): strip = strip + lax.ppermute(strip, 'row', pairs)]
  transfers between devices with their start and end apart: 9 -> 7, of which waited for: 3 -> 3; matrix products, arithmetic and copies ran while one was open for 0% -> 0% of each run, Pallas kernels for 3% -> 3%
where the time goes in v5:
time: 98.8 us; the launch traced here: 98.3 us
  waiting for transfers between devices  42.5 us (43%)
  starting transfers between devices  28.1 us (28%)
  blocking collectives  16.9 us (17%)
  Pallas kernels  8.28 us (8%)
    all_to_all x1, starting transfers between devices, on_device(): got = lax.all_to_all(sent, 'row', 0, 0)  19.3 us
    ppermute x5, waiting for transfers between devices, spread(): strip = strip + lax.ppermute(strip, 'row', pairs)  17.8 us
    all_to_all x1, blocking collectives, on_device(): panel = lax.all_to_all(sent, 'col', 0, 0)  16.9 us
    all_to_all x1, waiting for transfers between devices, on_device(): got = lax.all_to_all(sent, 'row', 0, 0)  13.6 us
    all_to_all x1, waiting for transfers between devices, on_device(): got = lax.all_to_all(sent, 'col', 0, 0)  11.1 us
    all_to_all x1, starting transfers between devices, on_device(): got = lax.all_to_all(sent, 'col', 0, 0)  4.76 us
    ppermute x5, starting transfers between devices, spread(): strip = strip + lax.ppermute(strip, 'row', pairs)  4.07 us
    pallas_call x1, Pallas kernels, on_device(): call(factor_kernel, array(2, 2 * B, B), array(8, LANES))(gram)  2.81 us
  transfers between devices with their start and end apart: 7, of which 3 were waited for; matrix products, arithmetic and copies ran while one was open for 0% of the time, Pallas kernels for 3%

profile of v5, /device:TPU:1, one launch (start us, length us, event | category | flops | bytes accessed | tf_op | source)
XLA Modules:
  0.0 98.3 jit_solution(134099139045354901)
XLA Ops:
  0.0 0.8 slice_select_fusion
  0.8 0.8 collective-permute-start
  1.6 0.0 collective-permute-done
  1.7 0.7 collective-permute-start.1
  2.3 0.0 collective-permute-done.1
  2.4 0.7 collective-permute-start.2
  3.0 0.0 collective-permute-done.2
  3.1 0.7 collective-permute-start.3
  3.7 0.0 collective-permute-done.3
  3.8 1.3 %collective-permute-start.4 = (f32[32,512]{1,0:T(8,128)S(1)}, f32[32,512]{1,0:T(8,128)S(1)}, u32[]{:S(2)}, u32[]{:S(2)}) collective-permute-start(f32[32,512]{1,0:T(8,128)S(1)} %add.152), channel_id=1, source_target_pairs={{0,16},{32,48},{64,80},{96,112},{128,144},{160,176},{192,208},{224... | collective-permute-start | bytes 196616 | tf_op jit(solution)/shard_map/ppermute | solution.py:325
  5.1 17.8 %collective-permute-done.4 = f32[32,512]{1,0:T(8,128)S(1)} collective-permute-done((f32[32,512]{1,0:T(8,128)S(1)}, f32[32,512]{1,0:T(8,128)S(1)}, u32[]{:S(2)}, u32[]{:S(2)}) %collective-permute-start.4) | collective-permute-done | bytes 65568 | tf_op jit(solution)/shard_map/ppermute | solution.py:325
  22.9 0.0 copy-done
  22.9 0.7 shard_map.19
  23.6 16.9 %all_to_all.27.in_ref.panel_ref = f32[16,32,128]{2,1,0:T(8,128)S(1)} all-to-all(f32[16,32,128]{2,1,0:T(8,128)S(1)} %shard_map.19), channel_id=1, replica_groups=mesh['row'=32,'col'=16] {'col'}, dimensions={0} | all-to-all | bytes 524288 | tf_op jit(solution)/shard_map/all_to_all | solution.py:332
  40.6 1.0 %shard_map.20 = (f32[32,8,128]{2,1,0:T(8,128)}, f32[16,128]{1,0:T(8,128)S(1)}, f32[16,128]{1,0:T(8,128)S(1)}) custom-call(f32[16,32,128]{2,1,0:T(8,128)S(1)} %all_to_all.27.in_ref.panel_ref), custom_call_target="tpu_custom_call" | custom-call | tf_op jit(solution)/shard_map/pallas_call | solution.py:333
  41.6 19.3 %all-to-all-start.4 = ((f32[32,8,128]{2,1,0:T(8,128)}), f32[32,8,128]{2,1,0:T(8,128)S(1)}, u32[]{:S(2)}, u32[]{:S(2)}) async-start(f32[32,8,128]{2,1,0:T(8,128)} %get-tuple-element.234), calls=%async_computation.4 | async-start | bytes 262144 | tf_op jit(solution)/shard_map/all_to_all | solution.py:337
  60.9 2.8 %shard_map.21 = (f32[2,64,32]{2,1,0:T(8,128)S(1)}, f32[8,128]{1,0:T(8,128)S(1)}) custom-call(f32[16,128]{1,0:T(8,128)S(1)} %get-tuple-element.236.gram_ref), custom_call_target="tpu_custom_call" | custom-call | tf_op jit(solution)/shard_map/pallas_call | solution.py:336
  63.7 13.6 %all-to-all-done.4.in_ref = f32[32,8,128]{2,1,0:T(8,128)S(1)} async-done(((f32[32,8,128]{2,1,0:T(8,128)}), f32[32,8,128]{2,1,0:T(8,128)S(1)}, u32[]{:S(2)}, u32[]{:S(2)}) %all-to-all-start.4) | async-done | bytes 131104 | tf_op jit(solution)/shard_map/all_to_all | solution.py:337
  77.2 1.6 %shard_map.22 = f32[16,40,128]{2,1,0:T(8,128)} custom-call(f32[32,8,128]{2,1,0:T(8,128)S(1)} %all-to-all-done.4.in_ref, f32[16,32,128]{2,1,0:T(8,128)S(1)} %all_to_all.27.in_ref.panel_ref, f32[16,128]{1,0:T(8,128)S(1)} %get-tuple-element.235.piece_ref, f32[2,64,32]{2,1,0:T(8,128)S(1)} %get-tuple-element.237.factor_ref, f32[8,128]{1,0:T(8,128)S(1)} %get-tuple-element.238.flag_ref), custom_call_target="tpu_custom_call" | custom-call | tf_op jit(solution)/shard_map/pallas_call | solution.py:338
  78.8 4.8 %all-to-all-start.5 = ((f32[16,40,128]{2,1,0:T(8,128)}), f32[16,40,128]{2,1,0:T(8,128)S(1)}, u32[]{:S(2)}, u32[]{:S(2)}) async-start(f32[16,40,128]{2,1,0:T(8,128)} %shard_map.22), calls=%async_computation.5 | async-start | bytes 655360 | tf_op jit(solution)/shard_map/all_to_all | solution.py:339
  83.6 11.1 %all-to-all-done.5.in_ref = f32[16,40,128]{2,1,0:T(8,128)S(1)} async-done(((f32[16,40,128]{2,1,0:T(8,128)}), f32[16,40,128]{2,1,0:T(8,128)S(1)}, u32[]{:S(2)}, u32[]{:S(2)}) %all-to-all-start.5) | async-done | bytes 327712 | tf_op jit(solution)/shard_map/all_to_all | solution.py:339
  94.7 2.2 %shard_map.23 = (f32[256,512]{1,0:T(8,128)S(1)}, s32[1,1]{1,0:T(1,128)}) custom-call(f32[256,512]{1,0:T(8,128)S(1)} %copy-done, f32[32,512]{1,0:T(8,128)S(1)} %add.153.strip_ref, f32[16,40,128]{2,1,0:T(8,128)S(1)} %all-to-all-done.5.in_ref, f32[2,64,32]{2,1,0:T(8,128)S(1)} %get-tuple-element.237.factor_ref), custom_call_target="tpu_custom_call" | custom-call | tf_op jit(solution)/shard_map/pallas_call | solution.py:340
  97.6 0.0 copy-start.1
  97.6 0.8 copy-done.1
  (7 shorter events, 0.1 us)
Async XLA Ops:
  0.8 22.1 %copy-start = (f32[256,512]{1,0:T(8,128)S(1)}, f32[256,512]{1,0:T(8,128)}, u32[]{:S(2)}) copy-start(f32[256,512]{1,0:T(8,128)} %a_ref.3) | copy-start | bytes 1572868
  0.8 0.8 collective-permute-start
  1.7 0.7 collective-permute-start.1
  2.4 0.7 collective-permute-start.2
  3.1 0.7 collective-permute-start.3
  3.8 19.1 %collective-permute-start.4 = (f32[32,512]{1,0:T(8,128)S(1)}, f32[32,512]{1,0:T(8,128)S(1)}, u32[]{:S(2)}, u32[]{:S(2)}) collective-permute-start(f32[32,512]{1,0:T(8,128)S(1)} %add.152), channel_id=1, source_target_pairs={{0,16},{32,48},{64,80},{96,112},{128,144},{160,176},{192,208},{224... | collective-permute-start | bytes 196616 | tf_op jit(solution)/shard_map/ppermute | solution.py:325
  41.6 35.7 %all-to-all-start.4 = ((f32[32,8,128]{2,1,0:T(8,128)}), f32[32,8,128]{2,1,0:T(8,128)S(1)}, u32[]{:S(2)}, u32[]{:S(2)}) async-start(f32[32,8,128]{2,1,0:T(8,128)} %get-tuple-element.234), calls=%async_computation.4 | async-start | bytes 262144 | tf_op jit(solution)/shard_map/all_to_all | solution.py:337
  78.8 15.9 %all-to-all-start.5 = ((f32[16,40,128]{2,1,0:T(8,128)}), f32[16,40,128]{2,1,0:T(8,128)S(1)}, u32[]{:S(2)}, u32[]{:S(2)}) async-start(f32[16,40,128]{2,1,0:T(8,128)} %shard_map.22), calls=%async_computation.5 | async-start | bytes 655360 | tf_op jit(solution)/shard_map/all_to_all | solution.py:339
  97.6 0.8 copy-start.1

commit v6 on v5

--- a/solution.py
+++ b/solution.py
@@ -163,7 +163,15 @@
     gram_ref[8:16, :] = in_ref[0, PIECE + 8 : PIECE + 16, :]
 
 
-def factor_kernel(gram_ref, out_ref, flag_ref):
+def placed(blocks):
+    wide = []
+    for block, quarter in blocks:
+        block = jnp.concatenate([block, jnp.zeros((B, LANES - B), jnp.float32)], axis=1)
+        wide.append(pltpu.roll(block, B * quarter, 1) if quarter else block)
+    return jnp.concatenate(wide, axis=0)
+
+
+def factor_kernel(gram_ref, strip_ref, mix_ref, vectors_ref, out_ref, flag_ref):
     gram = unfold(gram_ref[0:8, :])
     sub = iota((B, B), 0)
     lane = iota((B, B), 1)
@@ -214,8 +222,18 @@
     triangle = 2.0 * eye
     for k in range(B - 1, 0, -1):
         triangle = triangle - (2.0 * column(upper, k)) * triangle[k : k + 1, :]
-    out_ref[0] = vectors
-    out_ref[1] = dot(vectors, triangle)
+    vectors_t = dot(vectors, triangle)
+    vectors_ref[...] = vectors_t
+    coefs_t, top_t = vectors_t[:B], vectors_t[B:]
+    mix_ref[0] = placed([(coefs_t, 0), (coefs, 1), (top_t, 0), (top, 1)])
+    mix_ref[1] = placed([(coefs_t, 0), (top_t, 0), (coefs_t, 1), (top_t, 1)])
+    mix_ref[2] = placed([(coefs_t, 2), (top_t, 2), (coefs_t, 3), (top_t, 3)])
+    first_col = lax.axis_index("col") == 0
+    strip = strip_ref[...]
+    lane_c = iota(strip.shape, 1)
+    below_t = jnp.where(lane_c >= jnp.where(first_col, 2 * B, 0), strip, 0.0)
+    unit_t = jnp.where(first_col & (iota(strip.shape, 0) == lane_c - B), 1.0, 0.0)
+    out_ref[...] = dot_tn(vectors, jnp.concatenate([below_t, unit_t], axis=0))
     diag = jnp.sum(jnp.where(sub == lane, gram, 0.0), axis=1, keepdims=True)
     growth = total(jnp.abs(coefs) * jnp.sqrt(diag))
     wrong = jnp.where(growth <= AMPLIFY_MAX, wrong, 1.0)
@@ -230,23 +248,26 @@
     return jnp.concatenate([block, upper], axis=1).reshape(COLS * PIECE, LANES)
 
 
-def inner_kernel(in_ref, panel_ref, piece_ref, factor_ref, flag_ref, out_ref):
+def inner_kernel(in_ref, panel_ref, piece_ref, mix_ref, vectors_ref, flag_ref, out_ref):
+    row_at = lax.axis_index("row")
     col_at = lax.axis_index("col")
-    pairs = in_ref[...].reshape(COLS, 2, PIECE // 2, LANES)
-    first, second = unfold_rows(pairs[:, 0]), unfold_rows(pairs[:, 1])
+    half = PIECE // 2
+    pairs = in_ref[...].reshape(COLS, 2, half, LANES)
+    even, odd = pairs[:, 0], pairs[:, 1]
+    first, second = unfold_rows(even), unfold_rows(odd)
     panel = panel_ref[:, 0:PIECE, :]
     source = iota(panel.shape, 0)
     order = iota(panel.shape, 1) + col_at * PIECE
     above = (source == 0) & (order < 2 * B) & (iota(panel.shape, 2) < 2 * B)
     below = jnp.where(above, 0.0, panel).reshape(COLS * PIECE, LANES)
     square = dot_tn(below, first)[B : 2 * B, :B] + dot_tn(below, second)[2 * B : 3 * B, :B]
-    bad = beyond(in_ref[...].reshape(ROWS * PIECE // 2, LANES)) > 0.0
+    bad = beyond(in_ref[...].reshape(ROWS * half, LANES)) > 0.0
     near = jnp.concatenate(
         [jnp.where(col_at == k, first[:PIECE], 0.0) for k in (2, 3)], axis=0
     )
     corner = pltpu.roll(near, LANES - B, 1)[:, :B]
     near = near[:, :B]
-    vectors_t = factor_ref[1]
+    vectors_t = vectors_ref[...]
     coefs_t = vectors_t[:B]
     top_t = vectors_t[B:]
     images = jnp.concatenate(
@@ -255,45 +276,40 @@
     padded = jnp.concatenate([images, jnp.zeros((2 * B, LANES - B), jnp.float32)], axis=1)
     inner = fold(dot_tn(vectors_t, padded))
     inner = inner + jnp.where(bad, jnp.inf, flag_ref[0:1, 0:1])
-    out_ref[:, 0:PIECE, :] = jnp.broadcast_to(piece_ref[...][None], (COLS, PIECE, LANES))
-    out_ref[:, PIECE : 2 * PIECE, :] = in_ref[...].reshape(COLS, PIECE, LANES)
-    out_ref[:, 2 * PIECE : 2 * PIECE + 8, :] = jnp.broadcast_to(inner[None], (COLS, 8, LANES))
-
-
-def update_kernel(a_ref, strip_ref, in_ref, factor_ref, out_ref, ok_ref):
-    first_row = lax.axis_index("row") == 0
-    first_col = lax.axis_index("col") == 0
-    packed = jnp.sum(in_ref[:, 2 * PIECE : 2 * PIECE + 8, :], axis=0)
+    piece = piece_ref[...]
+    lane = iota(piece.shape, 1)
+    at = iota(piece.shape, 0) + (row_at * COLS + col_at) * PIECE
+    piece = jnp.where((lane >= B) & (lane < 2 * B) & (at < 2 * B), 0.0, piece)
+    piece = jnp.where(lane >= 3 * B, jnp.where(at - B == lane - 3 * B, 1.0, 0.0), piece)
+    piece = dot(piece, mix_ref[0])
+    piece = jnp.where(lane[:half] < 2 * B, piece[:half], pltpu.roll(piece[half:], LANES // 2, 1))
+    flat = (COLS * half, LANES)
+    columns = dot(even.reshape(flat), mix_ref[1]) + dot(odd.reshape(flat), mix_ref[2])
+    out_ref[:, 0:half, :] = jnp.broadcast_to(piece[None], (COLS, half, LANES))
+    out_ref[:, half : 2 * half, :] = columns.reshape(COLS, half, LANES)
+    out_ref[:, 2 * half : 3 * half, :] = jnp.broadcast_to(inner[None], (COLS, half, LANES))
+
+
+def update_kernel(a_ref, in_ref, right_ref, out_ref, ok_ref):
+    half = PIECE // 2
+    packed = jnp.sum(in_ref[:, 2 * half : 3 * half, :], axis=0)
     ok_ref[0, 0] = 1 - jnp.max(beyond(packed)).astype(jnp.int32)
-    shift = 0.5 * unfold(packed)
-    vectors = factor_ref[0]
-    vectors_t = factor_ref[1]
+    inner = unfold(packed)
+    shift = 0.5 * (inner + jnp.transpose(inner))
+    left = unfold_rows(in_ref[:, 0:half, :])[:, : 2 * B]
     zero = jnp.zeros((B, B), jnp.float32)
-    vector = jnp.concatenate([zero, vectors[:B], zero, vectors[B:]], axis=0)
-    coupled = jnp.concatenate([vectors_t[:B], zero, vectors_t[B:], zero], axis=0)
-    coupled = coupled - dot(vector, shift)
-    middle = dot_nt(coupled, vector) + dot_nt(vector, coupled)
-    rows = a_ref.shape[0]
-    left = in_ref[:, 0:PIECE, :].reshape(rows, LANES)
-    at = iota(left.shape, 0)
-    lane = iota(left.shape, 1)
-    start = jnp.where(first_row, 2 * B, 0)
-    left = jnp.where((lane >= B) & (lane < 2 * B) & (at < start), 0.0, left)
-    unit = jnp.where(first_row & (at - B == lane - 3 * B), 1.0, 0.0)
-    left = jnp.where(lane >= 3 * B, unit, left)
-    scaled = dot(left, middle)
-    strip = strip_ref[...]
-    lane_c = iota(strip.shape, 1)
-    start_c = jnp.where(first_col, 2 * B, 0)
-    below_t = jnp.where(lane_c >= start_c, strip, 0.0)
-    unit_t = jnp.where(first_col & (iota(strip.shape, 0) == lane_c - B), 1.0, 0.0)
-    halves = [
-        jnp.transpose(unfold_rows(in_ref[:, PIECE + 8 * k : PIECE + 8 * k + 8, :]))[: 2 * B]
-        for k in range(2)
-    ]
-    both = jnp.concatenate(halves, axis=1)
-    right = jnp.concatenate([both[:B], below_t, both[B:], unit_t], axis=0)
-    out_ref[...] = a_ref[...] - dot(scaled, right)
+    shift = jnp.concatenate([zero, shift], axis=0)
+    shift = jnp.concatenate([shift, jnp.zeros((2 * B, B), jnp.float32)], axis=1)
+    left = left - dot(left, shift)
+    flat = in_ref[:, half : 2 * half, :].reshape(COLS * half, LANES)
+    quarter = [flat] + [pltpu.roll(flat, LANES - B * k, 1) for k in (1, 2, 3)]
+    quarter = [part.reshape(COLS, half, LANES) for part in quarter]
+    halves = []
+    for k in (0, 2):
+        unfolded = jnp.concatenate([quarter[k], quarter[k + 1]], axis=1)
+        halves.append(jnp.transpose(unfolded.reshape(COLS * PIECE, LANES))[:B])
+    right = jnp.concatenate([right_ref[...], jnp.concatenate(halves, axis=1)], axis=0)
+    out_ref[...] = a_ref[...] - dot(left, right)
 
 
 def call(kernel, *shapes, smem=()):
@@ -333,13 +349,21 @@
     sent, piece, gram = call(
         sum_kernel, array(ROWS, PIECE // 2, LANES), array(PIECE, LANES), array(16, LANES)
     )(panel)
-    factor, flag = call(factor_kernel, array(2, 2 * B, B), array(8, LANES))(gram)
+    mix, vectors, right, flag = call(
+        factor_kernel,
+        array(3, LANES, LANES),
+        array(2 * B, B),
+        array(B, matrix.shape[1]),
+        array(8, LANES),
+    )(gram, strip)
     got = lax.all_to_all(sent, "row", 0, 0)
-    (sent,) = call(inner_kernel, array(COLS, 2 * PIECE + 8, LANES))(got, panel, piece, factor, flag)
+    (sent,) = call(inner_kernel, array(COLS, 3 * PIECE // 2, LANES))(
+        got, panel, piece, mix, vectors, flag
+    )
     got = lax.all_to_all(sent, "col", 0, 0)
     fast, fine = call(
         update_kernel, array(*matrix.shape), array(1, 1, dtype=jnp.int32), smem=(1,)
-    )(matrix, strip, got, factor)
+    )(matrix, got, right)
     return lax.cond(fine[0, 0] > 0, lambda: fast, lambda: general_path(matrix, strip))
 
 

time: 98.8 us -> 96.2 us (0.974)
  waiting for transfers between devices: 42.5 us -> 40.3 us
    all_to_all x1, waiting for transfers between devices: 11.1 us -> 8.99 us  [on_device(): got = lax.all_to_all(sent, 'col', 0, 0)]
where the time goes in v6:
time: 96.2 us; the launch traced here: 95.7 us
  waiting for transfers between devices  40.3 us (42%)
  starting transfers between devices  28.1 us (29%)
  blocking collectives  16.9 us (18%)
  Pallas kernels  7.84 us (8%)
    all_to_all x1, starting transfers between devices, on_device(): got = lax.all_to_all(sent, 'row', 0, 0)  19.3 us
    ppermute x5, waiting for transfers between devices, spread(): strip = strip + lax.ppermute(strip, 'row', pairs)  17.8 us
    all_to_all x1, blocking collectives, on_device(): panel = lax.all_to_all(sent, 'col', 0, 0)  16.9 us
    all_to_all x1, waiting for transfers between devices, on_device(): got = lax.all_to_all(sent, 'row', 0, 0)  13.5 us
    all_to_all x1, waiting for transfers between devices, on_device(): got = lax.all_to_all(sent, 'col', 0, 0)  8.99 us
    all_to_all x1, starting transfers between devices, on_device(): got = lax.all_to_all(sent, 'col', 0, 0)  4.77 us
    ppermute x5, starting transfers between devices, spread(): strip = strip + lax.ppermute(strip, 'row', pairs)  4.07 us
    pallas_call x1, Pallas kernels, on_device(): call(factor_kernel, array(3, LANES, LANES), array(2 * B, B), array(B, mat...  2.89 us
  transfers between devices with their start and end apart: 7, of which 3 were waited for; matrix products, arithmetic and copies ran while one was open for 0% of the time, Pallas kernels for 3%

profile of v6, /device:TPU:1, one launch (start us, length us, event | category | flops | bytes accessed | tf_op | source)
XLA Modules:
  0.0 95.7 jit_solution(17572246388324080349)
XLA Ops:
  0.0 0.8 slice_select_fusion
  0.8 0.8 collective-permute-start
  1.6 0.0 collective-permute-done
  1.7 0.7 collective-permute-start.1
  2.3 0.0 collective-permute-done.1
  2.4 0.7 collective-permute-start.2
  3.0 0.0 collective-permute-done.2
  3.1 0.7 collective-permute-start.3
  3.7 0.0 collective-permute-done.3
  3.8 1.3 %collective-permute-start.4 = (f32[32,512]{1,0:T(8,128)S(1)}, f32[32,512]{1,0:T(8,128)S(1)}, u32[]{:S(2)}, u32[]{:S(2)}) collective-permute-start(f32[32,512]{1,0:T(8,128)S(1)} %add.152), channel_id=1, source_target_pairs={{0,16},{32,48},{64,80},{96,112},{128,144},{160,176},{192,208},{224... | collective-permute-start | bytes 196616 | tf_op jit(solution)/shard_map/ppermute | solution.py:341
  5.1 17.8 %collective-permute-done.4 = f32[32,512]{1,0:T(8,128)S(1)} collective-permute-done((f32[32,512]{1,0:T(8,128)S(1)}, f32[32,512]{1,0:T(8,128)S(1)}, u32[]{:S(2)}, u32[]{:S(2)}) %collective-permute-start.4) | collective-permute-done | bytes 65568 | tf_op jit(solution)/shard_map/ppermute | solution.py:341
  22.9 0.0 copy-done
  22.9 0.7 shard_map.19
  23.6 16.9 %all_to_all.27.in_ref.panel_ref = f32[16,32,128]{2,1,0:T(8,128)S(1)} all-to-all(f32[16,32,128]{2,1,0:T(8,128)S(1)} %shard_map.19), channel_id=1, replica_groups=mesh['row'=32,'col'=16] {'col'}, dimensions={0} | all-to-all | bytes 524288 | tf_op jit(solution)/shard_map/all_to_all | solution.py:348
  40.6 1.0 %shard_map.20 = (f32[32,8,128]{2,1,0:T(8,128)}, f32[16,128]{1,0:T(8,128)S(1)}, f32[16,128]{1,0:T(8,128)S(1)}) custom-call(f32[16,32,128]{2,1,0:T(8,128)S(1)} %all_to_all.27.in_ref.panel_ref), custom_call_target="tpu_custom_call" | custom-call | tf_op jit(solution)/shard_map/pallas_call | solution.py:349
  41.6 19.3 %all-to-all-start.4 = ((f32[32,8,128]{2,1,0:T(8,128)}), f32[32,8,128]{2,1,0:T(8,128)S(1)}, u32[]{:S(2)}, u32[]{:S(2)}) async-start(f32[32,8,128]{2,1,0:T(8,128)} %get-tuple-element.236), calls=%async_computation.4 | async-start | bytes 262144 | tf_op jit(solution)/shard_map/all_to_all | solution.py:359
  60.9 2.9 %shard_map.21 = (f32[3,128,128]{2,1,0:T(8,128)S(1)}, f32[64,32]{1,0:T(8,128)S(1)}, f32[32,512]{1,0:T(8,128)S(1)}, f32[8,128]{1,0:T(8,128)S(1)}) custom-call(f32[16,128]{1,0:T(8,128)S(1)} %get-tuple-element.238.gram_ref, f32[32,512]{1,0:T(8,128)S(1)} %add.153.strip_ref), custom_call_target="tpu_custom_call" | custom-call | tf_op jit(solution)/shard_map/pallas_call | solution.py:352
  63.8 13.5 %all-to-all-done.4.in_ref = f32[32,8,128]{2,1,0:T(8,128)S(1)} async-done(((f32[32,8,128]{2,1,0:T(8,128)}), f32[32,8,128]{2,1,0:T(8,128)S(1)}, u32[]{:S(2)}, u32[]{:S(2)}) %all-to-all-start.4) | async-done | bytes 131104 | tf_op jit(solution)/shard_map/all_to_all | solution.py:359
  77.2 1.8 %shard_map.22 = f32[16,24,128]{2,1,0:T(8,128)} custom-call(f32[32,8,128]{2,1,0:T(8,128)S(1)} %all-to-all-done.4.in_ref, f32[16,32,128]{2,1,0:T(8,128)S(1)} %all_to_all.27.in_ref.panel_ref, f32[16,128]{1,0:T(8,128)S(1)} %get-tuple-element.237.piece_ref, f32[3,128,128]{2,1,0:T(8,128)S(1)} %get-tuple-element.239.mix_ref, ...), custom_call_target="tpu_custom_call" | custom-call | tf_op jit(solution)/shard_map/pallas_call | solution.py:360
  79.0 4.8 %all-to-all-start.5 = ((f32[16,24,128]{2,1,0:T(8,128)}), f32[16,24,128]{2,1,0:T(8,128)S(1)}, u32[]{:S(2)}, u32[]{:S(2)}) async-start(f32[16,24,128]{2,1,0:T(8,128)} %shard_map.22), calls=%async_computation.5 | async-start | bytes 393216 | tf_op jit(solution)/shard_map/all_to_all | solution.py:363
  83.8 9.0 %all-to-all-done.5.in_ref = f32[16,24,128]{2,1,0:T(8,128)S(1)} async-done(((f32[16,24,128]{2,1,0:T(8,128)}), f32[16,24,128]{2,1,0:T(8,128)S(1)}, u32[]{:S(2)}, u32[]{:S(2)}) %all-to-all-start.5) | async-done | bytes 196640 | tf_op jit(solution)/shard_map/all_to_all | solution.py:363
  92.8 1.5 %shard_map.23 = (f32[256,512]{1,0:T(8,128)S(1)}, s32[1,1]{1,0:T(1,128)}) custom-call(f32[256,512]{1,0:T(8,128)S(1)} %copy-done, f32[16,24,128]{2,1,0:T(8,128)S(1)} %all-to-all-done.5.in_ref, f32[32,512]{1,0:T(8,128)S(1)} %get-tuple-element.242.right_ref), custom_call_target="tpu_custom_call" | custom-call | tf_op jit(solution)/shard_map/pallas_call | solution.py:364
  94.9 0.0 copy-start.1
  95.0 0.8 copy-done.1
  (7 shorter events, 0.1 us)
Async XLA Ops:
  0.8 22.1 %copy-start = (f32[256,512]{1,0:T(8,128)S(1)}, f32[256,512]{1,0:T(8,128)}, u32[]{:S(2)}) copy-start(f32[256,512]{1,0:T(8,128)} %a_ref.3) | copy-start | bytes 1572868
  0.8 0.8 collective-permute-start
  1.7 0.7 collective-permute-start.1
  2.4 0.7 collective-permute-start.2
  3.1 0.7 collective-permute-start.3
  3.8 19.1 %collective-permute-start.4 = (f32[32,512]{1,0:T(8,128)S(1)}, f32[32,512]{1,0:T(8,128)S(1)}, u32[]{:S(2)}, u32[]{:S(2)}) collective-permute-start(f32[32,512]{1,0:T(8,128)S(1)} %add.152), channel_id=1, source_target_pairs={{0,16},{32,48},{64,80},{96,112},{128,144},{160,176},{192,208},{224... | collective-permute-start | bytes 196616 | tf_op jit(solution)/shard_map/ppermute | solution.py:341
  41.6 35.7 %all-to-all-start.4 = ((f32[32,8,128]{2,1,0:T(8,128)}), f32[32,8,128]{2,1,0:T(8,128)S(1)}, u32[]{:S(2)}, u32[]{:S(2)}) async-start(f32[32,8,128]{2,1,0:T(8,128)} %get-tuple-element.236), calls=%async_computation.4 | async-start | bytes 262144 | tf_op jit(solution)/shard_map/all_to_all | solution.py:359
  79.0 13.8 %all-to-all-start.5 = ((f32[16,24,128]{2,1,0:T(8,128)}), f32[16,24,128]{2,1,0:T(8,128)S(1)}, u32[]{:S(2)}, u32[]{:S(2)}) async-start(f32[16,24,128]{2,1,0:T(8,128)} %shard_map.22), calls=%async_computation.5 | async-start | bytes 393216 | tf_op jit(solution)/shard_map/all_to_all | solution.py:363
  94.9 0.8 copy-start.1

commit v7 on v6

--- a/solution.py
+++ b/solution.py
@@ -14,7 +14,9 @@
 AMPLIFY_MAX = 16.0
 GRAM_MIN = 1e-06
 GRAM_MAX = 1e08
-VALUE_MAX = 1e25
+VALUE_MAX = 1e12
+MIXED_MAX = 1e08
+FINITE_MAX = 3e38
 
 HIGHEST = lax.Precision.HIGHEST
 
@@ -102,8 +104,8 @@
     return lax.broadcasted_iota(jnp.int32, shape, axis)
 
 
-def beyond(x):
-    return jnp.max(jnp.where(jnp.abs(x) <= VALUE_MAX, 0.0, 1.0), keepdims=True)
+def beyond(x, limit):
+    return jnp.max(jnp.where(jnp.abs(x) <= limit, 0.0, 1.0), keepdims=True)
 
 
 def fold(square):
@@ -137,30 +139,10 @@
     piece = jnp.where(lane >= 3 * B, pltpu.roll(a[:, :LANES], 2 * B, 1), piece)
     out_ref[:, 0:PIECE, :] = piece.reshape(COLS, PIECE, LANES)
     gram = fold(dot_nt(below_t, padded))
+    gram = gram + jnp.where(beyond(piece, VALUE_MAX) > 0.0, jnp.inf, 0.0)
     corner = fold(pltpu.roll(panel[B : 2 * B], LANES - B, 1))
     out_ref[:, PIECE : PIECE + 8, :] = jnp.broadcast_to(gram[None], (COLS, 8, LANES))
     out_ref[:, PIECE + 8 : PIECE + 16, :] = jnp.broadcast_to(corner[None], (COLS, 8, LANES))
-
-
-def sum_kernel(in_ref, out_ref, piece_ref, gram_ref):
-    row_at = lax.axis_index("row")
-    lane = iota((PIECE, LANES), 1)
-    total = jnp.sum(in_ref[:, 0:PIECE, :], axis=0)
-    panel = in_ref[row_at // 2, 0:PIECE, :]
-    panel = jnp.where(row_at % 2 == 0, panel, pltpu.roll(panel, LANES - B, 1))
-    other = pltpu.roll(in_ref[0, 0:PIECE, :], LANES - B, 1)
-    piece = jnp.where(lane < B, total, jnp.where(lane < 2 * B, panel, other))
-    bad = jnp.where(beyond(jnp.where(lane < 3 * B, piece, 0.0)) > 0.0, jnp.inf, 0.0)
-    piece = jnp.where(lane < B, piece + bad, piece)
-    piece_ref[...] = piece
-    half = PIECE // 2
-    near = jnp.where(lane < B, piece, pltpu.roll(piece, LANES - B, 1))
-    folded = jnp.where(
-        iota((half, LANES), 1) < 2 * B, near[:half], pltpu.roll(near[half:], LANES // 2, 1)
-    )
-    out_ref[...] = jnp.broadcast_to(folded[None], (ROWS, half, LANES))
-    gram_ref[0:8, :] = jnp.sum(in_ref[:, PIECE : PIECE + 8, :], axis=0)
-    gram_ref[8:16, :] = in_ref[0, PIECE + 8 : PIECE + 16, :]
 
 
 def placed(blocks):
@@ -171,8 +153,10 @@
     return jnp.concatenate(wide, axis=0)
 
 
-def factor_kernel(gram_ref, strip_ref, mix_ref, vectors_ref, out_ref, flag_ref):
-    gram = unfold(gram_ref[0:8, :])
+def factor_kernel(in_ref, out_ref, own_ref, vectors_ref):
+    row_at = lax.axis_index("row")
+    col_at = lax.axis_index("col")
+    gram = unfold(jnp.sum(in_ref[:, PIECE : PIECE + 8, :], axis=0))
     sub = iota((B, B), 0)
     lane = iota((B, B), 1)
     eye = jnp.where(sub == lane, 1.0, 0.0)
@@ -183,7 +167,7 @@
     def total(x):
         return jnp.sum(x, axis=0, keepdims=True)
 
-    work = unfold(gram_ref[8:16, :])
+    work = unfold(in_ref[0, PIECE + 8 : PIECE + 16, :])
     coef = eye
     image = gram
     top = jnp.zeros((B, B), jnp.float32)
@@ -223,23 +207,68 @@
     for k in range(B - 1, 0, -1):
         triangle = triangle - (2.0 * column(upper, k)) * triangle[k : k + 1, :]
     vectors_t = dot(vectors, triangle)
-    vectors_ref[...] = vectors_t
-    coefs_t, top_t = vectors_t[:B], vectors_t[B:]
-    mix_ref[0] = placed([(coefs_t, 0), (coefs, 1), (top_t, 0), (top, 1)])
-    mix_ref[1] = placed([(coefs_t, 0), (top_t, 0), (coefs_t, 1), (top_t, 1)])
-    mix_ref[2] = placed([(coefs_t, 2), (top_t, 2), (coefs_t, 3), (top_t, 3)])
-    first_col = lax.axis_index("col") == 0
-    strip = strip_ref[...]
-    lane_c = iota(strip.shape, 1)
-    below_t = jnp.where(lane_c >= jnp.where(first_col, 2 * B, 0), strip, 0.0)
-    unit_t = jnp.where(first_col & (iota(strip.shape, 0) == lane_c - B), 1.0, 0.0)
-    out_ref[...] = dot_tn(vectors, jnp.concatenate([below_t, unit_t], axis=0))
+    vectors_ref[0] = vectors
+    vectors_ref[1] = vectors_t
     diag = jnp.sum(jnp.where(sub == lane, gram, 0.0), axis=1, keepdims=True)
     growth = total(jnp.abs(coefs) * jnp.sqrt(diag))
     wrong = jnp.where(growth <= AMPLIFY_MAX, wrong, 1.0)
     outside = jnp.where((diag >= GRAM_MIN) & (diag <= GRAM_MAX), 0.0, 1.0)
     wrong = jnp.maximum(jnp.max(wrong, keepdims=True), jnp.max(outside, keepdims=True))
-    flag_ref[...] = jnp.broadcast_to(jnp.where(wrong > 0.0, jnp.inf, 0.0), flag_ref.shape)
+    wrong = jnp.maximum(wrong, beyond(vectors_t, MIXED_MAX))
+    mix = placed([(vectors_t[:B], 0), (coefs, 1), (vectors_t[B:], 0), (top, 1)])
+    lane = iota((PIECE, LANES), 1)
+    panel = in_ref[row_at // 2, 0:PIECE, :]
+    panel = jnp.where(row_at % 2 == 0, panel, pltpu.roll(panel, LANES - B, 1))
+    other = pltpu.roll(in_ref[0, 0:PIECE, :], LANES - B, 1)
+    at = iota((PIECE, LANES), 0) + (row_at * COLS + col_at) * PIECE
+    piece = jnp.where(at < 2 * B, 0.0, panel)
+    piece = jnp.where(lane < B, jnp.sum(in_ref[:, 0:PIECE, :], axis=0), piece)
+    piece = jnp.where(lane >= 2 * B, other, piece)
+    piece = jnp.where(lane >= 3 * B, jnp.where(at - B == lane - 3 * B, 1.0, 0.0), piece)
+    piece = dot(piece, mix)
+    half = PIECE // 2
+    own_ref[...] = jnp.where(
+        lane[:half] < 2 * B, piece[:half], pltpu.roll(piece[half:], LANES // 2, 1)
+    )
+    rows = PIECE // 4
+    packed = piece[:rows]
+    for k in (1, 2, 3):
+        moved = pltpu.roll(piece, B * k, 1)[rows * k : rows * (k + 1)]
+        packed = jnp.where(lane[:rows] // B == k, moved, packed)
+    packed = packed + jnp.where(wrong > 0.0, jnp.inf, 0.0)
+    out_ref[...] = jnp.broadcast_to(packed[None], (ROWS, rows, LANES))
+
+
+def side_kernel(panel_ref, strip_ref, vectors_ref, mixed_ref, right_ref):
+    first_col = lax.axis_index("col") == 0
+    vectors = vectors_ref[0]
+    strip = strip_ref[...]
+    lane_c = iota(strip.shape, 1)
+    below_t = jnp.where(lane_c >= jnp.where(first_col, 2 * B, 0), strip, 0.0)
+    unit_t = jnp.where(first_col & (iota(strip.shape, 0) == lane_c - B), 1.0, 0.0)
+    right_ref[...] = dot_tn(vectors, jnp.concatenate([below_t, unit_t], axis=0))
+    panel = panel_ref[:, 0:PIECE, :]
+    source = iota(panel.shape, 0)
+    order = iota(panel.shape, 1) + lax.axis_index("col") * PIECE
+    lane = iota(panel.shape, 2)
+    panel = jnp.where((source == 0) & (order < 2 * B) & (lane < 2 * B), 0.0, panel)
+    unit = jnp.where((source == 0) & (order - B == lane - 3 * B), 1.0, 0.0)
+    panel = jnp.where(lane >= 3 * B, unit, panel).reshape(COLS * PIECE, LANES)
+    vectors_t = vectors_ref[1]
+    zero = jnp.zeros((B, B), jnp.float32)
+    mix = placed([(zero, 0), (vectors_t[:B], 0), (vectors_t[:B], 1), (vectors_t[B:], 0)])
+    mixed = dot(panel, mix)
+    moved = pltpu.roll(mixed, LANES - B, 1).reshape(COLS, PIECE, LANES)
+    mixed = mixed.reshape(COLS, PIECE, LANES)
+    rows = PIECE // 4
+    group = iota((COLS * 2 * rows, LANES), 1) // B
+    packed = jnp.zeros((COLS * 2 * rows, LANES), jnp.float32)
+    for k in range(4):
+        at = slice(rows * k, rows * (k + 1))
+        part = jnp.concatenate([mixed[:, at], moved[:, at]], axis=1).reshape(COLS * 2 * rows, LANES)
+        part = pltpu.roll(part, B * k, 1) if k else part
+        packed = jnp.where(group == k, part, packed)
+    mixed_ref[...] = packed
 
 
 def unfold_rows(block):
@@ -248,53 +277,24 @@
     return jnp.concatenate([block, upper], axis=1).reshape(COLS * PIECE, LANES)
 
 
-def inner_kernel(in_ref, panel_ref, piece_ref, mix_ref, vectors_ref, flag_ref, out_ref):
-    row_at = lax.axis_index("row")
-    col_at = lax.axis_index("col")
+def inner_kernel(in_ref, own_ref, mixed_ref, out_ref, ok_ref):
     half = PIECE // 2
-    pairs = in_ref[...].reshape(COLS, 2, half, LANES)
-    even, odd = pairs[:, 0], pairs[:, 1]
-    first, second = unfold_rows(even), unfold_rows(odd)
-    panel = panel_ref[:, 0:PIECE, :]
-    source = iota(panel.shape, 0)
-    order = iota(panel.shape, 1) + col_at * PIECE
-    above = (source == 0) & (order < 2 * B) & (iota(panel.shape, 2) < 2 * B)
-    below = jnp.where(above, 0.0, panel).reshape(COLS * PIECE, LANES)
-    square = dot_tn(below, first)[B : 2 * B, :B] + dot_tn(below, second)[2 * B : 3 * B, :B]
-    bad = beyond(in_ref[...].reshape(ROWS * half, LANES)) > 0.0
-    near = jnp.concatenate(
-        [jnp.where(col_at == k, first[:PIECE], 0.0) for k in (2, 3)], axis=0
-    )
-    corner = pltpu.roll(near, LANES - B, 1)[:, :B]
-    near = near[:, :B]
-    vectors_t = vectors_ref[...]
-    coefs_t = vectors_t[:B]
-    top_t = vectors_t[B:]
-    images = jnp.concatenate(
-        [dot(square, coefs_t) + dot_tn(near, top_t), dot(near, coefs_t) + dot(corner, top_t)], axis=0
-    )
-    padded = jnp.concatenate([images, jnp.zeros((2 * B, LANES - B), jnp.float32)], axis=1)
-    inner = fold(dot_tn(vectors_t, padded))
-    inner = inner + jnp.where(bad, jnp.inf, flag_ref[0:1, 0:1])
-    piece = piece_ref[...]
-    lane = iota(piece.shape, 1)
-    at = iota(piece.shape, 0) + (row_at * COLS + col_at) * PIECE
-    piece = jnp.where((lane >= B) & (lane < 2 * B) & (at < 2 * B), 0.0, piece)
-    piece = jnp.where(lane >= 3 * B, jnp.where(at - B == lane - 3 * B, 1.0, 0.0), piece)
-    piece = dot(piece, mix_ref[0])
-    piece = jnp.where(lane[:half] < 2 * B, piece[:half], pltpu.roll(piece[half:], LANES // 2, 1))
-    flat = (COLS * half, LANES)
-    columns = dot(even.reshape(flat), mix_ref[1]) + dot(odd.reshape(flat), mix_ref[2])
-    out_ref[:, 0:half, :] = jnp.broadcast_to(piece[None], (COLS, half, LANES))
-    out_ref[:, half : 2 * half, :] = columns.reshape(COLS, half, LANES)
-    out_ref[:, 2 * half : 3 * half, :] = jnp.broadcast_to(inner[None], (COLS, half, LANES))
-
-
-def update_kernel(a_ref, in_ref, right_ref, out_ref, ok_ref):
+    got = in_ref[...]
+    ok_ref[0, 0] = 1 - jnp.max(beyond(got.reshape(-1, LANES), FINITE_MAX)).astype(jnp.int32)
+    pairs = got.reshape(COLS, 2, PIECE // 4, LANES)
+    columns = jnp.concatenate([pairs[:, 0], pairs[:, 1]], axis=1)
+    square = dot_tn(mixed_ref[...], columns.reshape(COLS * half, LANES))
+    inner = square[:B]
+    for k in (1, 2, 3):
+        inner = inner + pltpu.roll(square[B * k : B * (k + 1)], LANES - B * k, 1)
+    out_ref[:, 0:half, :] = jnp.broadcast_to(own_ref[...][None], (COLS, half, LANES))
+    out_ref[:, half : 2 * half, :] = columns
+    out_ref[:, 2 * half : 3 * half, :] = jnp.broadcast_to(fold(inner)[None], (COLS, half, LANES))
+
+
+def update_kernel(a_ref, in_ref, right_ref, out_ref):
     half = PIECE // 2
-    packed = jnp.sum(in_ref[:, 2 * half : 3 * half, :], axis=0)
-    ok_ref[0, 0] = 1 - jnp.max(beyond(packed)).astype(jnp.int32)
-    inner = unfold(packed)
+    inner = unfold(jnp.sum(in_ref[:, 2 * half : 3 * half, :], axis=0))
     shift = 0.5 * (inner + jnp.transpose(inner))
     left = unfold_rows(in_ref[:, 0:half, :])[:, : 2 * B]
     zero = jnp.zeros((B, B), jnp.float32)
@@ -305,8 +305,9 @@
     quarter = [flat] + [pltpu.roll(flat, LANES - B * k, 1) for k in (1, 2, 3)]
     quarter = [part.reshape(COLS, half, LANES) for part in quarter]
     halves = []
-    for k in (0, 2):
-        unfolded = jnp.concatenate([quarter[k], quarter[k + 1]], axis=1)
+    for k in range(2):
+        at = slice(k * half // 2, (k + 1) * half // 2)
+        unfolded = jnp.concatenate([part[:, at] for part in quarter], axis=1)
         halves.append(jnp.transpose(unfolded.reshape(COLS * PIECE, LANES))[:B])
     right = jnp.concatenate([right_ref[...], jnp.concatenate(halves, axis=1)], axis=0)
     out_ref[...] = a_ref[...] - dot(left, right)
@@ -346,24 +347,24 @@
     strip = spread(matrix[:B, :])
     (sent,) = call(partial_kernel, array(COLS, 2 * PIECE, LANES))(matrix, strip)
     panel = lax.all_to_all(sent, "col", 0, 0)
-    sent, piece, gram = call(
-        sum_kernel, array(ROWS, PIECE // 2, LANES), array(PIECE, LANES), array(16, LANES)
+    sent, own, vectors = call(
+        factor_kernel,
+        array(ROWS, PIECE // 4, LANES),
+        array(PIECE // 2, LANES),
+        array(2, 2 * B, B),
     )(panel)
-    mix, vectors, right, flag = call(
-        factor_kernel,
-        array(3, LANES, LANES),
-        array(2 * B, B),
-        array(B, matrix.shape[1]),
-        array(8, LANES),
-    )(gram, strip)
+    mixed, right = call(side_kernel, array(LANES, LANES), array(B, matrix.shape[1]))(
+        panel, strip, vectors
+    )
     got = lax.all_to_all(sent, "row", 0, 0)
-    (sent,) = call(inner_kernel, array(COLS, 3 * PIECE // 2, LANES))(
-        got, panel, piece, mix, vectors, flag
-    )
+    sent, fine = call(
+        inner_kernel,
+        array(COLS, 3 * PIECE // 2, LANES),
+        array(1, 1, dtype=jnp.int32),
+        smem=(1,),
+    )(got, own, mixed)
     got = lax.all_to_all(sent, "col", 0, 0)
-    fast, fine = call(
-        update_kernel, array(*matrix.shape), array(1, 1, dtype=jnp.int32), smem=(1,)
-    )(matrix, got, right)
+    (fast,) = call(update_kernel, array(*matrix.shape))(matrix, got, right)
     return lax.cond(fine[0, 0] > 0, lambda: fast, lambda: general_path(matrix, strip))
 
 

time: 96.2 us -> 94.8 us (0.985)
  transfers between devices with their start and end apart: 7 -> 7, of which waited for: 3 -> 3; matrix products, arithmetic and copies ran while one was open for 0% -> 0% of each run, Pallas kernels for 3% -> 1%
where the time goes in v7:
time: 94.8 us; the launch traced here: 94.4 us
  waiting for transfers between devices  40.4 us (43%)
  starting transfers between devices  27.4 us (29%)
  blocking collectives  16.9 us (18%)
  Pallas kernels  7.15 us (8%)
    all_to_all x1, starting transfers between devices, on_device(): got = lax.all_to_all(sent, 'row', 0, 0)  19.3 us
    ppermute x5, waiting for transfers between devices, spread(): strip = strip + lax.ppermute(strip, 'row', pairs)  17.8 us
    all_to_all x1, blocking collectives, on_device(): panel = lax.all_to_all(sent, 'col', 0, 0)  16.9 us
    all_to_all x1, waiting for transfers between devices, on_device(): got = lax.all_to_all(sent, 'row', 0, 0)  14 us
    all_to_all x1, waiting for transfers between devices, on_device(): got = lax.all_to_all(sent, 'col', 0, 0)  8.6 us
    ppermute x5, starting transfers between devices, spread(): strip = strip + lax.ppermute(strip, 'row', pairs)  4.07 us
    all_to_all x1, starting transfers between devices, on_device(): got = lax.all_to_all(sent, 'col', 0, 0)  4.06 us
    pallas_call x1, Pallas kernels, on_device(): call(factor_kernel, array(ROWS, PIECE // 4, LANES), array(PIECE // 2, LAN...  3.69 us
  transfers between devices with their start and end apart: 7, of which 3 were waited for; matrix products, arithmetic and copies ran while one was open for 0% of the time, Pallas kernels for 1%

profile of v7, /device:TPU:1, one launch (start us, length us, event | category | flops | bytes accessed | tf_op | source)
XLA Modules:
  0.0 94.4 jit_solution(2456977866952064227)
XLA Ops:
  0.0 0.8 slice_select_fusion
  0.8 0.8 collective-permute-start
  1.6 0.0 collective-permute-done
  1.7 0.7 collective-permute-start.1
  2.3 0.0 collective-permute-done.1
  2.4 0.7 collective-permute-start.2
  3.0 0.0 collective-permute-done.2
  3.1 0.7 collective-permute-start.3
  3.7 0.0 collective-permute-done.3
  3.8 1.3 %collective-permute-start.4 = (f32[32,512]{1,0:T(8,128)S(1)}, f32[32,512]{1,0:T(8,128)S(1)}, u32[]{:S(2)}, u32[]{:S(2)}) collective-permute-start(f32[32,512]{1,0:T(8,128)S(1)} %add.152), channel_id=1, source_target_pairs={{0,16},{32,48},{64,80},{96,112},{128,144},{160,176},{192,208},{224... | collective-permute-start | bytes 196616 | tf_op jit(solution)/shard_map/ppermute | solution.py:342
  5.1 17.8 %collective-permute-done.4 = f32[32,512]{1,0:T(8,128)S(1)} collective-permute-done((f32[32,512]{1,0:T(8,128)S(1)}, f32[32,512]{1,0:T(8,128)S(1)}, u32[]{:S(2)}, u32[]{:S(2)}) %collective-permute-start.4) | collective-permute-done | bytes 65568 | tf_op jit(solution)/shard_map/ppermute | solution.py:342
  22.9 0.0 copy-done
  22.9 0.8 shard_map.19
  23.7 16.9 %all_to_all.27.in_ref.panel_ref = f32[16,32,128]{2,1,0:T(8,128)S(1)} all-to-all(f32[16,32,128]{2,1,0:T(8,128)S(1)} %shard_map.19), channel_id=1, replica_groups=mesh['row'=32,'col'=16] {'col'}, dimensions={0} | all-to-all | bytes 524288 | tf_op jit(solution)/shard_map/all_to_all | solution.py:349
  40.6 3.7 %shard_map.20 = (f32[32,4,128]{2,1,0:T(4,128)}, f32[8,128]{1,0:T(8,128)S(1)}, f32[2,64,32]{2,1,0:T(8,128)S(1)}) custom-call(f32[16,32,128]{2,1,0:T(8,128)S(1)} %all_to_all.27.in_ref.panel_ref), custom_call_target="tpu_custom_call" | custom-call | tf_op jit(solution)/shard_map/pallas_call | solution.py:350
  44.3 19.3 %all-to-all-start.4 = ((f32[32,4,128]{2,1,0:T(4,128)}), f32[32,4,128]{2,1,0:T(4,128)S(1)}, u32[]{:S(2)}, u32[]{:S(2)}) async-start(f32[32,4,128]{2,1,0:T(4,128)} %get-tuple-element.234), calls=%async_computation.4 | async-start | bytes 131072 | tf_op jit(solution)/shard_map/all_to_all | solution.py:359
  63.6 0.5 shard_map.21
  64.2 14.0 %all-to-all-done.4.in_ref = f32[32,4,128]{2,1,0:T(4,128)S(1)} async-done(((f32[32,4,128]{2,1,0:T(4,128)}), f32[32,4,128]{2,1,0:T(4,128)S(1)}, u32[]{:S(2)}, u32[]{:S(2)}) %all-to-all-start.4) | async-done | bytes 65568 | tf_op jit(solution)/shard_map/all_to_all | solution.py:359
  78.2 1.1 %shard_map.22 = (f32[16,24,128]{2,1,0:T(8,128)}, s32[1,1]{1,0:T(1,128)}) custom-call(f32[32,4,128]{2,1,0:T(4,128)S(1)} %all-to-all-done.4.in_ref, f32[8,128]{1,0:T(8,128)S(1)} %get-tuple-element.235.own_ref, f32[128,128]{1,0:T(8,128)S(1)} %get-tuple-element.237.mixed_ref), custom_call_target="tpu_custom_call" | custom-call | tf_op jit(solution)/shard_map/pallas_call | solution.py:360
  79.3 4.1 %all-to-all-start.5 = ((f32[16,24,128]{2,1,0:T(8,128)}), f32[16,24,128]{2,1,0:T(8,128)S(1)}, u32[]{:S(2)}, u32[]{:S(2)}) async-start(f32[16,24,128]{2,1,0:T(8,128)} %get-tuple-element.239), calls=%async_computation.5 | async-start | bytes 393216 | tf_op jit(solution)/shard_map/all_to_all | solution.py:366
  83.9 8.6 %all-to-all-done.5.in_ref = f32[16,24,128]{2,1,0:T(8,128)S(1)} async-done(((f32[16,24,128]{2,1,0:T(8,128)}), f32[16,24,128]{2,1,0:T(8,128)S(1)}, u32[]{:S(2)}, u32[]{:S(2)}) %all-to-all-start.5) | async-done | bytes 196640 | tf_op jit(solution)/shard_map/all_to_all | solution.py:366
  92.5 1.0 %shard_map.23 = f32[256,512]{1,0:T(8,128)S(1)} custom-call(f32[256,512]{1,0:T(8,128)S(1)} %copy-done, f32[16,24,128]{2,1,0:T(8,128)S(1)} %all-to-all-done.5.in_ref, f32[32,512]{1,0:T(8,128)S(1)} %get-tuple-element.240.right_ref), custom_call_target="tpu_custom_call" | custom-call | tf_op jit(solution)/shard_map/pallas_call | solution.py:367
  93.6 0.0 copy-start.1
  93.6 0.8 copy-done.1
  (7 shorter events, 0.1 us)
Async XLA Ops:
  0.8 22.1 %copy-start = (f32[256,512]{1,0:T(8,128)S(1)}, f32[256,512]{1,0:T(8,128)}, u32[]{:S(2)}) copy-start(f32[256,512]{1,0:T(8,128)} %a_ref.3) | copy-start | bytes 1572868
  0.8 0.8 collective-permute-start
  1.7 0.7 collective-permute-start.1
  2.4 0.7 collective-permute-start.2
  3.1 0.7 collective-permute-start.3
  3.8 19.1 %collective-permute-start.4 = (f32[32,512]{1,0:T(8,128)S(1)}, f32[32,512]{1,0:T(8,128)S(1)}, u32[]{:S(2)}, u32[]{:S(2)}) collective-permute-start(f32[32,512]{1,0:T(8,128)S(1)} %add.152), channel_id=1, source_target_pairs={{0,16},{32,48},{64,80},{96,112},{128,144},{160,176},{192,208},{224... | collective-permute-start | bytes 196616 | tf_op jit(solution)/shard_map/ppermute | solution.py:342
  44.3 33.9 %all-to-all-start.4 = ((f32[32,4,128]{2,1,0:T(4,128)}), f32[32,4,128]{2,1,0:T(4,128)S(1)}, u32[]{:S(2)}, u32[]{:S(2)}) async-start(f32[32,4,128]{2,1,0:T(4,128)} %get-tuple-element.234), calls=%async_computation.4 | async-start | bytes 131072 | tf_op jit(solution)/shard_map/all_to_all | solution.py:359
  79.3 13.2 %all-to-all-start.5 = ((f32[16,24,128]{2,1,0:T(8,128)}), f32[16,24,128]{2,1,0:T(8,128)S(1)}, u32[]{:S(2)}, u32[]{:S(2)}) async-start(f32[16,24,128]{2,1,0:T(8,128)} %get-tuple-element.239), calls=%async_computation.5 | async-start | bytes 393216 | tf_op jit(solution)/shard_map/all_to_all | solution.py:366
  93.6 0.8 copy-start.1

commit v8 on v7

--- a/solution.py
+++ b/solution.py
@@ -332,12 +332,13 @@
 
 def spread(strip):
     strip = lax.optimization_barrier(jnp.where(lax.axis_index("row") == 0, strip, 0.0))
+    chips = [(8 * x + core) for x in range(4) for core in range(2)]
     for pairs in (
         [(0, 16)],
         [(0, 8), (16, 24)],
-        [(8 * x, 8 * x + 2) for x in range(4)],
-        [(8 * x + z, 8 * x + (z + 2 if z else 6)) for x in range(4) for z in (0, 2)],
-        [(k, k + 1) for k in range(0, ROWS, 2)],
+        [(8 * x, 8 * x + 1) for x in range(4)],
+        [(k, k + 2) for k in chips],
+        [(k + z, k + (z + 2 if z else 6)) for k in chips for z in (0, 2)],
     ):
         strip = strip + lax.ppermute(strip, "row", pairs)
     return strip

time: 94.8 us -> 98.7 us (1.041)
  starting transfers between devices: 27.4 us -> 32.1 us
  waiting for transfers between devices: 40.4 us -> 39.4 us
    all_to_all x1, starting transfers between devices: 19.3 us -> 22.6 us  [on_device(): got = lax.all_to_all(sent, 'row', 0, 0)]
    ppermute x5, starting transfers between devices: 4.07 us -> 5.33 us  [spread(): strip = strip + lax.ppermute(strip, 'row', pairs)]
    ppermute x5, waiting for transfers between devices: 17.8 us -> 16.6 us  [spread(): strip = strip + lax.ppermute(strip, 'row', pairs)]
  transfers between devices with their start and end apart: 7 -> 7, of which waited for: 3 -> 5; matrix products, arithmetic and copies ran while one was open for 0% -> 0% of each run, Pallas kernels for 1% -> 1%
where the time goes in v8:
time: 98.7 us; the launch traced here: 98.2 us
  waiting for transfers between devices  39.4 us (40%)
  starting transfers between devices  32.1 us (33%)
  blocking collectives  17.2 us (17%)
  Pallas kernels  7.15 us (7%)
    all_to_all x1, starting transfers between devices, on_device(): got = lax.all_to_all(sent, 'row', 0, 0)  22.6 us
    all_to_all x1, blocking collectives, on_device(): panel = lax.all_to_all(sent, 'col', 0, 0)  17.2 us
    ppermute x5, waiting for transfers between devices, spread(): strip = strip + lax.ppermute(strip, 'row', pairs)  16.6 us
    all_to_all x1, waiting for transfers between devices, on_device(): got = lax.all_to_all(sent, 'row', 0, 0)  14 us
    all_to_all x1, waiting for transfers between devices, on_device(): got = lax.all_to_all(sent, 'col', 0, 0)  8.74 us
    ppermute x5, starting transfers between devices, spread(): strip = strip + lax.ppermute(strip, 'row', pairs)  5.33 us
    all_to_all x1, starting transfers between devices, on_device(): got = lax.all_to_all(sent, 'col', 0, 0)  4.17 us
    pallas_call x1, Pallas kernels, on_device(): call(factor_kernel, array(ROWS, PIECE // 4, LANES), array(PIECE // 2, LAN...  3.69 us
  transfers between devices with their start and end apart: 7, of which 5 were waited for; matrix products, arithmetic and copies ran while one was open for 0% of the time, Pallas kernels for 1%

profile of v8, /device:TPU:1, one launch (start us, length us, event | category | flops | bytes accessed | tf_op | source)
XLA Modules:
  0.0 98.2 jit_solution(17429066246525167913)
XLA Ops:
  0.0 0.8 slice_select_fusion
  0.8 0.8 collective-permute-start
  1.6 0.0 collective-permute-done
  1.7 0.7 collective-permute-start.1
  2.3 0.0 collective-permute-done.1
  2.4 1.3 %collective-permute-start.2 = (f32[32,512]{1,0:T(8,128)S(1)}, f32[32,512]{1,0:T(8,128)S(1)}, u32[]{:S(2)}, u32[]{:S(2)}) collective-permute-start(f32[32,512]{1,0:T(8,128)S(1)} %add.150), channel_id=1, source_target_pairs={{0,16},{128,144},{256,272},{384,400},{1,17},{129,145},{257,273},{3... | collective-permute-start | bytes 196616 | tf_op jit(solution)/shard_map/ppermute | solution.py:343
  3.7 12.6 %collective-permute-done.2 = f32[32,512]{1,0:T(8,128)S(1)} collective-permute-done((f32[32,512]{1,0:T(8,128)S(1)}, f32[32,512]{1,0:T(8,128)S(1)}, u32[]{:S(2)}, u32[]{:S(2)}) %collective-permute-start.2) | collective-permute-done | bytes 65568 | tf_op jit(solution)/shard_map/ppermute | solution.py:343
  16.3 1.3 %collective-permute-start.3 = (f32[32,512]{1,0:T(8,128)S(1)}, f32[32,512]{1,0:T(8,128)S(1)}, u32[]{:S(2)}, u32[]{:S(2)}) collective-permute-start(f32[32,512]{1,0:T(8,128)S(1)} %add.151), channel_id=1, source_target_pairs={{0,32},{16,48},{128,160},{144,176},{256,288},{272,304},{384,416},{... | collective-permute-start | bytes 196616 | tf_op jit(solution)/shard_map/ppermute | solution.py:343
  17.6 1.6 %collective-permute-done.3 = f32[32,512]{1,0:T(8,128)S(1)} collective-permute-done((f32[32,512]{1,0:T(8,128)S(1)}, f32[32,512]{1,0:T(8,128)S(1)}, u32[]{:S(2)}, u32[]{:S(2)}) %collective-permute-start.3) | collective-permute-done | bytes 65568 | tf_op jit(solution)/shard_map/ppermute | solution.py:343
  19.1 1.3 %collective-permute-start.4 = (f32[32,512]{1,0:T(8,128)S(1)}, f32[32,512]{1,0:T(8,128)S(1)}, u32[]{:S(2)}, u32[]{:S(2)}) collective-permute-start(f32[32,512]{1,0:T(8,128)S(1)} %add.152), channel_id=1, source_target_pairs={{0,96},{32,64},{16,112},{48,80},{128,224},{160,192},{144,240},{176... | collective-permute-start | bytes 196616 | tf_op jit(solution)/shard_map/ppermute | solution.py:343
  20.5 2.5 %collective-permute-done.4 = f32[32,512]{1,0:T(8,128)S(1)} collective-permute-done((f32[32,512]{1,0:T(8,128)S(1)}, f32[32,512]{1,0:T(8,128)S(1)}, u32[]{:S(2)}, u32[]{:S(2)}) %collective-permute-start.4) | collective-permute-done | bytes 65568 | tf_op jit(solution)/shard_map/ppermute | solution.py:343
  22.9 0.0 copy-done
  22.9 0.8 shard_map.19
  23.7 17.2 %all_to_all.27.in_ref.panel_ref = f32[16,32,128]{2,1,0:T(8,128)S(1)} all-to-all(f32[16,32,128]{2,1,0:T(8,128)S(1)} %shard_map.19), channel_id=1, replica_groups=mesh['row'=32,'col'=16] {'col'}, dimensions={0} | all-to-all | bytes 524288 | tf_op jit(solution)/shard_map/all_to_all | solution.py:350
  40.9 3.7 %shard_map.20 = (f32[32,4,128]{2,1,0:T(4,128)}, f32[8,128]{1,0:T(8,128)S(1)}, f32[2,64,32]{2,1,0:T(8,128)S(1)}) custom-call(f32[16,32,128]{2,1,0:T(8,128)S(1)} %all_to_all.27.in_ref.panel_ref), custom_call_target="tpu_custom_call" | custom-call | tf_op jit(solution)/shard_map/pallas_call | solution.py:351
  44.6 22.6 %all-to-all-start.4 = ((f32[32,4,128]{2,1,0:T(4,128)}), f32[32,4,128]{2,1,0:T(4,128)S(1)}, u32[]{:S(2)}, u32[]{:S(2)}) async-start(f32[32,4,128]{2,1,0:T(4,128)} %get-tuple-element.234), calls=%async_computation.4 | async-start | bytes 131072 | tf_op jit(solution)/shard_map/all_to_all | solution.py:360
  67.2 0.5 shard_map.21
  67.8 14.0 %all-to-all-done.4.in_ref = f32[32,4,128]{2,1,0:T(4,128)S(1)} async-done(((f32[32,4,128]{2,1,0:T(4,128)}), f32[32,4,128]{2,1,0:T(4,128)S(1)}, u32[]{:S(2)}, u32[]{:S(2)}) %all-to-all-start.4) | async-done | bytes 65568 | tf_op jit(solution)/shard_map/all_to_all | solution.py:360
  81.8 1.1 %shard_map.22 = (f32[16,24,128]{2,1,0:T(8,128)}, s32[1,1]{1,0:T(1,128)}) custom-call(f32[32,4,128]{2,1,0:T(4,128)S(1)} %all-to-all-done.4.in_ref, f32[8,128]{1,0:T(8,128)S(1)} %get-tuple-element.235.own_ref, f32[128,128]{1,0:T(8,128)S(1)} %get-tuple-element.237.mixed_ref), custom_call_target="tpu_custom_call" | custom-call | tf_op jit(solution)/shard_map/pallas_call | solution.py:361
  82.9 4.2 %all-to-all-start.5 = ((f32[16,24,128]{2,1,0:T(8,128)}), f32[16,24,128]{2,1,0:T(8,128)S(1)}, u32[]{:S(2)}, u32[]{:S(2)}) async-start(f32[16,24,128]{2,1,0:T(8,128)} %get-tuple-element.239), calls=%async_computation.5 | async-start | bytes 393216 | tf_op jit(solution)/shard_map/all_to_all | solution.py:367
  87.6 8.7 %all-to-all-done.5.in_ref = f32[16,24,128]{2,1,0:T(8,128)S(1)} async-done(((f32[16,24,128]{2,1,0:T(8,128)}), f32[16,24,128]{2,1,0:T(8,128)S(1)}, u32[]{:S(2)}, u32[]{:S(2)}) %all-to-all-start.5) | async-done | bytes 196640 | tf_op jit(solution)/shard_map/all_to_all | solution.py:367
  96.4 1.0 %shard_map.23 = f32[256,512]{1,0:T(8,128)S(1)} custom-call(f32[256,512]{1,0:T(8,128)S(1)} %copy-done, f32[16,24,128]{2,1,0:T(8,128)S(1)} %all-to-all-done.5.in_ref, f32[32,512]{1,0:T(8,128)S(1)} %get-tuple-element.240.right_ref), custom_call_target="tpu_custom_call" | custom-call | tf_op jit(solution)/shard_map/pallas_call | solution.py:368
  97.4 0.0 copy-start.1
  97.5 0.8 copy-done.1
  (7 shorter events, 0.1 us)
Async XLA Ops:
  0.8 22.1 %copy-start = (f32[256,512]{1,0:T(8,128)S(1)}, f32[256,512]{1,0:T(8,128)}, u32[]{:S(2)}) copy-start(f32[256,512]{1,0:T(8,128)} %a_ref.3) | copy-start | bytes 1572868
  0.8 0.8 collective-permute-start
  1.7 0.7 collective-permute-start.1
  2.4 13.9 %collective-permute-start.2 = (f32[32,512]{1,0:T(8,128)S(1)}, f32[32,512]{1,0:T(8,128)S(1)}, u32[]{:S(2)}, u32[]{:S(2)}) collective-permute-start(f32[32,512]{1,0:T(8,128)S(1)} %add.150), channel_id=1, source_target_pairs={{0,16},{128,144},{256,272},{384,400},{1,17},{129,145},{257,273},{3... | collective-permute-start | bytes 196616 | tf_op jit(solution)/shard_map/ppermute | solution.py:343
  16.3 2.9 %collective-permute-start.3 = (f32[32,512]{1,0:T(8,128)S(1)}, f32[32,512]{1,0:T(8,128)S(1)}, u32[]{:S(2)}, u32[]{:S(2)}) collective-permute-start(f32[32,512]{1,0:T(8,128)S(1)} %add.151), channel_id=1, source_target_pairs={{0,32},{16,48},{128,160},{144,176},{256,288},{272,304},{384,416},{... | collective-permute-start | bytes 196616 | tf_op jit(solution)/shard_map/ppermute | solution.py:343
  19.1 3.8 %collective-permute-start.4 = (f32[32,512]{1,0:T(8,128)S(1)}, f32[32,512]{1,0:T(8,128)S(1)}, u32[]{:S(2)}, u32[]{:S(2)}) collective-permute-start(f32[32,512]{1,0:T(8,128)S(1)} %add.152), channel_id=1, source_target_pairs={{0,96},{32,64},{16,112},{48,80},{128,224},{160,192},{144,240},{176... | collective-permute-start | bytes 196616 | tf_op jit(solution)/shard_map/ppermute | solution.py:343
  44.6 37.1 %all-to-all-start.4 = ((f32[32,4,128]{2,1,0:T(4,128)}), f32[32,4,128]{2,1,0:T(4,128)S(1)}, u32[]{:S(2)}, u32[]{:S(2)}) async-start(f32[32,4,128]{2,1,0:T(4,128)} %get-tuple-element.234), calls=%async_computation.4 | async-start | bytes 131072 | tf_op jit(solution)/shard_map/all_to_all | solution.py:360
  82.9 13.5 %all-to-all-start.5 = ((f32[16,24,128]{2,1,0:T(8,128)}), f32[16,24,128]{2,1,0:T(8,128)S(1)}, u32[]{:S(2)}, u32[]{:S(2)}) async-start(f32[16,24,128]{2,1,0:T(8,128)} %get-tuple-element.239), calls=%async_computation.5 | async-start | bytes 393216 | tf_op jit(solution)/shard_map/all_to_all | solution.py:367
  97.4 0.8 copy-start.1

commit v9 on v7

--- a/solution.py
+++ b/solution.py
@@ -335,8 +335,8 @@
     for pairs in (
         [(0, 16)],
         [(0, 8), (16, 24)],
-        [(8 * x, 8 * x + 2) for x in range(4)],
-        [(8 * x + z, 8 * x + (z + 2 if z else 6)) for x in range(4) for z in (0, 2)],
+        [(8 * x, 8 * x + 6) for x in range(4)],
+        [(8 * x + z, 8 * x + (4 if z else 2)) for x in range(4) for z in (0, 6)],
         [(k, k + 1) for k in range(0, ROWS, 2)],
     ):
         strip = strip + lax.ppermute(strip, "row", pairs)

time: 94.8 us -> 94.2 us (level)
  blocking collectives: 16.9 us -> 15.6 us
    all_to_all x1, blocking collectives: 16.9 us -> 15.6 us  [on_device(): panel = lax.all_to_all(sent, 'col', 0, 0)]
where the time goes in v9:
time: 94.2 us; the launch traced here: 93.8 us
  waiting for transfers between devices  41.3 us (44%)
  starting transfers between devices  27.4 us (29%)
  blocking collectives  15.6 us (17%)
  Pallas kernels  7.15 us (8%)
    all_to_all x1, starting transfers between devices, on_device(): got = lax.all_to_all(sent, 'row', 0, 0)  19.2 us
    ppermute x5, waiting for transfers between devices, spread(): strip = strip + lax.ppermute(strip, 'row', pairs)  18.7 us
    all_to_all x1, blocking collectives, on_device(): panel = lax.all_to_all(sent, 'col', 0, 0)  15.6 us
    all_to_all x1, waiting for transfers between devices, on_device(): got = lax.all_to_all(sent, 'row', 0, 0)  14 us
    all_to_all x1, waiting for transfers between devices, on_device(): got = lax.all_to_all(sent, 'col', 0, 0)  8.6 us
    ppermute x5, starting transfers between devices, spread(): strip = strip + lax.ppermute(strip, 'row', pairs)  4.07 us
    all_to_all x1, starting transfers between devices, on_device(): got = lax.all_to_all(sent, 'col', 0, 0)  4.06 us
    pallas_call x1, Pallas kernels, on_device(): call(factor_kernel, array(ROWS, PIECE // 4, LANES), array(PIECE // 2, LAN...  3.69 us
  transfers between devices with their start and end apart: 7, of which 3 were waited for; matrix products, arithmetic and copies ran while one was open for 0% of the time, Pallas kernels for 1%

profile of v9, /device:TPU:1, one launch (start us, length us, event | category | flops | bytes accessed | tf_op | source)
XLA Modules:
  0.0 93.8 jit_solution(4467502011199678213)
XLA Ops:
  0.0 0.8 slice_select_fusion
  0.8 0.8 collective-permute-start
  1.6 0.0 collective-permute-done
  1.7 0.7 collective-permute-start.1
  2.3 0.0 collective-permute-done.1
  2.4 0.7 collective-permute-start.2
  3.0 0.0 collective-permute-done.2
  3.1 0.7 collective-permute-start.3
  3.7 0.0 collective-permute-done.3
  3.8 1.3 %collective-permute-start.4 = (f32[32,512]{1,0:T(8,128)S(1)}, f32[32,512]{1,0:T(8,128)S(1)}, u32[]{:S(2)}, u32[]{:S(2)}) collective-permute-start(f32[32,512]{1,0:T(8,128)S(1)} %add.152), channel_id=1, source_target_pairs={{0,16},{32,48},{64,80},{96,112},{128,144},{160,176},{192,208},{224... | collective-permute-start | bytes 196616 | tf_op jit(solution)/shard_map/ppermute | solution.py:342
  5.1 18.7 %collective-permute-done.4 = f32[32,512]{1,0:T(8,128)S(1)} collective-permute-done((f32[32,512]{1,0:T(8,128)S(1)}, f32[32,512]{1,0:T(8,128)S(1)}, u32[]{:S(2)}, u32[]{:S(2)}) %collective-permute-start.4) | collective-permute-done | bytes 65568 | tf_op jit(solution)/shard_map/ppermute | solution.py:342
  23.8 0.0 copy-done
  23.8 0.8 shard_map.19
  24.5 15.6 %all_to_all.27.in_ref.panel_ref = f32[16,32,128]{2,1,0:T(8,128)S(1)} all-to-all(f32[16,32,128]{2,1,0:T(8,128)S(1)} %shard_map.19), channel_id=1, replica_groups=mesh['row'=32,'col'=16] {'col'}, dimensions={0} | all-to-all | bytes 524288 | tf_op jit(solution)/shard_map/all_to_all | solution.py:349
  40.1 3.7 %shard_map.20 = (f32[32,4,128]{2,1,0:T(4,128)}, f32[8,128]{1,0:T(8,128)S(1)}, f32[2,64,32]{2,1,0:T(8,128)S(1)}) custom-call(f32[16,32,128]{2,1,0:T(8,128)S(1)} %all_to_all.27.in_ref.panel_ref), custom_call_target="tpu_custom_call" | custom-call | tf_op jit(solution)/shard_map/pallas_call | solution.py:350
  43.8 19.2 %all-to-all-start.4 = ((f32[32,4,128]{2,1,0:T(4,128)}), f32[32,4,128]{2,1,0:T(4,128)S(1)}, u32[]{:S(2)}, u32[]{:S(2)}) async-start(f32[32,4,128]{2,1,0:T(4,128)} %get-tuple-element.234), calls=%async_computation.4 | async-start | bytes 131072 | tf_op jit(solution)/shard_map/all_to_all | solution.py:359
  63.0 0.5 shard_map.21
  63.6 14.0 %all-to-all-done.4.in_ref = f32[32,4,128]{2,1,0:T(4,128)S(1)} async-done(((f32[32,4,128]{2,1,0:T(4,128)}), f32[32,4,128]{2,1,0:T(4,128)S(1)}, u32[]{:S(2)}, u32[]{:S(2)}) %all-to-all-start.4) | async-done | bytes 65568 | tf_op jit(solution)/shard_map/all_to_all | solution.py:359
  77.6 1.1 %shard_map.22 = (f32[16,24,128]{2,1,0:T(8,128)}, s32[1,1]{1,0:T(1,128)}) custom-call(f32[32,4,128]{2,1,0:T(4,128)S(1)} %all-to-all-done.4.in_ref, f32[8,128]{1,0:T(8,128)S(1)} %get-tuple-element.235.own_ref, f32[128,128]{1,0:T(8,128)S(1)} %get-tuple-element.237.mixed_ref), custom_call_target="tpu_custom_call" | custom-call | tf_op jit(solution)/shard_map/pallas_call | solution.py:360
  78.7 4.1 %all-to-all-start.5 = ((f32[16,24,128]{2,1,0:T(8,128)}), f32[16,24,128]{2,1,0:T(8,128)S(1)}, u32[]{:S(2)}, u32[]{:S(2)}) async-start(f32[16,24,128]{2,1,0:T(8,128)} %get-tuple-element.239), calls=%async_computation.5 | async-start | bytes 393216 | tf_op jit(solution)/shard_map/all_to_all | solution.py:366
  83.3 8.6 %all-to-all-done.5.in_ref = f32[16,24,128]{2,1,0:T(8,128)S(1)} async-done(((f32[16,24,128]{2,1,0:T(8,128)}), f32[16,24,128]{2,1,0:T(8,128)S(1)}, u32[]{:S(2)}, u32[]{:S(2)}) %all-to-all-start.5) | async-done | bytes 196640 | tf_op jit(solution)/shard_map/all_to_all | solution.py:366
  91.9 1.0 %shard_map.23 = f32[256,512]{1,0:T(8,128)S(1)} custom-call(f32[256,512]{1,0:T(8,128)S(1)} %copy-done, f32[16,24,128]{2,1,0:T(8,128)S(1)} %all-to-all-done.5.in_ref, f32[32,512]{1,0:T(8,128)S(1)} %get-tuple-element.240.right_ref), custom_call_target="tpu_custom_call" | custom-call | tf_op jit(solution)/shard_map/pallas_call | solution.py:367
  93.0 0.0 copy-start.1
  93.0 0.8 copy-done.1
  (7 shorter events, 0.1 us)
Async XLA Ops:
  0.8 22.9 %copy-start = (f32[256,512]{1,0:T(8,128)S(1)}, f32[256,512]{1,0:T(8,128)}, u32[]{:S(2)}) copy-start(f32[256,512]{1,0:T(8,128)} %a_ref.3) | copy-start | bytes 1572868
  0.8 0.8 collective-permute-start
  1.7 0.7 collective-permute-start.1
  2.4 0.7 collective-permute-start.2
  3.1 0.7 collective-permute-start.3
  3.8 20.0 %collective-permute-start.4 = (f32[32,512]{1,0:T(8,128)S(1)}, f32[32,512]{1,0:T(8,128)S(1)}, u32[]{:S(2)}, u32[]{:S(2)}) collective-permute-start(f32[32,512]{1,0:T(8,128)S(1)} %add.152), channel_id=1, source_target_pairs={{0,16},{32,48},{64,80},{96,112},{128,144},{160,176},{192,208},{224... | collective-permute-start | bytes 196616 | tf_op jit(solution)/shard_map/ppermute | solution.py:342
  43.8 33.8 %all-to-all-start.4 = ((f32[32,4,128]{2,1,0:T(4,128)}), f32[32,4,128]{2,1,0:T(4,128)S(1)}, u32[]{:S(2)}, u32[]{:S(2)}) async-start(f32[32,4,128]{2,1,0:T(4,128)} %get-tuple-element.234), calls=%async_computation.4 | async-start | bytes 131072 | tf_op jit(solution)/shard_map/all_to_all | solution.py:359
  78.7 13.2 %all-to-all-start.5 = ((f32[16,24,128]{2,1,0:T(8,128)}), f32[16,24,128]{2,1,0:T(8,128)S(1)}, u32[]{:S(2)}, u32[]{:S(2)}) async-start(f32[16,24,128]{2,1,0:T(8,128)} %get-tuple-element.239), calls=%async_computation.5 | async-start | bytes 393216 | tf_op jit(solution)/shard_map/all_to_all | solution.py:366
  93.0 0.8 copy-start.1

commit v10 on v9

--- a/solution.py
+++ b/solution.py
@@ -332,14 +332,21 @@
 
 def spread(strip):
     strip = lax.optimization_barrier(jnp.where(lax.axis_index("row") == 0, strip, 0.0))
-    for pairs in (
-        [(0, 16)],
-        [(0, 8), (16, 24)],
-        [(8 * x, 8 * x + 6) for x in range(4)],
-        [(8 * x + z, 8 * x + (4 if z else 2)) for x in range(4) for z in (0, 6)],
-        [(k, k + 1) for k in range(0, ROWS, 2)],
+    first, second = [], []
+    for x in range(4):
+        for col in range(COLS):
+            near, far = (2, 6) if col < COLS // 2 else (6, 2)
+            first.append((8 * x * COLS + col, (8 * x + near) * COLS + col))
+            second.append(((8 * x + near) * COLS + col, (8 * x + 4) * COLS + col))
+            second.append((8 * x * COLS + col, (8 * x + far) * COLS + col))
+    for axes, pairs in (
+        ("row", [(0, 16)]),
+        ("row", [(0, 8), (16, 24)]),
+        (("row", "col"), first),
+        (("row", "col"), second),
+        ("row", [(k, k + 1) for k in range(0, ROWS, 2)]),
     ):
-        strip = strip + lax.ppermute(strip, "row", pairs)
+        strip = strip + lax.ppermute(strip, axes, pairs)
     return strip
 
 

time: 94.2 us -> 94 us (level)
  no operation moved by 1% of the time
where the time goes in v10:
time: 94 us; the launch traced here: 93.6 us
  waiting for transfers between devices  41 us (44%)
  starting transfers between devices  27.2 us (29%)
  blocking collectives  15.8 us (17%)
  Pallas kernels  7.15 us (8%)
    all_to_all x1, starting transfers between devices, on_device(): got = lax.all_to_all(sent, 'row', 0, 0)  19 us
    ppermute x5, waiting for transfers between devices, spread(): strip = strip + lax.ppermute(strip, axes, pairs)  18.4 us
    all_to_all x1, blocking collectives, on_device(): panel = lax.all_to_all(sent, 'col', 0, 0)  15.8 us
    all_to_all x1, waiting for transfers between devices, on_device(): got = lax.all_to_all(sent, 'row', 0, 0)  14 us
    all_to_all x1, waiting for transfers between devices, on_device(): got = lax.all_to_all(sent, 'col', 0, 0)  8.6 us
    ppermute x5, starting transfers between devices, spread(): strip = strip + lax.ppermute(strip, axes, pairs)  4.07 us
    all_to_all x1, starting transfers between devices, on_device(): got = lax.all_to_all(sent, 'col', 0, 0)  4.06 us
    pallas_call x1, Pallas kernels, on_device(): call(factor_kernel, array(ROWS, PIECE // 4, LANES), array(PIECE // 2, LAN...  3.69 us
  transfers between devices with their start and end apart: 7, of which 3 were waited for; matrix products, arithmetic and copies ran while one was open for 0% of the time, Pallas kernels for 1%

profile of v10, /device:TPU:1, one launch (start us, length us, event | category | flops | bytes accessed | tf_op | source)
XLA Modules:
  0.0 93.6 jit_solution(1940142086808198968)
XLA Ops:
  0.0 0.8 slice_select_fusion
  0.8 0.8 collective-permute-start
  1.6 0.0 collective-permute-done
  1.7 0.7 collective-permute-start.1
  2.3 0.0 collective-permute-done.1
  2.4 0.7 collective-permute-start.2
  3.0 0.0 collective-permute-done.2
  3.1 0.7 collective-permute-start.3
  3.7 0.0 collective-permute-done.3
  3.8 1.3 %collective-permute-start.4 = (f32[32,512]{1,0:T(8,128)S(1)}, f32[32,512]{1,0:T(8,128)S(1)}, u32[]{:S(2)}, u32[]{:S(2)}) collective-permute-start(f32[32,512]{1,0:T(8,128)S(1)} %add.152), channel_id=1, source_target_pairs={{0,16},{32,48},{64,80},{96,112},{128,144},{160,176},{192,208},{224... | collective-permute-start | bytes 196616 | tf_op jit(solution)/shard_map/ppermute | solution.py:349
  5.1 18.4 %collective-permute-done.4 = f32[32,512]{1,0:T(8,128)S(1)} collective-permute-done((f32[32,512]{1,0:T(8,128)S(1)}, f32[32,512]{1,0:T(8,128)S(1)}, u32[]{:S(2)}, u32[]{:S(2)}) %collective-permute-start.4) | collective-permute-done | bytes 65568 | tf_op jit(solution)/shard_map/ppermute | solution.py:349
  23.5 0.0 copy-done
  23.5 0.8 shard_map.19
  24.3 15.8 %all_to_all.27.in_ref.panel_ref = f32[16,32,128]{2,1,0:T(8,128)S(1)} all-to-all(f32[16,32,128]{2,1,0:T(8,128)S(1)} %shard_map.19), channel_id=1, replica_groups=mesh['row'=32,'col'=16] {'col'}, dimensions={0} | all-to-all | bytes 524288 | tf_op jit(solution)/shard_map/all_to_all | solution.py:356
  40.1 3.7 %shard_map.20 = (f32[32,4,128]{2,1,0:T(4,128)}, f32[8,128]{1,0:T(8,128)S(1)}, f32[2,64,32]{2,1,0:T(8,128)S(1)}) custom-call(f32[16,32,128]{2,1,0:T(8,128)S(1)} %all_to_all.27.in_ref.panel_ref), custom_call_target="tpu_custom_call" | custom-call | tf_op jit(solution)/shard_map/pallas_call | solution.py:357
  43.8 19.0 %all-to-all-start.4 = ((f32[32,4,128]{2,1,0:T(4,128)}), f32[32,4,128]{2,1,0:T(4,128)S(1)}, u32[]{:S(2)}, u32[]{:S(2)}) async-start(f32[32,4,128]{2,1,0:T(4,128)} %get-tuple-element.234), calls=%async_computation.4 | async-start | bytes 131072 | tf_op jit(solution)/shard_map/all_to_all | solution.py:366
  62.8 0.5 shard_map.21
  63.4 14.0 %all-to-all-done.4.in_ref = f32[32,4,128]{2,1,0:T(4,128)S(1)} async-done(((f32[32,4,128]{2,1,0:T(4,128)}), f32[32,4,128]{2,1,0:T(4,128)S(1)}, u32[]{:S(2)}, u32[]{:S(2)}) %all-to-all-start.4) | async-done | bytes 65568 | tf_op jit(solution)/shard_map/all_to_all | solution.py:366
  77.4 1.1 %shard_map.22 = (f32[16,24,128]{2,1,0:T(8,128)}, s32[1,1]{1,0:T(1,128)}) custom-call(f32[32,4,128]{2,1,0:T(4,128)S(1)} %all-to-all-done.4.in_ref, f32[8,128]{1,0:T(8,128)S(1)} %get-tuple-element.235.own_ref, f32[128,128]{1,0:T(8,128)S(1)} %get-tuple-element.237.mixed_ref), custom_call_target="tpu_custom_call" | custom-call | tf_op jit(solution)/shard_map/pallas_call | solution.py:367
  78.5 4.1 %all-to-all-start.5 = ((f32[16,24,128]{2,1,0:T(8,128)}), f32[16,24,128]{2,1,0:T(8,128)S(1)}, u32[]{:S(2)}, u32[]{:S(2)}) async-start(f32[16,24,128]{2,1,0:T(8,128)} %get-tuple-element.239), calls=%async_computation.5 | async-start | bytes 393216 | tf_op jit(solution)/shard_map/all_to_all | solution.py:373
  83.1 8.6 %all-to-all-done.5.in_ref = f32[16,24,128]{2,1,0:T(8,128)S(1)} async-done(((f32[16,24,128]{2,1,0:T(8,128)}), f32[16,24,128]{2,1,0:T(8,128)S(1)}, u32[]{:S(2)}, u32[]{:S(2)}) %all-to-all-start.5) | async-done | bytes 196640 | tf_op jit(solution)/shard_map/all_to_all | solution.py:373
  91.7 1.0 %shard_map.23 = f32[256,512]{1,0:T(8,128)S(1)} custom-call(f32[256,512]{1,0:T(8,128)S(1)} %copy-done, f32[16,24,128]{2,1,0:T(8,128)S(1)} %all-to-all-done.5.in_ref, f32[32,512]{1,0:T(8,128)S(1)} %get-tuple-element.240.right_ref), custom_call_target="tpu_custom_call" | custom-call | tf_op jit(solution)/shard_map/pallas_call | solution.py:374
  92.8 0.0 copy-start.1
  92.8 0.8 copy-done.1
  (7 shorter events, 0.1 us)
Async XLA Ops:
  0.8 22.6 %copy-start = (f32[256,512]{1,0:T(8,128)S(1)}, f32[256,512]{1,0:T(8,128)}, u32[]{:S(2)}) copy-start(f32[256,512]{1,0:T(8,128)} %a_ref.3) | copy-start | bytes 1572868
  0.8 0.8 collective-permute-start
  1.7 0.7 collective-permute-start.1
  2.4 0.7 collective-permute-start.2
  3.1 0.7 collective-permute-start.3
  3.8 19.7 %collective-permute-start.4 = (f32[32,512]{1,0:T(8,128)S(1)}, f32[32,512]{1,0:T(8,128)S(1)}, u32[]{:S(2)}, u32[]{:S(2)}) collective-permute-start(f32[32,512]{1,0:T(8,128)S(1)} %add.152), channel_id=1, source_target_pairs={{0,16},{32,48},{64,80},{96,112},{128,144},{160,176},{192,208},{224... | collective-permute-start | bytes 196616 | tf_op jit(solution)/shard_map/ppermute | solution.py:349
  43.8 33.6 %all-to-all-start.4 = ((f32[32,4,128]{2,1,0:T(4,128)}), f32[32,4,128]{2,1,0:T(4,128)S(1)}, u32[]{:S(2)}, u32[]{:S(2)}) async-start(f32[32,4,128]{2,1,0:T(4,128)} %get-tuple-element.234), calls=%async_computation.4 | async-start | bytes 131072 | tf_op jit(solution)/shard_map/all_to_all | solution.py:366
  78.5 13.2 %all-to-all-start.5 = ((f32[16,24,128]{2,1,0:T(8,128)}), f32[16,24,128]{2,1,0:T(8,128)S(1)}, u32[]{:S(2)}, u32[]{:S(2)}) async-start(f32[16,24,128]{2,1,0:T(8,128)} %get-tuple-element.239), calls=%async_computation.5 | async-start | bytes 393216 | tf_op jit(solution)/shard_map/all_to_all | solution.py:373
  92.8 0.8 copy-start.1

commit v11 on v10

--- a/solution.py
+++ b/solution.py
@@ -335,13 +335,13 @@
     first, second = [], []
     for x in range(4):
         for col in range(COLS):
-            near, far = (2, 6) if col < COLS // 2 else (6, 2)
+            near, far = (2, 6) if col < 3 * COLS // 4 else (6, 2)
             first.append((8 * x * COLS + col, (8 * x + near) * COLS + col))
             second.append(((8 * x + near) * COLS + col, (8 * x + 4) * COLS + col))
             second.append((8 * x * COLS + col, (8 * x + far) * COLS + col))
     for axes, pairs in (
-        ("row", [(0, 16)]),
-        ("row", [(0, 8), (16, 24)]),
+        ("row", [(0, 8)]),
+        ("row", [(0, 24), (8, 16)]),
         (("row", "col"), first),
         (("row", "col"), second),
         ("row", [(k, k + 1) for k in range(0, ROWS, 2)]),

time: 94 us -> 92.4 us (0.983)
  starting transfers between devices: 27.2 us -> 25.6 us
    all_to_all x1, starting transfers between devices: 19 us -> 17.5 us  [on_device(): got = lax.all_to_all(sent, 'row', 0, 0)]
where the time goes in v11:
time: 92.4 us; the launch traced here: 92 us
  waiting for transfers between devices  41.3 us (45%)
  starting transfers between devices  25.6 us (28%)
  blocking collectives  15.6 us (17%)
  Pallas kernels  7.14 us (8%)
    ppermute x5, waiting for transfers between devices, spread(): strip = strip + lax.ppermute(strip, axes, pairs)  18.6 us
    all_to_all x1, starting transfers between devices, on_device(): got = lax.all_to_all(sent, 'row', 0, 0)  17.5 us
    all_to_all x1, blocking collectives, on_device(): panel = lax.all_to_all(sent, 'col', 0, 0)  15.6 us
    all_to_all x1, waiting for transfers between devices, on_device(): got = lax.all_to_all(sent, 'row', 0, 0)  14 us
    all_to_all x1, waiting for transfers between devices, on_device(): got = lax.all_to_all(sent, 'col', 0, 0)  8.6 us
    ppermute x5, starting transfers between devices, spread(): strip = strip + lax.ppermute(strip, axes, pairs)  4.07 us
    all_to_all x1, starting transfers between devices, on_device(): got = lax.all_to_all(sent, 'col', 0, 0)  4.06 us
    pallas_call x1, Pallas kernels, on_device(): call(factor_kernel, array(ROWS, PIECE // 4, LANES), array(PIECE // 2, LAN...  3.69 us
  transfers between devices with their start and end apart: 7, of which 3 were waited for; matrix products, arithmetic and copies ran while one was open for 0% of the time, Pallas kernels for 1%

profile of v11, /device:TPU:1, one launch (start us, length us, event | category | flops | bytes accessed | tf_op | source)
XLA Modules:
  0.0 92.0 jit_solution(9103182790234675615)
XLA Ops:
  0.0 0.8 slice_select_fusion
  0.8 0.8 collective-permute-start
  1.6 0.0 collective-permute-done
  1.7 0.7 collective-permute-start.1
  2.3 0.0 collective-permute-done.1
  2.4 0.7 collective-permute-start.2
  3.0 0.0 collective-permute-done.2
  3.1 0.7 collective-permute-start.3
  3.7 0.0 collective-permute-done.3
  3.8 1.3 %collective-permute-start.4 = (f32[32,512]{1,0:T(8,128)S(1)}, f32[32,512]{1,0:T(8,128)S(1)}, u32[]{:S(2)}, u32[]{:S(2)}) collective-permute-start(f32[32,512]{1,0:T(8,128)S(1)} %add.152), channel_id=1, source_target_pairs={{0,16},{32,48},{64,80},{96,112},{128,144},{160,176},{192,208},{224... | collective-permute-start | bytes 196616 | tf_op jit(solution)/shard_map/ppermute | solution.py:349
  5.1 18.6 %collective-permute-done.4 = f32[32,512]{1,0:T(8,128)S(1)} collective-permute-done((f32[32,512]{1,0:T(8,128)S(1)}, f32[32,512]{1,0:T(8,128)S(1)}, u32[]{:S(2)}, u32[]{:S(2)}) %collective-permute-start.4) | collective-permute-done | bytes 65568 | tf_op jit(solution)/shard_map/ppermute | solution.py:349
  23.7 0.0 copy-done
  23.7 0.8 shard_map.19
  24.5 15.6 %all_to_all.27.in_ref.panel_ref = f32[16,32,128]{2,1,0:T(8,128)S(1)} all-to-all(f32[16,32,128]{2,1,0:T(8,128)S(1)} %shard_map.19), channel_id=1, replica_groups=mesh['row'=32,'col'=16] {'col'}, dimensions={0} | all-to-all | bytes 524288 | tf_op jit(solution)/shard_map/all_to_all | solution.py:356
  40.1 3.7 %shard_map.20 = (f32[32,4,128]{2,1,0:T(4,128)}, f32[8,128]{1,0:T(8,128)S(1)}, f32[2,64,32]{2,1,0:T(8,128)S(1)}) custom-call(f32[16,32,128]{2,1,0:T(8,128)S(1)} %all_to_all.27.in_ref.panel_ref), custom_call_target="tpu_custom_call" | custom-call | tf_op jit(solution)/shard_map/pallas_call | solution.py:357
  43.8 17.5 %all-to-all-start.4 = ((f32[32,4,128]{2,1,0:T(4,128)}), f32[32,4,128]{2,1,0:T(4,128)S(1)}, u32[]{:S(2)}, u32[]{:S(2)}) async-start(f32[32,4,128]{2,1,0:T(4,128)} %get-tuple-element.234), calls=%async_computation.4 | async-start | bytes 131072 | tf_op jit(solution)/shard_map/all_to_all | solution.py:366
  61.3 0.5 shard_map.21
  61.8 14.0 %all-to-all-done.4.in_ref = f32[32,4,128]{2,1,0:T(4,128)S(1)} async-done(((f32[32,4,128]{2,1,0:T(4,128)}), f32[32,4,128]{2,1,0:T(4,128)S(1)}, u32[]{:S(2)}, u32[]{:S(2)}) %all-to-all-start.4) | async-done | bytes 65568 | tf_op jit(solution)/shard_map/all_to_all | solution.py:366
  75.8 1.1 %shard_map.22 = (f32[16,24,128]{2,1,0:T(8,128)}, s32[1,1]{1,0:T(1,128)}) custom-call(f32[32,4,128]{2,1,0:T(4,128)S(1)} %all-to-all-done.4.in_ref, f32[8,128]{1,0:T(8,128)S(1)} %get-tuple-element.235.own_ref, f32[128,128]{1,0:T(8,128)S(1)} %get-tuple-element.237.mixed_ref), custom_call_target="tpu_custom_call" | custom-call | tf_op jit(solution)/shard_map/pallas_call | solution.py:367
  76.9 4.1 %all-to-all-start.5 = ((f32[16,24,128]{2,1,0:T(8,128)}), f32[16,24,128]{2,1,0:T(8,128)S(1)}, u32[]{:S(2)}, u32[]{:S(2)}) async-start(f32[16,24,128]{2,1,0:T(8,128)} %get-tuple-element.239), calls=%async_computation.5 | async-start | bytes 393216 | tf_op jit(solution)/shard_map/all_to_all | solution.py:373
  81.6 8.6 %all-to-all-done.5.in_ref = f32[16,24,128]{2,1,0:T(8,128)S(1)} async-done(((f32[16,24,128]{2,1,0:T(8,128)}), f32[16,24,128]{2,1,0:T(8,128)S(1)}, u32[]{:S(2)}, u32[]{:S(2)}) %all-to-all-start.5) | async-done | bytes 196640 | tf_op jit(solution)/shard_map/all_to_all | solution.py:373
  90.2 1.0 %shard_map.23 = f32[256,512]{1,0:T(8,128)S(1)} custom-call(f32[256,512]{1,0:T(8,128)S(1)} %copy-done, f32[16,24,128]{2,1,0:T(8,128)S(1)} %all-to-all-done.5.in_ref, f32[32,512]{1,0:T(8,128)S(1)} %get-tuple-element.240.right_ref), custom_call_target="tpu_custom_call" | custom-call | tf_op jit(solution)/shard_map/pallas_call | solution.py:374
  91.2 0.0 copy-start.1
  91.2 0.8 copy-done.1
  (7 shorter events, 0.1 us)
Async XLA Ops:
  0.8 22.9 %copy-start = (f32[256,512]{1,0:T(8,128)S(1)}, f32[256,512]{1,0:T(8,128)}, u32[]{:S(2)}) copy-start(f32[256,512]{1,0:T(8,128)} %a_ref.3) | copy-start | bytes 1572868
  0.8 0.8 collective-permute-start
  1.7 0.7 collective-permute-start.1
  2.4 0.7 collective-permute-start.2
  3.1 0.7 collective-permute-start.3
  3.8 19.9 %collective-permute-start.4 = (f32[32,512]{1,0:T(8,128)S(1)}, f32[32,512]{1,0:T(8,128)S(1)}, u32[]{:S(2)}, u32[]{:S(2)}) collective-permute-start(f32[32,512]{1,0:T(8,128)S(1)} %add.152), channel_id=1, source_target_pairs={{0,16},{32,48},{64,80},{96,112},{128,144},{160,176},{192,208},{224... | collective-permute-start | bytes 196616 | tf_op jit(solution)/shard_map/ppermute | solution.py:349
  43.8 32.1 %all-to-all-start.4 = ((f32[32,4,128]{2,1,0:T(4,128)}), f32[32,4,128]{2,1,0:T(4,128)S(1)}, u32[]{:S(2)}, u32[]{:S(2)}) async-start(f32[32,4,128]{2,1,0:T(4,128)} %get-tuple-element.234), calls=%async_computation.4 | async-start | bytes 131072 | tf_op jit(solution)/shard_map/all_to_all | solution.py:366
  76.9 13.2 %all-to-all-start.5 = ((f32[16,24,128]{2,1,0:T(8,128)}), f32[16,24,128]{2,1,0:T(8,128)S(1)}, u32[]{:S(2)}, u32[]{:S(2)}) async-start(f32[16,24,128]{2,1,0:T(8,128)} %get-tuple-element.239), calls=%async_computation.5 | async-start | bytes 393216 | tf_op jit(solution)/shard_map/all_to_all | solution.py:373
  91.2 0.8 copy-start.1

commit v12 on v11

--- a/solution.py
+++ b/solution.py
@@ -360,10 +360,11 @@
         array(PIECE // 2, LANES),
         array(2, 2 * B, B),
     )(panel)
+    got = lax.all_to_all(sent, "row", 0, 0)
+    got, panel = lax.optimization_barrier((got, panel))
     mixed, right = call(side_kernel, array(LANES, LANES), array(B, matrix.shape[1]))(
         panel, strip, vectors
     )
-    got = lax.all_to_all(sent, "row", 0, 0)
     sent, fine = call(
         inner_kernel,
         array(COLS, 3 * PIECE // 2, LANES),

time: 92.4 us -> 92.1 us (level)
  blocking collectives: 15.6 us -> 47.4 us
  starting transfers between devices: 25.6 us -> 8.13 us
  waiting for transfers between devices: 41.3 us -> 27.2 us
    all_to_all x0 -> x1, blocking collectives: none -> 31.8 us  [on_device(): got = lax.all_to_all(sent, 'row', 0, 0)]
    all_to_all x1 -> x0, starting transfers between devices: 17.5 us -> none  [on_device(): got = lax.all_to_all(sent, 'row', 0, 0)]
    all_to_all x1 -> x0, waiting for transfers between devices: 14 us -> none  [on_device(): got = lax.all_to_all(sent, 'row', 0, 0)]
  transfers between devices with their start and end apart: 7 -> 6, of which waited for: 3 -> 2; matrix products, arithmetic and copies ran while one was open for 0% -> 0% of each run, Pallas kernels for 1% -> 0%
where the time goes in v12:
time: 92.1 us; the launch traced here: 91.7 us
  blocking collectives  47.4 us (51%)
  waiting for transfers between devices  27.2 us (30%)
  starting transfers between devices  8.13 us (9%)
  Pallas kernels  6.51 us (7%)
    all_to_all x1, blocking collectives, on_device(): got = lax.all_to_all(sent, 'row', 0, 0)  31.8 us
    ppermute x5, waiting for transfers between devices, spread(): strip = strip + lax.ppermute(strip, axes, pairs)  18.6 us
    all_to_all x1, blocking collectives, on_device(): panel = lax.all_to_all(sent, 'col', 0, 0)  15.6 us
    all_to_all x1, waiting for transfers between devices, on_device(): got = lax.all_to_all(sent, 'col', 0, 0)  8.53 us
    ppermute x5, starting transfers between devices, spread(): strip = strip + lax.ppermute(strip, axes, pairs)  4.07 us
    all_to_all x1, starting transfers between devices, on_device(): got = lax.all_to_all(sent, 'col', 0, 0)  4.06 us
    pallas_call x1, Pallas kernels, on_device(): call(factor_kernel, array(ROWS, PIECE // 4, LANES), array(PIECE // 2, LAN...  3.06 us
  transfers between devices with their start and end apart: 6, of which 2 were waited for; matrix products, arithmetic and copies ran while one was open for 0% of the time, Pallas kernels for 0%

profile of v12, /device:TPU:1, one launch (start us, length us, event | category | flops | bytes accessed | tf_op | source)
XLA Modules:
  0.0 91.7 jit_solution(9403589079946741015)
XLA Ops:
  0.0 0.8 slice_select_fusion
  0.8 0.0 copy-start
  0.8 0.8 collective-permute-start
  1.6 0.0 collective-permute-done
  1.7 0.7 collective-permute-start.1
  2.3 0.0 collective-permute-done.1
  2.4 0.7 collective-permute-start.2
  3.0 0.0 collective-permute-done.2
  3.1 0.7 collective-permute-start.3
  3.7 0.0 collective-permute-done.3
  3.8 1.3 %collective-permute-start.4 = (f32[32,512]{1,0:T(8,128)S(1)}, f32[32,512]{1,0:T(8,128)S(1)}, u32[]{:S(2)}, u32[]{:S(2)}) collective-permute-start(f32[32,512]{1,0:T(8,128)S(1)} %add.152), channel_id=1, source_target_pairs={{0,16},{32,48},{64,80},{96,112},{128,144},{160,176},{192,208},{224... | collective-permute-start | bytes 196616 | tf_op jit(solution)/shard_map/ppermute | solution.py:349
  5.1 18.6 %collective-permute-done.4 = f32[32,512]{1,0:T(8,128)S(1)} collective-permute-done((f32[32,512]{1,0:T(8,128)S(1)}, f32[32,512]{1,0:T(8,128)S(1)}, u32[]{:S(2)}, u32[]{:S(2)}) %collective-permute-start.4) | collective-permute-done | bytes 65568 | tf_op jit(solution)/shard_map/ppermute | solution.py:349
  23.7 0.0 copy-done
  23.7 0.8 shard_map.19
  24.5 15.6 %all_to_all.27.in_ref.panel_ref = f32[16,32,128]{2,1,0:T(8,128)S(1)} all-to-all(f32[16,32,128]{2,1,0:T(8,128)S(1)} %shard_map.19), channel_id=1, replica_groups=mesh['row'=32,'col'=16] {'col'}, dimensions={0} | all-to-all | bytes 524288 | tf_op jit(solution)/shard_map/all_to_all | solution.py:356
  40.1 3.1 %shard_map.20 = (f32[32,4,128]{2,1,0:T(4,128)S(1)}, f32[8,128]{1,0:T(8,128)S(1)}, f32[2,64,32]{2,1,0:T(8,128)S(1)}) custom-call(f32[16,32,128]{2,1,0:T(8,128)S(1)} %all_to_all.27.in_ref.panel_ref), custom_call_target="tpu_custom_call" | custom-call | tf_op jit(solution)/shard_map/pallas_call | solution.py:357
  43.2 31.8 %all_to_all.28.in_ref = f32[32,4,128]{2,1,0:T(4,128)S(1)} all-to-all(f32[32,4,128]{2,1,0:T(4,128)S(1)} %get-tuple-element.236), channel_id=1, replica_groups=mesh['row'=32,'col'=16] {'row'}, dimensions={0} | all-to-all | bytes 131072 | tf_op jit(solution)/shard_map/all_to_all | solution.py:363
  75.0 0.5 shard_map.21
  75.5 1.1 %shard_map.22 = (f32[16,24,128]{2,1,0:T(8,128)}, s32[1,1]{1,0:T(1,128)}) custom-call(f32[32,4,128]{2,1,0:T(4,128)S(1)} %all_to_all.28.in_ref, f32[8,128]{1,0:T(8,128)S(1)} %get-tuple-element.238.own_ref, f32[128,128]{1,0:T(8,128)S(1)} %get-tuple-element.241.mixed_ref), custom_call_target="tpu_custom_call" | custom-call | tf_op jit(solution)/shard_map/pallas_call | solution.py:368
  76.7 4.1 %all-to-all-start.5 = ((f32[16,24,128]{2,1,0:T(8,128)}), f32[16,24,128]{2,1,0:T(8,128)S(1)}, u32[]{:S(2)}, u32[]{:S(2)}) async-start(f32[16,24,128]{2,1,0:T(8,128)} %get-tuple-element.243), calls=%async_computation.5 | async-start | bytes 393216 | tf_op jit(solution)/shard_map/all_to_all | solution.py:374
  81.3 8.5 %all-to-all-done.5.in_ref = f32[16,24,128]{2,1,0:T(8,128)S(1)} async-done(((f32[16,24,128]{2,1,0:T(8,128)}), f32[16,24,128]{2,1,0:T(8,128)S(1)}, u32[]{:S(2)}, u32[]{:S(2)}) %all-to-all-start.5) | async-done | bytes 196640 | tf_op jit(solution)/shard_map/all_to_all | solution.py:374
  89.9 1.0 %shard_map.23 = f32[256,512]{1,0:T(8,128)S(1)} custom-call(f32[256,512]{1,0:T(8,128)S(1)} %copy-done, f32[16,24,128]{2,1,0:T(8,128)S(1)} %all-to-all-done.5.in_ref, f32[32,512]{1,0:T(8,128)S(1)} %get-tuple-element.244.right_ref), custom_call_target="tpu_custom_call" | custom-call | tf_op jit(solution)/shard_map/pallas_call | solution.py:375
  90.9 0.0 copy-start.1
  91.0 0.8 copy-done.1
  (6 shorter events, 0.1 us)
Async XLA Ops:
  0.8 22.9 %copy-start = (f32[256,512]{1,0:T(8,128)S(1)}, f32[256,512]{1,0:T(8,128)}, u32[]{:S(2)}) copy-start(f32[256,512]{1,0:T(8,128)} %a_ref.3) | copy-start | bytes 1572868
  0.8 0.8 collective-permute-start
  1.7 0.7 collective-permute-start.1
  2.4 0.7 collective-permute-start.2
  3.1 0.7 collective-permute-start.3
  3.8 19.9 %collective-permute-start.4 = (f32[32,512]{1,0:T(8,128)S(1)}, f32[32,512]{1,0:T(8,128)S(1)}, u32[]{:S(2)}, u32[]{:S(2)}) collective-permute-start(f32[32,512]{1,0:T(8,128)S(1)} %add.152), channel_id=1, source_target_pairs={{0,16},{32,48},{64,80},{96,112},{128,144},{160,176},{192,208},{224... | collective-permute-start | bytes 196616 | tf_op jit(solution)/shard_map/ppermute | solution.py:349
  76.7 13.2 %all-to-all-start.5 = ((f32[16,24,128]{2,1,0:T(8,128)}), f32[16,24,128]{2,1,0:T(8,128)S(1)}, u32[]{:S(2)}, u32[]{:S(2)}) async-start(f32[16,24,128]{2,1,0:T(8,128)} %get-tuple-element.243), calls=%async_computation.5 | async-start | bytes 393216 | tf_op jit(solution)/shard_map/all_to_all | solution.py:374
  90.9 0.8 copy-start.1

commit v13 on v12

--- a/solution.py
+++ b/solution.py
@@ -239,7 +239,7 @@
     out_ref[...] = jnp.broadcast_to(packed[None], (ROWS, rows, LANES))
 
 
-def side_kernel(panel_ref, strip_ref, vectors_ref, mixed_ref, right_ref):
+def columns_kernel(strip_ref, vectors_ref, right_ref):
     first_col = lax.axis_index("col") == 0
     vectors = vectors_ref[0]
     strip = strip_ref[...]
@@ -247,6 +247,9 @@
     below_t = jnp.where(lane_c >= jnp.where(first_col, 2 * B, 0), strip, 0.0)
     unit_t = jnp.where(first_col & (iota(strip.shape, 0) == lane_c - B), 1.0, 0.0)
     right_ref[...] = dot_tn(vectors, jnp.concatenate([below_t, unit_t], axis=0))
+
+
+def rows_kernel(panel_ref, vectors_ref, mixed_ref):
     panel = panel_ref[:, 0:PIECE, :]
     source = iota(panel.shape, 0)
     order = iota(panel.shape, 1) + lax.axis_index("col") * PIECE
@@ -362,15 +365,15 @@
     )(panel)
     got = lax.all_to_all(sent, "row", 0, 0)
     got, panel = lax.optimization_barrier((got, panel))
-    mixed, right = call(side_kernel, array(LANES, LANES), array(B, matrix.shape[1]))(
-        panel, strip, vectors
-    )
+    (mixed,) = call(rows_kernel, array(LANES, LANES))(panel, vectors)
     sent, fine = call(
         inner_kernel,
         array(COLS, 3 * PIECE // 2, LANES),
         array(1, 1, dtype=jnp.int32),
         smem=(1,),
     )(got, own, mixed)
+    sent, vectors = lax.optimization_barrier((sent, vectors))
+    (right,) = call(columns_kernel, array(B, matrix.shape[1]))(strip, vectors)
     got = lax.all_to_all(sent, "col", 0, 0)
     (fast,) = call(update_kernel, array(*matrix.shape))(matrix, got, right)
     return lax.cond(fine[0, 0] > 0, lambda: fast, lambda: general_path(matrix, strip))

time: 92.1 us -> 92.1 us (level)
  no operation moved by 1% of the time
where the time goes in v13:
time: 92.1 us; the launch traced here: 91.7 us
  blocking collectives  47.4 us (51%)
  waiting for transfers between devices  26.9 us (29%)
  starting transfers between devices  8.13 us (9%)
  Pallas kernels  6.7 us (7%)
    all_to_all x1, blocking collectives, on_device(): got = lax.all_to_all(sent, 'row', 0, 0)  31.8 us
    ppermute x5, waiting for transfers between devices, spread(): strip = strip + lax.ppermute(strip, axes, pairs)  18.6 us
    all_to_all x1, blocking collectives, on_device(): panel = lax.all_to_all(sent, 'col', 0, 0)  15.6 us
    all_to_all x1, waiting for transfers between devices, on_device(): got = lax.all_to_all(sent, 'col', 0, 0)  8.27 us
    ppermute x5, starting transfers between devices, spread(): strip = strip + lax.ppermute(strip, axes, pairs)  4.07 us
    all_to_all x1, starting transfers between devices, on_device(): got = lax.all_to_all(sent, 'col', 0, 0)  4.06 us
    pallas_call x1, Pallas kernels, on_device(): call(factor_kernel, array(ROWS, PIECE // 4, LANES), array(PIECE // 2, LAN...  3.06 us
  transfers between devices with their start and end apart: 6, of which 2 were waited for; matrix products, arithmetic and copies ran while one was open for 0% of the time, Pallas kernels for 0%

profile of v13, /device:TPU:1, one launch (start us, length us, event | category | flops | bytes accessed | tf_op | source)
XLA Modules:
  0.0 91.7 jit_solution(14105074815875247665)
XLA Ops:
  0.0 0.8 slice_select_fusion
  0.8 0.8 collective-permute-start
  1.6 0.0 collective-permute-done
  1.7 0.7 collective-permute-start.1
  2.3 0.0 collective-permute-done.1
  2.4 0.7 collective-permute-start.2
  3.0 0.0 collective-permute-done.2
  3.1 0.7 collective-permute-start.3
  3.7 0.0 collective-permute-done.3
  3.8 1.3 %collective-permute-start.4 = (f32[32,512]{1,0:T(8,128)S(1)}, f32[32,512]{1,0:T(8,128)S(1)}, u32[]{:S(2)}, u32[]{:S(2)}) collective-permute-start(f32[32,512]{1,0:T(8,128)S(1)} %add.152), channel_id=1, source_target_pairs={{0,16},{32,48},{64,80},{96,112},{128,144},{160,176},{192,208},{224... | collective-permute-start | bytes 196616 | tf_op jit(solution)/shard_map/ppermute | solution.py:352
  5.1 18.6 %collective-permute-done.4 = f32[32,512]{1,0:T(8,128)S(1)} collective-permute-done((f32[32,512]{1,0:T(8,128)S(1)}, f32[32,512]{1,0:T(8,128)S(1)}, u32[]{:S(2)}, u32[]{:S(2)}) %collective-permute-start.4) | collective-permute-done | bytes 65568 | tf_op jit(solution)/shard_map/ppermute | solution.py:352
  23.7 0.0 copy-done
  23.7 0.8 shard_map.19
  24.5 15.6 %all_to_all.27.in_ref.panel_ref = f32[16,32,128]{2,1,0:T(8,128)S(1)} all-to-all(f32[16,32,128]{2,1,0:T(8,128)S(1)} %shard_map.19), channel_id=1, replica_groups=mesh['row'=32,'col'=16] {'col'}, dimensions={0} | all-to-all | bytes 524288 | tf_op jit(solution)/shard_map/all_to_all | solution.py:359
  40.1 3.1 %shard_map.20 = (f32[32,4,128]{2,1,0:T(4,128)S(1)}, f32[8,128]{1,0:T(8,128)S(1)}, f32[2,64,32]{2,1,0:T(8,128)S(1)}) custom-call(f32[16,32,128]{2,1,0:T(8,128)S(1)} %all_to_all.27.in_ref.panel_ref), custom_call_target="tpu_custom_call" | custom-call | tf_op jit(solution)/shard_map/pallas_call | solution.py:360
  43.2 31.8 %all_to_all.28.in_ref = f32[32,4,128]{2,1,0:T(4,128)S(1)} all-to-all(f32[32,4,128]{2,1,0:T(4,128)S(1)} %get-tuple-element.236), channel_id=1, replica_groups=mesh['row'=32,'col'=16] {'row'}, dimensions={0} | all-to-all | bytes 131072 | tf_op jit(solution)/shard_map/all_to_all | solution.py:366
  75.0 0.5 shard_map.21.mixed_ref
  75.5 1.1 %shard_map.22 = (f32[16,24,128]{2,1,0:T(8,128)}, s32[1,1]{1,0:T(1,128)}) custom-call(f32[32,4,128]{2,1,0:T(4,128)S(1)} %all_to_all.28.in_ref, f32[8,128]{1,0:T(8,128)S(1)} %get-tuple-element.238.own_ref, f32[128,128]{1,0:T(8,128)S(1)} %shard_map.21.mixed_ref), custom_call_target="tpu_custom_call" | custom-call | tf_op jit(solution)/shard_map/pallas_call | solution.py:369
  76.6 4.1 %all-to-all-start.5 = ((f32[16,24,128]{2,1,0:T(8,128)}), f32[16,24,128]{2,1,0:T(8,128)S(1)}, u32[]{:S(2)}, u32[]{:S(2)}) async-start(f32[16,24,128]{2,1,0:T(8,128)} %get-tuple-element.243), calls=%async_computation.5 | async-start | bytes 393216 | tf_op jit(solution)/shard_map/all_to_all | solution.py:377
  81.3 0.2 shard_map.23.right_ref
  81.5 8.3 %all-to-all-done.5.in_ref = f32[16,24,128]{2,1,0:T(8,128)S(1)} async-done(((f32[16,24,128]{2,1,0:T(8,128)}), f32[16,24,128]{2,1,0:T(8,128)S(1)}, u32[]{:S(2)}, u32[]{:S(2)}) %all-to-all-start.5) | async-done | bytes 196640 | tf_op jit(solution)/shard_map/all_to_all | solution.py:377
  89.8 1.1 %shard_map.24 = f32[256,512]{1,0:T(8,128)S(1)} custom-call(f32[256,512]{1,0:T(8,128)S(1)} %copy-done, f32[16,24,128]{2,1,0:T(8,128)S(1)} %all-to-all-done.5.in_ref, f32[32,512]{1,0:T(8,128)S(1)} %shard_map.23.right_ref), custom_call_target="tpu_custom_call" | custom-call | tf_op jit(solution)/shard_map/pallas_call | solution.py:378
  90.9 0.0 copy-start.1
  90.9 0.8 copy-done.1
  (7 shorter events, 0.1 us)
Async XLA Ops:
  0.8 22.9 %copy-start = (f32[256,512]{1,0:T(8,128)S(1)}, f32[256,512]{1,0:T(8,128)}, u32[]{:S(2)}) copy-start(f32[256,512]{1,0:T(8,128)} %a_ref.3) | copy-start | bytes 1572868
  0.8 0.8 collective-permute-start
  1.7 0.7 collective-permute-start.1
  2.4 0.7 collective-permute-start.2
  3.1 0.7 collective-permute-start.3
  3.8 19.9 %collective-permute-start.4 = (f32[32,512]{1,0:T(8,128)S(1)}, f32[32,512]{1,0:T(8,128)S(1)}, u32[]{:S(2)}, u32[]{:S(2)}) collective-permute-start(f32[32,512]{1,0:T(8,128)S(1)} %add.152), channel_id=1, source_target_pairs={{0,16},{32,48},{64,80},{96,112},{128,144},{160,176},{192,208},{224... | collective-permute-start | bytes 196616 | tf_op jit(solution)/shard_map/ppermute | solution.py:352
  76.6 13.2 %all-to-all-start.5 = ((f32[16,24,128]{2,1,0:T(8,128)}), f32[16,24,128]{2,1,0:T(8,128)S(1)}, u32[]{:S(2)}, u32[]{:S(2)}) async-start(f32[16,24,128]{2,1,0:T(8,128)} %get-tuple-element.243), calls=%async_computation.5 | async-start | bytes 393216 | tf_op jit(solution)/shard_map/all_to_all | solution.py:377
  90.9 0.8 copy-start.1
